TPU v7x, 32 devices: a whole 2x2x4 slice. The times are simulated.
32 devices in a mesh: section: 4 (over y, core), frame: 8 (over z, x).
Axes of the slice: x: 2, y: 2, z: 4, core: 2. Of those that a mesh axis runs over, the one named last changes fastest.
Arguments:
- newcomer_groups: bfloat16 [1, 2048, 1536], P(None, 'frame'), may hold values from -6 to 6
- pending_inputs: bfloat16 [4, 2048, 1536], P('section', 'frame'), may hold values from -6 to 6
- speaker_clip_ids: int32 [5, 2048], P(None, 'frame'), may hold values from 0 to 15, never falling along the last dimension, each value on 1 to 256 neighbouring positions
- selfattend_scaling: float32 [4, 1536], P('section'), may hold values from 0.1 to 1.9
- triple_projection_matrix: bfloat16 [4, 1536, 4608], P('section', 'frame'), may hold values from -1 to 1
- selfattend_final_matrix: bfloat16 [4, 1536, 1536], P('section', 'frame'), may hold values from -0.15625 to 0.15625
- depthwise_scaling: float32 [4, 1536], P('section'), may hold values from 0.1 to 1.9
- sigmoid_expand_matrix: bfloat16 [4, 1536, 3072], P('section', 'frame'), may hold values from -0.15625 to 0.15625
- filter_taps: float32 [4, 31, 1536], P('section'), may hold values from -1 to 1
- combine_channel_matrix: bfloat16 [4, 1536, 1536], P('section', 'frame'), may hold values from -0.15625 to 0.15625
Outputs:
- section_out: bfloat16 [2, 4, 2048, 1536], P(None, 'section', 'frame')
Inputs may be any that keep to these rules, and one draw needn't show every extreme that they name: `speaker_clip_ids`: in every row the ids never fall along frames; every utterance has 1 to 256 frames, and one utterance of each row has exactly 256.
All inputs are finite; a program needn't handle non-finite values.
Results may differ from a plain program's by a relative error of at most 0.008.
Values may be sent and summed in bfloat16 or wider, within the bound.
No kernel may reach another device: no remote copies, remote signals or barrier semaphores. Data moves between devices by JAX's collectives and lax.ppermute only.
A program may use at most 192 MiB of HBM per device.

v0:
```python
import jax
import jax.numpy as jnp
from jax import lax
from jax.sharding import PartitionSpec as P

HEADS = 24
KERNEL = 31


EPS = 1e-05


def extended(block, sides, width):
    for axis, dim in sides:
        count = lax.axis_size(axis)
        forward = [(i, i + 1) for i in range(count - 1)]
        backward = [(target, source) for source, target in forward]
        low = lax.ppermute(
            lax.slice_in_dim(block, block.shape[dim] - width, None, axis=dim), axis, forward
        )
        high = lax.ppermute(lax.slice_in_dim(block, 0, width, axis=dim), axis, backward)
        block = jnp.concatenate([low, block, high], axis=dim)
    return block


def shifted(value, axis, steps):
    count = lax.axis_size(axis)
    leading, last = (max(0, -steps), min(count, count - steps))
    return lax.ppermute(value, axis, [(source, source + steps) for source in range(leading, last)])


def layer_norm(sample_lines, gain):
    mean = jnp.mean(sample_lines, axis=-1, keepdims=True)
    centred = sample_lines - mean
    spread = jnp.mean(centred * centred, axis=-1, keepdims=True)
    return centred * lax.rsqrt(spread + EPS) * gain


def attend(query, wide_keys, wide_values, seg_wide, seg_own):
    sample_lines, feature_count = query.shape
    head_dim = feature_count // HEADS
    shaped_q = query.reshape(sample_lines, HEADS, head_dim)
    shaped_k = wide_keys.reshape(wide_keys.shape[0], HEADS, head_dim)
    shaped_v = wide_values.reshape(wide_values.shape[0], HEADS, head_dim)
    scores = jnp.einsum("qhd,khd->hqk", shaped_q, shaped_k, preferred_element_type=jnp.float32)
    allowed = (seg_own[:, None] == seg_wide[None, :])[None]
    scores = jnp.where(allowed, scores, -1e30)
    top = jnp.max(scores, axis=-1, keepdims=True)
    expd = jnp.exp(scores - top)
    probs = (expd / jnp.sum(expd, axis=-1, keepdims=True)).astype(jnp.bfloat16)
    context = jnp.einsum("hqk,khd->qhd", probs, shaped_v, preferred_element_type=jnp.float32)
    return context.astype(jnp.bfloat16).reshape(sample_lines, feature_count)


def depthwise(wide_glu, seg_conv, seg_own, taps):
    sample_lines = seg_own.shape[0]
    total = jnp.zeros((sample_lines, wide_glu.shape[1]), jnp.float32)
    for tap in range(taps.shape[0]):
        same = (seg_conv[tap : tap + sample_lines] == seg_own)[:, None]
        total = total + jnp.where(
            same, wide_glu[tap : tap + sample_lines].astype(jnp.float32) * taps[tap], 0.0
        )
    return total


def on_device(
    newcomer_groups,
    pending_inputs,
    speaker_clip_ids,
    selfattend_scaling,
    triple_projection_matrix,
    selfattend_final_matrix,
    depthwise_scaling,
    sigmoid_expand_matrix,
    filter_taps,
    combine_channel_matrix,
):
    sample_lines = pending_inputs.shape[1]
    feature_count = pending_inputs.shape[2]
    half = KERNEL // 2
    sections = lax.axis_size("section")
    section = lax.axis_index("section")
    ticks = newcomer_groups.shape[0] + 1
    seg_all = extended(speaker_clip_ids + 1, (("frame", 1),), sample_lines)
    full_qkv, full_out, full_glu, full_mix = (
        lax.all_gather(triple_projection_matrix[0], "frame", axis=0, tiled=True),
        lax.all_gather(selfattend_final_matrix[0], "frame", axis=0, tiled=True),
        lax.all_gather(sigmoid_expand_matrix[0], "frame", axis=0, tiled=True),
        lax.all_gather(combine_channel_matrix[0], "frame", axis=0, tiled=True),
    )
    present_activity = pending_inputs[0]
    made_all = []
    for tick in range(ticks):
        batch_index = sections - 1 - section + tick
        seg_wide = lax.dynamic_index_in_dim(seg_all, batch_index, 0, keepdims=False)
        seg_own = seg_wide[sample_lines : 2 * sample_lines]
        resid = present_activity.astype(jnp.float32)
        normed = layer_norm(resid, selfattend_scaling[0]).astype(jnp.bfloat16)
        projected = jnp.dot(normed, full_qkv, preferred_element_type=jnp.float32)
        query = (projected[:, :feature_count] * (feature_count // HEADS) ** (-0.5)).astype(
            jnp.bfloat16
        )
        keys = projected[:, feature_count : 2 * feature_count].astype(jnp.bfloat16)
        values = projected[:, 2 * feature_count :].astype(jnp.bfloat16)
        wide_keys, wide_values = (
            extended(keys, (("frame", 0),), sample_lines),
            extended(values, (("frame", 0),), sample_lines),
        )
        context = attend(query, wide_keys, wide_values, seg_wide, seg_own)
        resid = resid + jnp.dot(context, full_out, preferred_element_type=jnp.float32)
        conv_in = layer_norm(resid, depthwise_scaling[0]).astype(jnp.bfloat16)
        doubled = jnp.dot(conv_in, full_glu, preferred_element_type=jnp.float32)
        glu = (doubled[:, :feature_count] * jax.nn.sigmoid(doubled[:, feature_count:])).astype(
            jnp.bfloat16
        )
        wide_glu = extended(glu, (("frame", 0),), half)
        depth = depthwise(
            wide_glu,
            seg_wide[sample_lines - half : 2 * sample_lines + half],
            seg_own,
            filter_taps[0],
        )
        act = (depth * jax.nn.sigmoid(depth)).astype(jnp.bfloat16)
        resid = resid + jnp.dot(act, full_mix, preferred_element_type=jnp.float32)
        made = resid.astype(jnp.bfloat16)
        made_all.append(made)
        if tick + 1 < ticks:
            arrived = shifted(made, "section", 1)
            present_activity = jnp.where(section == 0, newcomer_groups[tick], arrived)
    return jnp.stack(made_all)[:, None]


def solution(mesh):
    in_specs = (
        P(None, "frame", None),
        P("section", "frame", None),
        P(None, "frame"),
        P("section", None),
        P("section", "frame", None),
        P("section", "frame", None),
        P("section", None),
        P("section", "frame", None),
        P("section", None, None),
        P("section", "frame", None),
    )
    out_specs = P(None, "section", "frame", None)
    return jax.shard_map(
        on_device, mesh=mesh, in_specs=in_specs, out_specs=out_specs, check_vma=False
    )
```

profile of v0, /device:TPU:6, one launch (start us, length us, event | category | flops | bytes accessed | tf_op | source)
XLA Modules:
  0.0 725.2 jit_solution(8449373130412584461)
XLA Ops:
  6.5 0.7 all-gather.9.cloned.1.call-update
  7.3 0.7 all-gather.11.cloned.1.call-update
  8.1 0.7 all-gather.13.cloned.1.call-update
  8.8 3.5 collective-permute-start.2
  12.3 2.4 collective-permute-start.3
  15.6 0.8 slice_reduce_fusion.29
  16.5 2.3 collective-permute-done.3
  18.9 0.9 fusion.163
  19.9 185.6 %all-gather.9.cloned.1.call-done = bf16[1,1536,4608]{2,1,0:T(8,128)(2,1)} async-done(((bf16[1,192,4608]{2,1,0:T(8,128)(2,1)}), bf16[1,1536,4608]{2,1,0:T(8,128)(2,1)}) %all-gather.9.cloned.1.call-update) | async-done | bytes 14155792 | tf_op jit(solution)/shard_map/all_gather | solution.py:86
  205.5 7.3 %fusion.169 = (bf16[256,4608]{1,0:T(8,128)(2,1)S(1)}, f32[256,4608]{1,0:T(8,128)S(1)}) fusion(bf16[1,1536,4608]{2,1,0:T(8,128)(2,1)} %all-gather.9.cloned.1.call-done, bf16[1,256,1536]{2,1,0:T(8,128)(2,1)S(1)} %copy-done, f32[1536]{0:T(1024)S(1)} %reduce.1, f32[256]{0:T(256)S(1)} %add_rsqrt_fusion.3, f32[256]{0:T(256)S(1)} %broadcast_multiply_fusion.3), kind=kOutput, calls=%fused_computation.312 | convolution fusion | flops 3627024384 | bytes 22028288 | tf_op jit(solution)/shard_map/dot_general | solution.py:99
  212.8 1.0 fusion.159
  213.8 2.4 collective-permute-start.4
  216.2 3.4 collective-permute-start.5
  219.6 0.7 fusion.167
  220.4 0.9 broadcast_compare_fusion
  221.3 3.3 collective-permute-start
  224.6 3.6 collective-permute-start.1
  228.3 1.2 copy.19
  229.5 42.6 %collective-permute-done.4 = bf16[256,1536]{1,0:T(8,128)(2,1)S(1)} collective-permute-done((bf16[256,1536]{1,0:T(8,128)(2,1)S(1)}, bf16[256,1536]{1,0:T(8,128)(2,1)S(1)}, u32[]{:S(2)}, u32[]{:S(2)}) %collective-permute-start.4) | collective-permute-done | bytes 786464 | tf_op jit(solution)/shard_map/ppermute | solution.py:18
  272.2 0.9 copy-done.4
  273.1 1.8 pad_maximum_fusion.1
  274.8 2.5 copy.20
  277.3 33.5 %collective-permute-done = bf16[256,1536]{1,0:T(8,128)(2,1)} collective-permute-done((bf16[256,1536]{1,0:T(8,128)(2,1)}, bf16[256,1536]{1,0:T(8,128)(2,1)}, u32[]{:S(2)}, u32[]{:S(2)}) %collective-permute-start) | collective-permute-done | bytes 786464 | tf_op jit(solution)/shard_map/ppermute | solution.py:18
  310.8 1.8 pad_maximum_fusion
  312.5 2.4 copy.18
  315.0 11.6 %fusion.170 = (f32[24,256]{1,0:T(8,128)S(1)}, f32[24,256,768]{2,1,0:T(8,128)}) fusion(pred[256,768]{1,0:T(8,128)(4,1)} %get-tuple-element.183, bf16[256,24,64]{0,2,1:T(8,128)(2,1)} %bitcast.166, bf16[768,24,64]{0,2,1:T(8,128)(2,1)} %bitcast.162), kind=kOutput, calls=%fused_computation.313 | convolution fusion | flops 618136320 | bytes 22241280 | tf_op jit(solution)/shard_map/sub | solution.py:49
  326.6 9.0 %fusion.79 = bf16[24,64,256]{2,1,0:T(8,128)(2,1)S(1)} fusion(bf16[768,24,64]{0,2,1:T(8,128)(2,1)} %bitcast.164, f32[24,256,768]{2,1,0:T(8,128)} %get-tuple-element.173, f32[24,256]{1,0:T(8,128)S(1)} %get-tuple-element.172), kind=kOutput, calls=%fused_computation.140 | convolution fusion | flops 613810176 | bytes 22044672 | tf_op jit(solution)/shard_map/hqk,khd->qhd/dot_general | solution.py:51
  335.6 3.8 fusion.171
  339.8 131.3 %all-gather.13.cloned.1.call-done = bf16[1,1536,3072]{2,1,0:T(8,128)(2,1)} async-done(((bf16[1,192,3072]{2,1,0:T(8,128)(2,1)}), bf16[1,1536,3072]{2,1,0:T(8,128)(2,1)}) %all-gather.13.cloned.1.call-update) | async-done | bytes 9437200 | tf_op jit(solution)/shard_map/all_gather | solution.py:88
  471.1 5.2 fusion.14
  476.4 0.4 fusion.76
  476.9 2.5 collective-permute-start.6
  479.4 3.6 collective-permute-start.7
  483.1 0.6 fusion.168
  483.7 67.9 %all-gather.15.cloned.1.call-done = bf16[1,1536,1536]{2,1,0:T(8,128)(2,1)} async-done(((bf16[1,192,1536]{2,1,0:T(8,128)(2,1)}), bf16[1,1536,1536]{2,1,0:T(8,128)(2,1)}) %all-gather.15.cloned.1.call-update) | async-done | bytes 4718608 | tf_op jit(solution)/shard_map/all_gather | solution.py:89
  551.6 0.6 copy-done.59
  552.3 21.7 %fusion.45 = bf16[256,1536]{1,0:T(8,128)(2,1)S(1)} fusion(f32[256,1536]{1,0:T(8,128)S(1)} %get-tuple-element.175, bf16[1,1536,1536]{2,1,0:T(8,128)(2,1)} %all-gather.15.cloned.1.call-done, bf16[256,1536]{1,0:T(8,128)(2,1)S(1)} %fusion.76, bf16[15,1536]{1,0:T(8,128)(2,1)} %copy-done.60, bf16[15,1536]{1,0:T(8,128)(2,1)} %copy-done.59, ...), kind=kOutput, calls=%fused_computation.93 | convolution fusion | flops 1294073856 | bytes 8154624 | tf_op jit(solution)/shard_map/dot_general | solution.py:124
  574.0 2.3 collective-permute-start.8
  576.3 11.0 %collective-permute-done.8 = bf16[256,1536]{1,0:T(8,128)(2,1)S(1)} collective-permute-done((bf16[256,1536]{1,0:T(8,128)(2,1)S(1)}, bf16[256,1536]{1,0:T(8,128)(2,1)S(1)}, u32[]{:S(2)}, u32[]{:S(2)}) %collective-permute-start.8) | collective-permute-done | bytes 786464 | tf_op jit(solution)/shard_map/ppermute | solution.py:29
  587.3 1.4 convert_reduce_fusion
  589.1 7.3 %fusion.172 = (bf16[256,4608]{1,0:T(8,128)(2,1)S(1)}, f32[256,4608]{1,0:T(8,128)S(1)}) fusion(bf16[1,1536,4608]{2,1,0:T(8,128)(2,1)} %all-gather.9.cloned.1.call-done, bf16[256,1536]{1,0:T(8,128)(2,1)S(1)} %get-tuple-element.39, f32[256]{0:T(256)S(1)} %add_rsqrt_fusion.1, f32[256]{0:T(256)S(1)} %broadcast_multiply_fusion.1, f32[1536]{0:T(1024)S(1)} %reduce.1), kind=kOutput, calls=%fused_computation.315 | convolution fusion | flops 3627024384 | bytes 22028288 | tf_op jit(solution)/shard_map/dot_general | solution.py:99
  596.4 1.0 fusion.158
  597.4 3.3 collective-permute-start.11
  600.7 2.5 collective-permute-start.12
  603.5 0.7 fusion.165
  604.2 1.9 collective-permute-start.10
  606.1 4.8 collective-permute-start.9
  611.0 1.2 copy.22
  612.2 35.2 %collective-permute-done.11 = bf16[256,1536]{1,0:T(8,128)(2,1)S(1)} collective-permute-done((bf16[256,1536]{1,0:T(8,128)(2,1)S(1)}, bf16[256,1536]{1,0:T(8,128)(2,1)S(1)}, u32[]{:S(2)}, u32[]{:S(2)}) %collective-permute-start.11) | collective-permute-done | bytes 786464 | tf_op jit(solution)/shard_map/ppermute | solution.py:18
  647.5 0.9 copy-done.3
  648.4 1.8 pad_maximum_fusion.3
  650.1 2.5 copy.23
  652.6 7.7 %collective-permute-done.9 = bf16[256,1536]{1,0:T(8,128)(2,1)} collective-permute-done((bf16[256,1536]{1,0:T(8,128)(2,1)}, bf16[256,1536]{1,0:T(8,128)(2,1)}, u32[]{:S(2)}, u32[]{:S(2)}) %collective-permute-start.9) | collective-permute-done | bytes 786464 | tf_op jit(solution)/shard_map/ppermute | solution.py:18
  660.3 1.8 pad_maximum_fusion.2
  662.0 2.5 copy.21
  664.5 11.7 %fusion.173 = (f32[24,256]{1,0:T(8,128)S(1)}, f32[24,256,768]{2,1,0:T(8,128)}) fusion(pred[256,768]{1,0:T(8,128)(4,1)S(1)} %get-tuple-element.182, bf16[256,24,64]{0,2,1:T(8,128)(2,1)} %bitcast.165, bf16[768,24,64]{0,2,1:T(8,128)(2,1)} %bitcast.161), kind=kOutput, calls=%fused_computation.316 | convolution fusion | flops 618136320 | bytes 22241280 | tf_op jit(solution)/shard_map/sub | solution.py:49
  676.2 9.1 %fusion.78 = bf16[24,64,256]{2,1,0:T(8,128)(2,1)S(1)} fusion(bf16[768,24,64]{0,2,1:T(8,128)(2,1)} %bitcast.163, f32[24,256,768]{2,1,0:T(8,128)} %get-tuple-element.179, f32[24,256]{1,0:T(8,128)S(1)} %get-tuple-element.178), kind=kOutput, calls=%fused_computation.139 | convolution fusion | flops 613810176 | bytes 22044672 | tf_op jit(solution)/shard_map/hqk,khd->qhd/dot_general | solution.py:51
  685.3 1.5 fusion.174
  687.2 5.4 fusion.12
  693.4 4.3 collective-permute-start.13
  697.6 2.1 collective-permute-start.14
  699.9 4.6 collective-permute-done.14
  704.8 12.4 %fusion.48 = bf16[1,256,1536]{2,1,0:T(8,128)(2,1)S(1)} fusion(f32[256,1536]{1,0:T(8,128)S(1)} %get-tuple-element.181, bf16[1,1536,1536]{2,1,0:T(8,128)(2,1)S(1)} %bitcast.235, bf16[256,1536]{1,0:T(8,128)(2,1)S(1)} %fusion.77, bf16[15,1536]{1,0:T(8,128)(2,1)S(1)} %collective-permute-done.14, bf16[15,1536]{1,0:T(8,128)(2,1)S(1)} %collective-permute-done.13, ...), kind=kOutput, calls=%fused_computation.94 | convolution fusion | flops 1294073856 | bytes 8154624 | tf_op jit(solution)/shard_map/dot_general | solution.py:124
  717.2 1.3 maximum_bitcast_fusion
  (170 shorter events, 3.4 us)
Async XLA Ops:
  6.5 198.9 %all-gather.9.cloned.1.call-start = ((), (), s32[]{:S(2)}) async-start(), calls=%async_computation | async-start | bytes 15925248 | tf_op jit(solution)/shard_map/all_gather | solution.py:86
  7.3 7.5 %copy-start = (bf16[1,256,1536]{2,1,0:T(8,128)(2,1)S(1)}, bf16[1,256,1536]{2,1,0:T(8,128)(2,1)}, u32[]{:S(2)}) copy-start(bf16[1,256,1536]{2,1,0:T(8,128)(2,1)} %param.11) | copy-start | bytes 2359300
  7.3 328.3 %all-gather.11.cloned.1.call-start = ((), (), s32[]{:S(2)}) async-start(), calls=%async_computation.1 | async-start | bytes 5308416 | tf_op jit(solution)/shard_map/all_gather | solution.py:87
  8.0 7.3 %copy-start.7 = (f32[1,31,1536]{2,0,1:T(1,128)S(1)}, f32[1,31,1536]{2,0,1:T(1,128)}, u32[]{:S(2)}) copy-start(f32[1,31,1536]{2,0,1:T(1,128)} %param.18) | copy-start | bytes 571396
  8.0 463.0 %all-gather.13.cloned.1.call-start = ((), (), s32[]{:S(2)}) async-start(), calls=%async_computation.2 | async-start | bytes 10616832 | tf_op jit(solution)/shard_map/all_gather | solution.py:88
  8.8 7.6 %copy-start.20 = (f32[1,1536]{1,0:T(1,128)S(1)}, f32[1,1536]{1,0:T(1,128)}, u32[]{:S(2)}) copy-start(f32[1,1536]{1,0:T(1,128)} %param.13) | copy-start | bytes 18436
  8.8 7.6 %copy-start.21 = (f32[1,1536]{1,0:T(1,128)S(1)}, f32[1,1536]{1,0:T(1,128)}, u32[]{:S(2)}) copy-start(f32[1,1536]{1,0:T(1,128)} %param.16) | copy-start | bytes 18436
  8.8 542.8 %all-gather.15.cloned.1.call-start = ((), (), s32[]{:S(2)}) async-start(), calls=%async_computation.3 | async-start | bytes 5308416 | tf_op jit(solution)/shard_map/all_gather | solution.py:89
  8.8 7.6 %collective-permute-start.2 = (s32[5,256]{1,0:T(8,128)S(1)}, s32[5,256]{1,0:T(8,128)S(1)}, u32[]{:S(2)}, u32[]{:S(2)}) collective-permute-start(s32[5,256]{1,0:T(8,128)S(1)} %broadcast_add_fusion), channel_id=1, source_target_pairs={{0,1},{1,2},{2,3},{3,4},{4,5},{5,6},{6,7},{8,9},{9,10},{10,11},{11... | collective-permute-start | bytes 15368 | tf_op jit(solution)/shard_map/ppermute | solution.py:18
  12.3 6.4 collective-permute-start.3
  213.7 58.4 %copy-start.2 = (bf16[256,1536]{1,0:T(8,128)(2,1)}, bf16[256,1536]{1,0:T(8,128)(2,1)S(1)}, u32[]{:S(2)}) copy-start(bf16[256,1536]{1,0:T(8,128)(2,1)S(1)} %get-tuple-element.42) | copy-start | bytes 2359300
  213.8 58.4 %collective-permute-start.4 = (bf16[256,1536]{1,0:T(8,128)(2,1)S(1)}, bf16[256,1536]{1,0:T(8,128)(2,1)S(1)}, u32[]{:S(2)}, u32[]{:S(2)}) collective-permute-start(bf16[256,1536]{1,0:T(8,128)(2,1)S(1)} %get-tuple-element.42), channel_id=1, source_target_pairs={{0,1},{1,2},{2,3},{3,4},{4,5},{5,6},{6,7},{8,9},{9,10},{10,11},{11... | collective-permute-start | bytes 2359304 | tf_op jit(solution)/shard_map/ppermute | solution.py:18
  216.2 56.9 %collective-permute-start.5 = (bf16[256,1536]{1,0:T(8,128)(2,1)S(1)}, bf16[256,1536]{1,0:T(8,128)(2,1)}, u32[]{:S(2)}, u32[]{:S(2)}) collective-permute-start(bf16[256,1536]{1,0:T(8,128)(2,1)S(1)} %get-tuple-element.42), channel_id=1, source_target_pairs={{1,0},{2,1},{3,2},{4,3},{5,4},{6,5},{7,6},{9,8},{10,9},{11,10},{12... | collective-permute-start | bytes 2359304 | tf_op jit(solution)/shard_map/ppermute | solution.py:21
  221.3 89.5 %collective-permute-start = (bf16[256,1536]{1,0:T(8,128)(2,1)}, bf16[256,1536]{1,0:T(8,128)(2,1)}, u32[]{:S(2)}, u32[]{:S(2)}) collective-permute-start(bf16[256,1536]{1,0:T(8,128)(2,1)} %get-tuple-element.43), channel_id=1, source_target_pairs={{0,1},{1,2},{2,3},{3,4},{4,5},{5,6},{6,7},{8,9},{9,10},{10,11},{11... | collective-permute-start | bytes 2359304 | tf_op jit(solution)/shard_map/ppermute | solution.py:18
  224.6 86.2 %collective-permute-start.1 = (bf16[256,1536]{1,0:T(8,128)(2,1)}, bf16[256,1536]{1,0:T(8,128)(2,1)}, u32[]{:S(2)}, u32[]{:S(2)}) collective-permute-start(bf16[256,1536]{1,0:T(8,128)(2,1)} %get-tuple-element.43), channel_id=1, source_target_pairs={{1,0},{2,1},{3,2},{4,3},{5,4},{6,5},{7,6},{9,8},{10,9},{11,10},{12... | collective-permute-start | bytes 2359304 | tf_op jit(solution)/shard_map/ppermute | solution.py:21
  476.9 74.7 %collective-permute-start.6 = (bf16[15,1536]{1,0:T(8,128)(2,1)S(1)}, bf16[15,1536]{1,0:T(8,128)(2,1)S(1)}, u32[]{:S(2)}, u32[]{:S(2)}) collective-permute-start(bf16[15,1536]{1,0:T(8,128)(2,1)S(1)} %get-tuple-element.46), channel_id=1, source_target_pairs={{0,1},{1,2},{2,3},{3,4},{4,5},{5,6},{6,7},{8,9},{9,10},{10,11},{11... | collective-permute-start | bytes 138248 | tf_op jit(solution)/shard_map/ppermute | solution.py:18
  479.4 72.3 %collective-permute-start.7 = (bf16[15,1536]{1,0:T(8,128)(2,1)S(1)}, bf16[15,1536]{1,0:T(8,128)(2,1)S(1)}, u32[]{:S(2)}, u32[]{:S(2)}) collective-permute-start(bf16[15,1536]{1,0:T(8,128)(2,1)S(1)} %get-tuple-element.47), channel_id=1, source_target_pairs={{1,0},{2,1},{3,2},{4,3},{5,4},{6,5},{7,6},{9,8},{10,9},{11,10},{12... | collective-permute-start | bytes 138248 | tf_op jit(solution)/shard_map/ppermute | solution.py:21
  574.0 13.3 %collective-permute-start.8 = (bf16[256,1536]{1,0:T(8,128)(2,1)S(1)}, bf16[256,1536]{1,0:T(8,128)(2,1)S(1)}, u32[]{:S(2)}, u32[]{:S(2)}) collective-permute-start(bf16[256,1536]{1,0:T(8,128)(2,1)S(1)} %fusion.45), channel_id=1, source_target_pairs={{0,8},{8,16},{16,24},{1,9},{9,17},{17,25},{2,10},{10,18},{18,26},{... | collective-permute-start | bytes 2359304 | tf_op jit(solution)/shard_map/ppermute | solution.py:29
  597.4 50.1 %copy-start.1 = (bf16[256,1536]{1,0:T(8,128)(2,1)}, bf16[256,1536]{1,0:T(8,128)(2,1)S(1)}, u32[]{:S(2)}) copy-start(bf16[256,1536]{1,0:T(8,128)(2,1)S(1)} %get-tuple-element.40) | copy-start | bytes 2359300
  597.4 50.1 %collective-permute-start.11 = (bf16[256,1536]{1,0:T(8,128)(2,1)S(1)}, bf16[256,1536]{1,0:T(8,128)(2,1)S(1)}, u32[]{:S(2)}, u32[]{:S(2)}) collective-permute-start(bf16[256,1536]{1,0:T(8,128)(2,1)S(1)} %get-tuple-element.40), channel_id=1, source_target_pairs={{0,1},{1,2},{2,3},{3,4},{4,5},{5,6},{6,7},{8,9},{9,10},{10,11},{11... | collective-permute-start | bytes 2359304 | tf_op jit(solution)/shard_map/ppermute | solution.py:18
  600.7 47.6 %collective-permute-start.12 = (bf16[256,1536]{1,0:T(8,128)(2,1)S(1)}, bf16[256,1536]{1,0:T(8,128)(2,1)}, u32[]{:S(2)}, u32[]{:S(2)}) collective-permute-start(bf16[256,1536]{1,0:T(8,128)(2,1)S(1)} %get-tuple-element.40), channel_id=1, source_target_pairs={{1,0},{2,1},{3,2},{4,3},{5,4},{6,5},{7,6},{9,8},{10,9},{11,10},{12... | collective-permute-start | bytes 2359304 | tf_op jit(solution)/shard_map/ppermute | solution.py:21
  604.2 48.4 %collective-permute-start.10 = (bf16[256,1536]{1,0:T(8,128)(2,1)}, bf16[256,1536]{1,0:T(8,128)(2,1)}, u32[]{:S(2)}, u32[]{:S(2)}) collective-permute-start(bf16[256,1536]{1,0:T(8,128)(2,1)} %get-tuple-element.41), channel_id=1, source_target_pairs={{1,0},{2,1},{3,2},{4,3},{5,4},{6,5},{7,6},{9,8},{10,9},{11,10},{12... | collective-permute-start | bytes 2359304 | tf_op jit(solution)/shard_map/ppermute | solution.py:21
  606.1 54.2 %collective-permute-start.9 = (bf16[256,1536]{1,0:T(8,128)(2,1)}, bf16[256,1536]{1,0:T(8,128)(2,1)}, u32[]{:S(2)}, u32[]{:S(2)}) collective-permute-start(bf16[256,1536]{1,0:T(8,128)(2,1)} %get-tuple-element.41), channel_id=1, source_target_pairs={{0,1},{1,2},{2,3},{3,4},{4,5},{5,6},{6,7},{8,9},{9,10},{10,11},{11... | collective-permute-start | bytes 2359304 | tf_op jit(solution)/shard_map/ppermute | solution.py:18
  664.5 20.8 %slice-start = ((s8[4718592]{0:T(1024)(128)(4,1)}), s8[524288]{0:T(1024)(128)(4,1)S(1)}, s32[]{:S(2)}) async-start(s8[4718592]{0:T(1024)(128)(4,1)} %bitcast.157), calls=%async_computation.4 | async-start | bytes 1048576
  676.2 9.1 %slice-start.1 = ((s8[4718592]{0:T(1024)(128)(4,1)}), s8[4194304]{0:T(1024)(128)(4,1)S(1)}, s32[]{:S(2)}) async-start(s8[4718592]{0:T(1024)(128)(4,1)} %bitcast.157), calls=%async_computation.5 | async-start | bytes 8388608
  685.3 19.2 %slice-start.2 = ((s8[4718592]{0:T(1024)(128)(4,1)}), s8[524288]{0:T(1024)(128)(4,1)S(1)}, s32[]{:S(2)}) async-start(s8[4718592]{0:T(1024)(128)(4,1)} %bitcast.234), calls=%async_computation.6 | async-start | bytes 1048576
  687.2 17.4 %slice-start.3 = ((s8[4718592]{0:T(1024)(128)(4,1)}), s8[4194304]{0:T(1024)(128)(4,1)S(1)}, s32[]{:S(2)}) async-start(s8[4718592]{0:T(1024)(128)(4,1)} %bitcast.234), calls=%async_computation.7 | async-start | bytes 8388608
  692.6 7.2 copy-start.22
  692.6 7.2 copy-start.23
  692.6 7.2 copy-start.24
  692.6 7.2 copy-start.25
  692.6 7.2 copy-start.26
  692.6 7.2 copy-start.27
  692.6 7.2 copy-start.28
  692.6 7.2 copy-start.29
  692.7 7.2 copy-start.30
  692.7 7.2 copy-start.31
  692.7 7.2 copy-start.32
  692.7 11.8 %copy-start.9 = (f32[1536]{0:T(1024)S(1)}, f32[1536]{0:T(1024)}, u32[]{:S(2)}) copy-start(f32[1536]{0:T(1024)} %get-tuple-element.25) | copy-start | bytes 18436
  692.7 11.8 %copy-start.10 = (f32[1536]{0:T(1024)S(1)}, f32[1536]{0:T(1024)}, u32[]{:S(2)}) copy-start(f32[1536]{0:T(1024)} %get-tuple-element.26) | copy-start | bytes 18436
  692.7 11.8 %copy-start.11 = (f32[1536]{0:T(1024)S(1)}, f32[1536]{0:T(1024)}, u32[]{:S(2)}) copy-start(f32[1536]{0:T(1024)} %get-tuple-element.27) | copy-start | bytes 18436
  692.7 11.8 %copy-start.12 = (f32[1536]{0:T(1024)S(1)}, f32[1536]{0:T(1024)}, u32[]{:S(2)}) copy-start(f32[1536]{0:T(1024)} %get-tuple-element.28) | copy-start | bytes 18436
  692.7 11.8 %copy-start.13 = (f32[1536]{0:T(1024)S(1)}, f32[1536]{0:T(1024)}, u32[]{:S(2)}) copy-start(f32[1536]{0:T(1024)} %get-tuple-element.29) | copy-start | bytes 18436
  692.7 11.8 %copy-start.14 = (f32[1536]{0:T(1024)S(1)}, f32[1536]{0:T(1024)}, u32[]{:S(2)}) copy-start(f32[1536]{0:T(1024)} %get-tuple-element.30) | copy-start | bytes 18436
  692.8 11.8 %copy-start.15 = (f32[1536]{0:T(1024)S(1)}, f32[1536]{0:T(1024)}, u32[]{:S(2)}) copy-start(f32[1536]{0:T(1024)} %get-tuple-element.31) | copy-start | bytes 18436
  692.8 11.8 %copy-start.16 = (f32[1536]{0:T(1024)S(1)}, f32[1536]{0:T(1024)}, u32[]{:S(2)}) copy-start(f32[1536]{0:T(1024)} %get-tuple-element.32) | copy-start | bytes 18436
  692.8 11.8 %copy-start.17 = (f32[1536]{0:T(1024)S(1)}, f32[1536]{0:T(1024)}, u32[]{:S(2)}) copy-start(f32[1536]{0:T(1024)} %get-tuple-element.33) | copy-start | bytes 18436
  692.8 11.8 %copy-start.18 = (f32[1536]{0:T(1024)S(1)}, f32[1536]{0:T(1024)}, u32[]{:S(2)}) copy-start(f32[1536]{0:T(1024)} %get-tuple-element.34) | copy-start | bytes 18436
  692.8 11.8 %copy-start.19 = (f32[1536]{0:T(1024)S(1)}, f32[1536]{0:T(1024)}, u32[]{:S(2)}) copy-start(f32[1536]{0:T(1024)} %get-tuple-element.35) | copy-start | bytes 18436
  692.8 11.8 %copy-start.47 = (pred[256]{0:T(512)(128)(4,1)S(1)}, pred[256]{0:T(512)(128)(4,1)}, u32[]{:S(2)}) copy-start(pred[256]{0:T(512)(128)(4,1)} %get-tuple-element.116) | copy-start | bytes 772
  692.8 11.8 %copy-start.48 = (pred[256]{0:T(512)(128)(4,1)S(1)}, pred[256]{0:T(512)(128)(4,1)}, u32[]{:S(2)}) copy-start(pred[256]{0:T(512)(128)(4,1)} %get-tuple-element.117) | copy-start | bytes 772
  692.8 11.8 %copy-start.49 = (pred[256]{0:T(512)(128)(4,1)S(1)}, pred[256]{0:T(512)(128)(4,1)}, u32[]{:S(2)}) copy-start(pred[256]{0:T(512)(128)(4,1)} %get-tuple-element.118) | copy-start | bytes 772
  692.8 11.8 %copy-start.50 = (pred[256]{0:T(512)(128)(4,1)S(1)}, pred[256]{0:T(512)(128)(4,1)}, u32[]{:S(2)}) copy-start(pred[256]{0:T(512)(128)(4,1)} %get-tuple-element.119) | copy-start | bytes 772
  692.8 11.8 %copy-start.51 = (pred[256]{0:T(512)(128)(4,1)S(1)}, pred[256]{0:T(512)(128)(4,1)}, u32[]{:S(2)}) copy-start(pred[256]{0:T(512)(128)(4,1)} %get-tuple-element.120) | copy-start | bytes 772
  692.9 11.8 %copy-start.52 = (pred[256]{0:T(512)(128)(4,1)S(1)}, pred[256]{0:T(512)(128)(4,1)}, u32[]{:S(2)}) copy-start(pred[256]{0:T(512)(128)(4,1)} %get-tuple-element.121) | copy-start | bytes 772
  692.9 11.8 %copy-start.53 = (pred[256]{0:T(512)(128)(4,1)S(1)}, pred[256]{0:T(512)(128)(4,1)}, u32[]{:S(2)}) copy-start(pred[256]{0:T(512)(128)(4,1)} %get-tuple-element.122) | copy-start | bytes 772
  692.9 11.8 %copy-start.54 = (pred[256]{0:T(512)(128)(4,1)S(1)}, pred[256]{0:T(512)(128)(4,1)}, u32[]{:S(2)}) copy-start(pred[256]{0:T(512)(128)(4,1)} %get-tuple-element.123) | copy-start | bytes 772
  692.9 11.8 %copy-start.55 = (pred[256]{0:T(512)(128)(4,1)S(1)}, pred[256]{0:T(512)(128)(4,1)}, u32[]{:S(2)}) copy-start(pred[256]{0:T(512)(128)(4,1)} %get-tuple-element.124) | copy-start | bytes 772
  692.9 11.8 %copy-start.56 = (pred[256]{0:T(512)(128)(4,1)S(1)}, pred[256]{0:T(512)(128)(4,1)}, u32[]{:S(2)}) copy-start(pred[256]{0:T(512)(128)(4,1)} %get-tuple-element.125) | copy-start | bytes 772
  692.9 11.8 %copy-start.57 = (pred[256]{0:T(512)(128)(4,1)S(1)}, pred[256]{0:T(512)(128)(4,1)}, u32[]{:S(2)}) copy-start(pred[256]{0:T(512)(128)(4,1)} %get-tuple-element.126) | copy-start | bytes 772
  692.9 11.8 %copy-start.58 = (pred[256]{0:T(512)(128)(4,1)S(1)}, pred[256]{0:T(512)(128)(4,1)}, u32[]{:S(2)}) copy-start(pred[256]{0:T(512)(128)(4,1)} %get-tuple-element.127) | copy-start | bytes 772
  693.4 6.5 collective-permute-start.13
  697.6 6.9 collective-permute-start.14
  704.8 12.4 %copy-start.6 = (bf16[256,1536]{1,0:T(8,128)(2,1)S(1)}, bf16[256,1536]{1,0:T(8,128)(2,1)}, u32[]{:S(2)}) copy-start(bf16[256,1536]{1,0:T(8,128)(2,1)} %copy-done.5) | copy-start | bytes 2359300
  (20 other events, 101.6 us)
Sparse Core Ops, SparseCore 0:
  9.5 195.8 all-gather.8
  207.6 123.1 all-gather.10
  333.0 138.0 all-gather.12
  473.1 78.4 all-gather.14
where the time goes:
time: 730 us; the launch traced here: 725 us
  waiting for transfers between devices  524 us (72%)
  matrix products  106 us (15%)
  starting transfers between devices  46.1 us (6%)
  local copies, waits for them, and re-layouts  19.3 us (3%)
  other arithmetic  15.4 us (2%)
  between operations  14.6 us (2%)
    all_gather x1, waiting for transfers between devices, on_device(): lax.all_gather(triple_projection_matrix[0], 'frame', axis=0, tiled=True)  186 us
    all_gather x1, waiting for transfers between devices, on_device(): lax.all_gather(sigmoid_expand_matrix[0], 'frame', axis=0, tiled=True)  131 us
    ppermute x7, waiting for transfers between devices, extended(): lax.ppermute(lax.slice_in_dim(block, block.shape[dim] - width, None, axis...  119 us
    all_gather x1, waiting for transfers between devices, on_device(): lax.all_gather(combine_channel_matrix[0], 'frame', axis=0, tiled=True)  67.9 us
    dot_general x2, matrix products, on_device(): resid = resid + jnp.dot(act, full_mix, preferred_element_type=jnp.float32)  34.1 us
    ppermute x7, starting transfers between devices, extended(): lax.ppermute(lax.slice_in_dim(block, block.shape[dim] - width, None, axis...  24.1 us
    sub x2, matrix products, attend(): expd = jnp.exp(scores - top)  23.3 us
    ppermute x7, starting transfers between devices, extended(): lax.ppermute(lax.slice_in_dim(block, 0, width, axis=dim), axis, backward)  19.6 us
  transfers between devices with their start and end apart: 19, of which 10 were waited for; matrix products, arithmetic and copies ran while one was open for 8% of the time, Pallas kernels for 0%

commit v1 on v0

v1 whole, which is shorter than its diff:
```python
import jax
import jax.numpy as jnp
from jax import lax
from jax.sharding import PartitionSpec as P

HEADS = 24
KERNEL = 31
EPS = 1e-05
EDGE = 16
AXES = ("section", "frame")


def layer_norm(sample_lines, gain):
    mean = jnp.mean(sample_lines, axis=-1, keepdims=True)
    centred = sample_lines - mean
    spread = jnp.mean(centred * centred, axis=-1, keepdims=True)
    return centred * lax.rsqrt(spread + EPS) * gain


class Layout:
    def __init__(self, sections, frames):
        self.sections, self.frames, self.half = sections, frames, frames // 2
        self.gray = [r ^ (r >> 1) for r in range(self.half)]
        if sorted(self.gray) != list(range(self.half)):
            self.gray = list(range(self.half))

    def flat(self, section, frame):
        return section * self.frames + frame

    def worker(self, section, block):
        pair, high = divmod(section, 2)
        return self.flat(2 * pair + block % 2, high * self.half + self.gray.index(block // 2))

    def each(self):
        return [(s, b) for s in range(self.sections) for b in range(self.frames)]

    def to_workers(self):
        return [(self.flat(s, b), self.worker(s, b)) for s, b in self.each()]

    def to_homes(self):
        return [(there, here) for here, there in self.to_workers()]

    def shifted(self, step):
        return [
            (self.worker(s, b), self.worker(s, b + step))
            for s, b in self.each()
            if 0 <= b + step < self.frames
        ]

    def relay(self):
        return [
            (self.worker(s, b), self.worker(s + 1, b)) for s, b in self.each() if s + 1 < self.sections
        ]

    def first(self):
        return [(self.flat(0, b), self.worker(0, b)) for b in range(self.frames)]

    def rows_to_half(self):
        moves = []
        for s, f in self.each():
            (pair, high), (core, rest) = divmod(s, 2), divmod(f, self.half)
            if core != high:
                moves.append((self.flat(s, f), self.flat(2 * pair + core, high * self.half + rest)))
        return moves

    def flipped(self, section_bit, frame_bits):
        return [(self.flat(s, f), self.flat(s ^ section_bit, f ^ frame_bits)) for s, f in self.each()]

    def diagonal(self):
        return [
            (self.flat(s, f), self.flat(s, f ^ (1 if s % 2 == f // self.half else 2)))
            for s, f in self.each()
        ]

    def groups(self):
        return [
            [self.flat(2 * k + c, h * self.half + r) for c in range(2) for r in range(self.half)]
            for k in range(self.sections // 2)
            for h in range(2)
        ]


def send(value, moves):
    return lax.ppermute(value, AXES, moves)


def gathered(layout, chunks):
    core = lax.axis_index("section") % 2
    rest = lax.axis_index("frame") % layout.half
    at_home = core == lax.axis_index("frame") // layout.half
    held = []
    for chunk in chunks:
        if held:
            chunk, held[-1] = lax.optimization_barrier((chunk, held[-1]))
        held.append(jnp.where(at_home, chunk, send(chunk, layout.rows_to_half())))
    if layout.half != 4:
        return [
            lax.all_gather(own, AXES, axis=0, tiled=True, axis_index_groups=layout.groups())
            for own in held
        ]
    pieces = []
    for own in held:
        cut = own.shape[1] // 2
        along_x = send(own, layout.flipped(0, 1))
        along_z = send(own, layout.flipped(0, 2))
        low = send(along_z[:, :cut], layout.flipped(0, 1))
        high = send(jnp.where(at_home, along_z[:, cut:], along_x[:, cut:]), layout.diagonal())
        pieces.append((own, along_x, along_z, jnp.concatenate([low, high], axis=1)))
    whole = []
    block = jnp.arange(8)
    order = jnp.where(block // 4 == core, 0, 4) + ((block % 4) ^ rest)
    for index, piece in enumerate(pieces):
        near = jnp.stack(piece)
        if index + 1 < len(pieces):
            near, _ = lax.optimization_barrier((near, pieces[index + 1][1]))
        far = send(near, layout.flipped(1, 0))
        both = jnp.concatenate([near, far], axis=0)
        whole.append(both[order].reshape(-1, both.shape[-1]))
    return whole


def attend(query, wide_keys, wide_values, seg_wide, seg_own):
    sample_lines, feature_count = query.shape
    head_dim = feature_count // HEADS
    shaped_q = query.reshape(sample_lines, HEADS, head_dim)
    shaped_k = wide_keys.reshape(wide_keys.shape[0], HEADS, head_dim)
    shaped_v = wide_values.reshape(wide_values.shape[0], HEADS, head_dim)
    scores = jnp.einsum("qhd,khd->hqk", shaped_q, shaped_k, preferred_element_type=jnp.float32)
    allowed = (seg_own[:, None] == seg_wide[None, :])[None]
    scores = jnp.where(allowed, scores, -1e30)
    top = jnp.max(scores, axis=-1, keepdims=True)
    expd = jnp.exp(scores - top)
    probs = (expd / jnp.sum(expd, axis=-1, keepdims=True)).astype(jnp.bfloat16)
    context = jnp.einsum("hqk,khd->qhd", probs, shaped_v, preferred_element_type=jnp.float32)
    return context.astype(jnp.bfloat16).reshape(sample_lines, feature_count)


def depthwise(wide_glu, seg_conv, seg_own, taps):
    sample_lines = seg_own.shape[0]
    total = jnp.zeros((sample_lines, wide_glu.shape[1]), jnp.float32)
    for tap in range(taps.shape[0]):
        same = (seg_conv[tap : tap + sample_lines] == seg_own)[:, None]
        total = total + jnp.where(
            same, wide_glu[tap : tap + sample_lines].astype(jnp.float32) * taps[tap], 0.0
        )
    return total


def tick_of(wide, seg_wide, weights, gains, taps):
    full_qkv, full_out, full_glu, full_mix = weights
    rows, width = wide.shape[0] // 3, wide.shape[1]
    start, stop = rows - EDGE, 2 * rows + EDGE
    half = KERNEL // 2
    resid = wide.astype(jnp.float32)
    normed = layer_norm(resid, gains[0]).astype(jnp.bfloat16)
    query = jnp.dot(normed[start:stop], full_qkv[:, :width], preferred_element_type=jnp.float32)
    query = (query * (width // HEADS) ** (-0.5)).astype(jnp.bfloat16)
    pair = jnp.dot(normed, full_qkv[:, width:], preferred_element_type=jnp.float32).astype(jnp.bfloat16)
    context = attend(query, pair[:, :width], pair[:, width:], seg_wide, seg_wide[start:stop])
    resid = resid[start:stop] + jnp.dot(context, full_out, preferred_element_type=jnp.float32)
    conv_in = layer_norm(resid, gains[1]).astype(jnp.bfloat16)
    doubled = jnp.dot(conv_in, full_glu, preferred_element_type=jnp.float32)
    glu = (doubled[:, :width] * jax.nn.sigmoid(doubled[:, width:])).astype(jnp.bfloat16)
    first = EDGE - half
    depth = depthwise(
        glu[first:], seg_wide[start + first : stop], seg_wide[rows : 2 * rows], taps
    )
    act = (depth * jax.nn.sigmoid(depth)).astype(jnp.bfloat16)
    resid = resid[EDGE : EDGE + rows] + jnp.dot(act, full_mix, preferred_element_type=jnp.float32)
    return resid.astype(jnp.bfloat16)


def on_device(
    layout,
    newcomer_groups,
    pending_inputs,
    speaker_clip_ids,
    selfattend_scaling,
    triple_projection_matrix,
    selfattend_final_matrix,
    depthwise_scaling,
    sigmoid_expand_matrix,
    filter_taps,
    combine_channel_matrix,
):
    rows, width = pending_inputs.shape[1:]
    sections, frames, half = layout.sections, layout.frames, layout.half
    core = lax.axis_index("section") % 2
    pair = lax.axis_index("section") // 2
    high = lax.axis_index("frame") // half
    rest = lax.axis_index("frame") % half
    section = 2 * pair + high
    block = 2 * jnp.asarray(layout.gray)[rest] + core
    ticks = newcomer_groups.shape[0] + 1

    present = send(pending_inputs[0], layout.to_workers())
    newcomers = [send(newcomer_groups[tick], layout.first()) for tick in range(ticks - 1)]
    ids = lax.all_gather(speaker_clip_ids + 1, "frame", axis=1, tiled=True)
    ids = jnp.pad(ids, ((0, 0), (rows, rows)))

    def small(value):
        other = send(value, layout.flipped(1, 0))
        return jnp.where(core == high, value, other)

    gains = (small(selfattend_scaling[0]), small(depthwise_scaling[0]))
    taps = small(filter_taps[0])
    joined = jnp.concatenate([selfattend_final_matrix[0], sigmoid_expand_matrix[0]], axis=1)
    full_qkv, full_joined, full_mix = gathered(
        layout, [triple_projection_matrix[0], joined, combine_channel_matrix[0]]
    )
    weights = (full_qkv, full_joined[:, :width], full_joined[:, width:], full_mix)
    made_all = []
    for tick in range(ticks):
        batch = sections - 1 - section + tick
        seg_wide = lax.dynamic_slice(ids, (batch, block * rows), (1, 3 * rows))[0]
        low = send(present, layout.shifted(1))
        up = send(present, layout.shifted(-1))
        wide = jnp.concatenate([low, present, up], axis=0)
        made = tick_of(wide, seg_wide, weights, gains, taps)
        made_all.append(send(made, layout.to_homes()))
        if tick + 1 < ticks:
            arrived = send(made, layout.relay())
            present = jnp.where(section == 0, newcomers[tick], arrived)
    return jnp.stack(made_all)[:, None]


def solution(mesh):
    layout = Layout(mesh.shape["section"], mesh.shape["frame"])
    in_specs = (
        P(None, "frame", None),
        P("section", "frame", None),
        P(None, "frame"),
        P("section", None),
        P("section", "frame", None),
        P("section", "frame", None),
        P("section", None),
        P("section", "frame", None),
        P("section", None, None),
        P("section", "frame", None),
    )
    out_specs = P(None, "section", "frame", None)

    def local(*args):
        return on_device(layout, *args)

    return jax.shard_map(
        local, mesh=mesh, in_specs=in_specs, out_specs=out_specs, check_vma=False
    )
```

time: 730 us -> 616 us (0.84)
  the two profiles are of different devices: /device:TPU:6 before, /device:TPU:8 now
where the time goes in v1:
time: 616 us; the launch traced here: 609 us
  waiting for transfers between devices  182 us (30%)
  starting transfers between devices  125 us (20%)
  matrix products  125 us (20%)
  other arithmetic  66 us (11%)
  local copies, waits for them, and re-layouts  60.3 us (10%)
  blocking collectives  48.5 us (8%)
    ppermute x30, waiting for transfers between devices, send(): return lax.ppermute(value, AXES, moves)  182 us
    ppermute x30, starting transfers between devices, send(): return lax.ppermute(value, AXES, moves)  125 us
    all_gather x1, blocking collectives, on_device(): ids = lax.all_gather(speaker_clip_ids + 1, 'frame', axis=1, tiled=True)  48.5 us
    gather x3, local copies, waits for them, and re-layouts, gathered(): whole.append(both[order].reshape(-1, both.shape[-1]))  29.7 us
    dot_general x2, matrix products, tick_of(): jnp.dot(act, full_mix, preferred_element_type=jnp.float32)  27 us
    sub x2, matrix products, attend(): expd = jnp.exp(scores - top)  26.8 us
    concatenate x2, other arithmetic, gathered(): both = jnp.concatenate([near, far], axis=0)  24.6 us
    dot_general x2, matrix products, attend(): jnp.einsum('hqk,khd->qhd', probs, shaped_v, preferred_element_type=jnp.fl...  20.1 us
  transfers between devices with their start and end apart: 30, of which 13 were waited for; matrix products, arithmetic and copies ran while one was open for 41% of the time, Pallas kernels for 0%

profile of v1, /device:TPU:8, one launch (start us, length us, event | category | flops | bytes accessed | tf_op | source)
XLA Modules:
  0.0 609.3 jit_solution(7652606165083414951)
XLA Ops:
  0.8 2.9 pad_maximum_fusion.7
  4.0 1.9 collective-permute-start.5
  5.9 3.4 collective-permute-start.25
  9.4 38.0 %collective-permute-start.3 = (f32[1536]{0:T(1024)S(1)}, f32[1536]{0:T(1024)}, u32[]{:S(2)}, u32[]{:S(2)}) collective-permute-start(f32[1536]{0:T(1024)S(1)} %reduce), channel_id=1, source_target_pairs={{0,8},{1,9},{2,10},{3,11},{4,12},{5,13},{6,14},{7,15},{8,0},{9,1},... | collective-permute-start | bytes 18440 | tf_op jit(solution)/shard_map/ppermute | solution.py:84
  50.0 48.5 %all_gather.3 = s32[5,2048]{1,0:T(8,128)S(1)} all-gather(s32[5,256]{1,0:T(8,128)S(1)} %broadcast_add_fusion), channel_id=1, replica_groups=mesh['section'=4,'frame'=8] {'frame'}, dimensions={1}, use_global_device_ids=true | all-gather | bytes 46080 | tf_op jit(solution)/shard_map/all_gather | solution.py:198
  101.0 1.9 collective-permute-start.9
  107.6 2.6 collective-permute-start.18
  111.2 1.9 collective-permute-start
  113.9 1.4 fusion.94
  115.4 2.0 collective-permute-start.7
  117.8 16.7 %collective-permute-done = bf16[256,1536]{1,0:T(8,128)(2,1)S(1)} collective-permute-done((bf16[256,1536]{1,0:T(8,128)(2,1)}, bf16[256,1536]{1,0:T(8,128)(2,1)S(1)}, u32[]{:S(2)}, u32[]{:S(2)}) %collective-permute-start) | collective-permute-done | bytes 786464 | tf_op jit(solution)/shard_map/ppermute | solution.py:84
  134.5 26.0 %collective-permute-start.2 = (bf16[256,1536]{1,0:T(8,128)(2,1)S(1)}, bf16[256,1536]{1,0:T(8,128)(2,1)S(1)}, u32[]{:S(2)}, u32[]{:S(2)}) collective-permute-start(bf16[256,1536]{1,0:T(8,128)(2,1)S(1)} %collective-permute-done), channel_id=1, source_target_pairs={{8,0},{1,8},{9,1},{3,9},{11,3},{2,11},{10,2},{12,4},{5,12},{13,5},... | collective-permute-start | bytes 2359304 | tf_op jit(solution)/shard_map/ppermute | solution.py:84
  160.5 2.0 collective-permute-start.1
  162.6 5.1 pad_maximum_fusion.2
  167.7 9.5 %collective-permute-done.10 = bf16[192,4608]{1,0:T(8,128)(2,1)S(1)} collective-permute-done((bf16[192,4608]{1,0:T(8,128)(2,1)S(1)}, bf16[192,4608]{1,0:T(8,128)(2,1)S(1)}, u32[]{:S(2)}, u32[]{:S(2)}) %collective-permute-start.10) | collective-permute-done | bytes 1769504 | tf_op jit(solution)/shard_map/ppermute | solution.py:84
  177.2 22.6 %collective-permute-start.11 = (bf16[4,192,4608]{2,1,0:T(8,128)(2,1)}, bf16[4,192,4608]{2,1,0:T(8,128)(2,1)}, u32[]{:S(2)}, u32[]{:S(2)}) collective-permute-start(bf16[4,192,4608]{2,1,0:T(8,128)(2,1)} %pad_maximum_fusion.2), channel_id=1, source_target_pairs={{0,8},{1,9},{2,10},{3,11},{4,12},{5,13},{6,14},{7,15},{8,0},{9,1},... | collective-permute-start | bytes 21233672 | tf_op jit(solution)/shard_map/ppermute | solution.py:84
  206.8 2.0 collective-permute-start.20
  208.8 2.0 multiply_convert_fusion.1
  210.8 4.6 collective-permute-done.16
  215.4 46.6 %collective-permute-done.20 = bf16[192,1536]{1,0:T(8,128)(2,1)S(1)} collective-permute-done((bf16[192,1536]{1,0:T(8,128)(2,1)S(1)}, bf16[192,1536]{1,0:T(8,128)(2,1)S(1)}, u32[]{:S(2)}, u32[]{:S(2)}) %collective-permute-start.20) | collective-permute-done | bytes 589856 | tf_op jit(solution)/shard_map/ppermute | solution.py:84
  264.2 2.8 fusion.88
  266.9 3.4 collective-permute-done.22
  270.4 4.8 collective-permute-done.21
  280.5 16.2 %collective-permute-done.14 = bf16[192,2304]{1,0:T(8,128)(2,1)S(1)} collective-permute-done((bf16[192,2304]{1,0:T(8,128)(2,1)S(1)}, bf16[192,2304]{1,0:T(8,128)(2,1)S(1)}, u32[]{:S(2)}, u32[]{:S(2)}) %collective-permute-start.14) | collective-permute-done | bytes 884768 | tf_op jit(solution)/shard_map/ppermute | solution.py:84
  296.7 11.2 %collective-permute-done.13 = bf16[192,2304]{1,0:T(8,128)(2,1)S(1)} collective-permute-done((bf16[192,2304]{1,0:T(8,128)(2,1)S(1)}, bf16[192,2304]{1,0:T(8,128)(2,1)S(1)}, u32[]{:S(2)}, u32[]{:S(2)}) %collective-permute-start.13) | collective-permute-done | bytes 884768 | tf_op jit(solution)/shard_map/ppermute | solution.py:84
  308.0 3.4 pad_maximum_fusion.3
  311.4 1.6 constant_dynamic-update-slice_fusion
  313.0 5.5 gather_fusion.2
  318.5 12.3 %pad_maximum_fusion = bf16[8,192,4608]{2,1,0:T(8,128)(2,1)} fusion(bf16[4,192,4608]{2,1,0:T(8,128)(2,1)} %collective-permute-done.11, bf16[4,192,4608]{2,1,0:T(8,128)(2,1)} %pad_maximum_fusion.2), kind=kLoop, calls=%fused_computation.13 | loop fusion | flops 7077888 | bytes 28311552 | tf_op jit(solution)/shard_map/concatenate | solution.py:117
  330.7 12.1 %gather_fusion = bf16[8,192,4608]{2,1,0:T(8,128)(2,1)} fusion(bf16[8,192,4608]{2,1,0:T(8,128)(2,1)} %pad_maximum_fusion, s32[1024]{0:T(1024)} %pad_clamp_fusion), kind=kCustom, calls=%fused_computation | custom fusion | bytes 28311584 | tf_op jit(solution)/shard_map/gather | solution.py:118
  342.9 10.0 %fusion.26 = bf16[768,3072]{1,0:T(8,128)(2,1)S(1)} fusion(bf16[768,1536]{1,0:T(8,128)(2,1)S(1)} %multiply_convert_fusion.1, bf16[1536,4608]{1,0:T(8,128)(2,1)} %bitcast.76), kind=kOutput, calls=%fused_computation.33 | convolution fusion | flops 7250116608 | bytes 16515072 | tf_op jit(solution)/shard_map/dot_general | solution.py:158
  352.9 1.7 fusion.92
  354.6 4.3 copy.19
  358.9 5.1 fusion.49
  363.9 1.6 copy.20
  365.6 2.4 copy.21
  368.0 13.6 %fusion.96 = (f32[24,288]{1,0:T(8,128)}, f32[24,288,768]{2,1,0:T(8,128)}) fusion(bf16[288,24,64]{0,2,1:T(8,128)(2,1)S(1)} %bitcast.101, bf16[768,24,64]{0,2,1:T(8,128)(2,1)} %bitcast.97, pred[288,768]{1,0:T(8,128)(4,1)} %get-tuple-element.135), kind=kOutput, calls=%fused_computation.309 | convolution fusion | flops 695403264 | bytes 24726528 | tf_op jit(solution)/shard_map/sub | solution.py:132
  381.6 8.9 %fusion.65 = bf16[24,64,288]{2,1,0:T(8,128)(2,1)S(1)} fusion(bf16[768,24,64]{0,2,1:T(8,128)(2,1)S(1)} %bitcast.94, f32[24,288,768]{2,1,0:T(8,128)} %get-tuple-element.131, f32[24,288]{1,0:T(8,128)} %get-tuple-element.130), kind=kOutput, calls=%fused_computation.87 | convolution fusion | flops 690536448 | bytes 24505344 | tf_op jit(solution)/shard_map/hqk,khd->qhd/dot_general | solution.py:134
  390.5 12.3 %pad_maximum_fusion.1 = bf16[8,192,4608]{2,1,0:T(8,128)(2,1)} fusion(bf16[4,192,4608]{2,1,0:T(8,128)(2,1)} %collective-permute-done.17, bf16[4,192,4608]{2,1,0:T(8,128)(2,1)} %pad_maximum_fusion.3), kind=kLoop, calls=%fused_computation.14 | loop fusion | flops 7077888 | bytes 28311552 | tf_op jit(solution)/shard_map/concatenate | solution.py:117
  402.8 12.1 %gather_fusion.1 = bf16[8,192,4608]{2,1,0:T(8,128)(2,1)} fusion(bf16[8,192,4608]{2,1,0:T(8,128)(2,1)} %pad_maximum_fusion.1, s32[1024]{0:T(1024)} %pad_clamp_fusion), kind=kCustom, calls=%fused_computation.1 | custom fusion | bytes 28311584 | tf_op jit(solution)/shard_map/gather | solution.py:118
  414.9 4.7 fusion.90
  420.0 6.2 %fusion.20 = f32[288,3072]{1,0:T(8,128)S(1)} fusion(bf16[1536,4608]{1,0:T(8,128)(2,1)} %bitcast.73, f32[288,1536]{1,0:T(8,128)S(1)} %get-tuple-element.117, f32[1536]{0:T(1024)S(1)} %broadcast_select_fusion.5, f32[288]{0:T(512)S(1)} %add_rsqrt_fusion.3, f32[288]{0:T(512)S(1)} %broadcast_multiply_fusion.3), kind=kOutput, calls=%fused_computation.25 | convolution fusion | flops 2719678464 | bytes 14754048 | tf_op jit(solution)/shard_map/dot_general | solution.py:162
  427.5 14.1 %fusion.52 = bf16[256,1536]{1,0:T(8,128)(2,1)} fusion(bf16[1536,1536]{1,0:T(8,128)(2,1)S(1)} %bitcast.87, f32[288,1536]{1,0:T(8,128)S(1)} %get-tuple-element.117, bf16[288,1536]{1,0:T(8,128)(2,1)S(1)} %fusion.62, f32[1536]{0:T(1024)S(1)} %copy-done.10, f32[1536]{0:T(1024)S(1)} %copy-done.12, f32[1536]{0:T(1024)S(1)} %copy-done.14, f32[1536]{0:T(1024)S(1)} %copy-done.16, ...), kind=kOutput, calls=%fused_computation.55 | convolution fusion | flops 1258684416 | bytes 31720704 | tf_op jit(solution)/shard_map/dot_general | solution.py:169
  441.5 1.5 collective-permute-start.26
  443.1 34.8 %collective-permute-done.26 = bf16[256,1536]{1,0:T(8,128)(2,1)S(1)} collective-permute-done((bf16[256,1536]{1,0:T(8,128)(2,1)}, bf16[256,1536]{1,0:T(8,128)(2,1)S(1)}, u32[]{:S(2)}, u32[]{:S(2)}) %collective-permute-start.26) | collective-permute-done | bytes 786464 | tf_op jit(solution)/shard_map/ppermute | solution.py:84
  479.1 2.0 collective-permute-start.28
  481.1 2.3 collective-permute-start.27
  486.5 4.0 collective-permute-start.24
  490.6 20.7 %collective-permute-done.27 = bf16[256,1536]{1,0:T(8,128)(2,1)S(1)} collective-permute-done((bf16[256,1536]{1,0:T(8,128)(2,1)S(1)}, bf16[256,1536]{1,0:T(8,128)(2,1)S(1)}, u32[]{:S(2)}, u32[]{:S(2)}) %collective-permute-start.27) | collective-permute-done | bytes 786464 | tf_op jit(solution)/shard_map/ppermute | solution.py:84
  512.4 2.0 multiply_convert_fusion
  514.5 10.0 %fusion.29 = bf16[768,3072]{1,0:T(8,128)(2,1)S(1)} fusion(bf16[768,1536]{1,0:T(8,128)(2,1)S(1)} %multiply_convert_fusion, bf16[1536,4608]{1,0:T(8,128)(2,1)} %bitcast.78), kind=kOutput, calls=%fused_computation.34 | convolution fusion | flops 7250116608 | bytes 16515072 | tf_op jit(solution)/shard_map/dot_general | solution.py:158
  524.5 4.8 fusion.46
  529.3 2.5 fusion.91
  531.9 4.3 copy.22
  536.1 1.6 copy.23
  537.8 4.3 copy.24
  542.1 13.2 %fusion.97 = (f32[24,288]{1,0:T(8,128)}, f32[24,288,768]{2,1,0:T(8,128)}) fusion(bf16[288,24,64]{0,2,1:T(8,128)(2,1)S(1)} %bitcast.100, bf16[768,24,64]{0,2,1:T(8,128)(2,1)} %bitcast.96, pred[288,768]{1,0:T(8,128)(4,1)} %get-tuple-element.134), kind=kOutput, calls=%fused_computation.310 | convolution fusion | flops 695403264 | bytes 24726528 | tf_op jit(solution)/shard_map/sub | solution.py:132
  555.3 11.2 %fusion.64 = bf16[24,64,288]{2,1,0:T(8,128)(2,1)S(1)} fusion(bf16[768,24,64]{0,2,1:T(8,128)(2,1)} %bitcast.95, f32[24,288,768]{2,1,0:T(8,128)} %get-tuple-element.133, f32[24,288]{1,0:T(8,128)} %get-tuple-element.132), kind=kOutput, calls=%fused_computation.86 | convolution fusion | flops 690536448 | bytes 24505344 | tf_op jit(solution)/shard_map/hqk,khd->qhd/dot_general | solution.py:134
  567.2 4.1 fusion.89
  571.7 5.9 fusion.18
  578.9 13.0 %fusion.53 = bf16[256,1536]{1,0:T(8,128)(2,1)S(1)} fusion(bf16[1536,1536]{1,0:T(8,128)(2,1)S(1)} %bitcast.90, f32[288,1536]{1,0:T(8,128)S(1)} %get-tuple-element.114, bf16[288,1536]{1,0:T(8,128)(2,1)S(1)} %fusion.63, f32[1536]{0:T(1024)S(1)} %copy-done.11, f32[1536]{0:T(1024)S(1)} %copy-done.13, f32[1536]{0:T(1024)S(1)} %copy-done.15, ...), kind=kOutput, calls=%fused_computation.56 | convolution fusion | flops 1258684416 | bytes 31720704 | tf_op jit(solution)/shard_map/dot_general | solution.py:169
  591.9 1.9 collective-permute-start.29
  593.8 12.8 %collective-permute-done.29 = bf16[256,1536]{1,0:T(8,128)(2,1)S(1)} collective-permute-done((bf16[256,1536]{1,0:T(8,128)(2,1)S(1)}, bf16[256,1536]{1,0:T(8,128)(2,1)S(1)}, u32[]{:S(2)}, u32[]{:S(2)}) %collective-permute-start.29) | collective-permute-done | bytes 786464 | tf_op jit(solution)/shard_map/ppermute | solution.py:84
  606.6 2.4 maximum_bitcast_fusion.2
  (266 shorter events, 35.1 us)
Async XLA Ops:
  0.0 3.7 collective-permute-start.4
  0.8 2.9 copy-start.5
  3.7 5.7 copy-start.70
  3.9 110.0 %collective-permute-start.6 = (bf16[192,4608]{1,0:T(8,128)(2,1)S(1)}, bf16[192,4608]{1,0:T(8,128)(2,1)S(1)}, u32[]{:S(2)}, u32[]{:S(2)}) collective-permute-start(bf16[192,4608]{1,0:T(8,128)(2,1)S(1)} %broadcast_select_fusion.1), channel_id=1, source_target_pairs={{0,2},{1,3},{2,0},{3,1},{4,6},{5,7},{6,4},{7,5},{8,10},{9,11},{10,... | collective-permute-start | bytes 5308424 | tf_op jit(solution)/shard_map/ppermute | solution.py:84
  4.0 109.9 %collective-permute-start.5 = (bf16[192,4608]{1,0:T(8,128)(2,1)S(1)}, bf16[192,4608]{1,0:T(8,128)(2,1)}, u32[]{:S(2)}, u32[]{:S(2)}) collective-permute-start(bf16[192,4608]{1,0:T(8,128)(2,1)S(1)} %broadcast_select_fusion.1), channel_id=1, source_target_pairs={{0,1},{1,0},{2,3},{3,2},{4,5},{5,4},{6,7},{7,6},{8,9},{9,8},{10,11... | collective-permute-start | bytes 5308424 | tf_op jit(solution)/shard_map/ppermute | solution.py:84
  5.9 437.2 %collective-permute-start.25 = (bf16[256,1536]{1,0:T(8,128)(2,1)}, bf16[256,1536]{1,0:T(8,128)(2,1)}, u32[]{:S(2)}, u32[]{:S(2)}) collective-permute-start(bf16[256,1536]{1,0:T(8,128)(2,1)} %bitcast.28), channel_id=1, source_target_pairs={{0,0},{1,8},{2,1},{3,9},{4,3},{5,11},{6,2},{7,10}} | collective-permute-start | bytes 2359304 | tf_op jit(solution)/shard_map/ppermute | solution.py:84
  9.4 98.3 %collective-permute-start.3 = (f32[1536]{0:T(1024)S(1)}, f32[1536]{0:T(1024)}, u32[]{:S(2)}, u32[]{:S(2)}) collective-permute-start(f32[1536]{0:T(1024)S(1)} %reduce), channel_id=1, source_target_pairs={{0,8},{1,9},{2,10},{3,11},{4,12},{5,13},{6,14},{7,15},{8,0},{9,1},... | collective-permute-start | bytes 18440 | tf_op jit(solution)/shard_map/ppermute | solution.py:84
  98.5 4.4 copy-start
  101.0 14.4 %collective-permute-start.9 = (bf16[192,4608]{1,0:T(8,128)(2,1)}, bf16[192,4608]{1,0:T(8,128)(2,1)}, u32[]{:S(2)}, u32[]{:S(2)}) collective-permute-start(bf16[192,4608]{1,0:T(8,128)(2,1)} %pad_maximum_fusion.7), channel_id=1, source_target_pairs={{4,8},{5,9},{6,10},{7,11},{8,4},{9,5},{10,6},{11,7},{20,24},{21,25... | collective-permute-start | bytes 5308424 | tf_op jit(solution)/shard_map/ppermute | solution.py:84
  107.6 3.6 collective-permute-start.18
  111.2 23.2 %collective-permute-start = (bf16[256,1536]{1,0:T(8,128)(2,1)}, bf16[256,1536]{1,0:T(8,128)(2,1)S(1)}, u32[]{:S(2)}, u32[]{:S(2)}) collective-permute-start(bf16[256,1536]{1,0:T(8,128)(2,1)} %bitcast.107), channel_id=1, source_target_pairs={{0,0},{1,8},{2,1},{3,9},{4,3},{5,11},{6,2},{7,10},{8,4},{9,12},{10... | collective-permute-start | bytes 2359304 | tf_op jit(solution)/shard_map/ppermute | solution.py:84
  113.9 3.6 copy-start.2
  113.9 3.8 collective-permute-start.19
  115.3 45.1 %collective-permute-start.8 = (bf16[192,2304]{1,0:T(8,128)(2,1)S(1)}, bf16[192,2304]{1,0:T(8,128)(2,1)S(1)}, u32[]{:S(2)}, u32[]{:S(2)}) collective-permute-start(bf16[192,2304]{1,0:T(8,128)(2,1)S(1)} %get-tuple-element.127), channel_id=1, source_target_pairs={{0,1},{1,0},{2,3},{3,2},{4,6},{5,7},{6,4},{7,5},{8,10},{9,11},{10,... | collective-permute-start | bytes 2654216 | tf_op jit(solution)/shard_map/ppermute | solution.py:84
  115.4 2.4 copy-start.6
  115.4 47.0 %collective-permute-start.7 = (bf16[192,2304]{1,0:T(8,128)(2,1)S(1)}, bf16[192,2304]{1,0:T(8,128)(2,1)S(1)}, u32[]{:S(2)}, u32[]{:S(2)}) collective-permute-start(bf16[192,2304]{1,0:T(8,128)(2,1)S(1)} %get-tuple-element.126), channel_id=1, source_target_pairs={{0,1},{1,0},{2,3},{3,2},{4,5},{5,4},{6,7},{7,6},{8,9},{9,8},{10,11... | collective-permute-start | bytes 2654216 | tf_op jit(solution)/shard_map/ppermute | solution.py:84
  117.6 59.6 %collective-permute-start.10 = (bf16[192,4608]{1,0:T(8,128)(2,1)S(1)}, bf16[192,4608]{1,0:T(8,128)(2,1)S(1)}, u32[]{:S(2)}, u32[]{:S(2)}) collective-permute-start(bf16[192,4608]{1,0:T(8,128)(2,1)S(1)} %broadcast_select_fusion), channel_id=1, source_target_pairs={{0,1},{1,0},{2,3},{3,2},{4,5},{5,4},{6,7},{7,6},{8,9},{9,8},{10,11... | collective-permute-start | bytes 5308424 | tf_op jit(solution)/shard_map/ppermute | solution.py:84
  134.5 67.9 %collective-permute-start.2 = (bf16[256,1536]{1,0:T(8,128)(2,1)S(1)}, bf16[256,1536]{1,0:T(8,128)(2,1)S(1)}, u32[]{:S(2)}, u32[]{:S(2)}) collective-permute-start(bf16[256,1536]{1,0:T(8,128)(2,1)S(1)} %collective-permute-done), channel_id=1, source_target_pairs={{8,0},{1,8},{9,1},{3,9},{11,3},{2,11},{10,2},{12,4},{5,12},{13,5},... | collective-permute-start | bytes 2359304 | tf_op jit(solution)/shard_map/ppermute | solution.py:84
  160.5 41.9 %collective-permute-start.1 = (bf16[256,1536]{1,0:T(8,128)(2,1)S(1)}, bf16[256,1536]{1,0:T(8,128)(2,1)S(1)}, u32[]{:S(2)}, u32[]{:S(2)}) collective-permute-start(bf16[256,1536]{1,0:T(8,128)(2,1)S(1)} %collective-permute-done), channel_id=1, source_target_pairs={{0,8},{8,1},{1,9},{9,3},{3,11},{11,2},{2,10},{4,12},{12,5},{5,13},... | collective-permute-start | bytes 2359304 | tf_op jit(solution)/shard_map/ppermute | solution.py:84
  162.6 38.9 %copy-start.7 = (bf16[1,192,1536]{2,1,0:T(8,128)(2,1)S(1)}, bf16[1,192,1536]{2,1,0:T(8,128)(2,1)}, u32[]{:S(2)}) copy-start(bf16[1,192,1536]{2,1,0:T(8,128)(2,1)} %param.20) | copy-start | bytes 1769476
  177.2 141.2 %collective-permute-start.11 = (bf16[4,192,4608]{2,1,0:T(8,128)(2,1)}, bf16[4,192,4608]{2,1,0:T(8,128)(2,1)}, u32[]{:S(2)}, u32[]{:S(2)}) collective-permute-start(bf16[4,192,4608]{2,1,0:T(8,128)(2,1)} %pad_maximum_fusion.2), channel_id=1, source_target_pairs={{0,8},{1,9},{2,10},{3,11},{4,12},{5,13},{6,14},{7,15},{8,0},{9,1},... | collective-permute-start | bytes 21233672 | tf_op jit(solution)/shard_map/ppermute | solution.py:84
  201.5 3.1 collective-permute-start.15
  203.6 72.1 %collective-permute-start.12 = (bf16[192,4608]{1,0:T(8,128)(2,1)S(1)}, bf16[192,4608]{1,0:T(8,128)(2,1)S(1)}, u32[]{:S(2)}, u32[]{:S(2)}) collective-permute-start(bf16[192,4608]{1,0:T(8,128)(2,1)S(1)} %broadcast_select_fusion), channel_id=1, source_target_pairs={{0,2},{1,3},{2,0},{3,1},{4,6},{5,7},{6,4},{7,5},{8,10},{9,11},{10,... | collective-permute-start | bytes 5308424 | tf_op jit(solution)/shard_map/ppermute | solution.py:84
  205.6 9.9 %collective-permute-start.16 = (bf16[192,1536]{1,0:T(8,128)(2,1)S(1)}, bf16[192,1536]{1,0:T(8,128)(2,1)S(1)}, u32[]{:S(2)}, u32[]{:S(2)}) collective-permute-start(bf16[192,1536]{1,0:T(8,128)(2,1)S(1)} %get-tuple-element.119), channel_id=1, source_target_pairs={{0,1},{1,0},{2,3},{3,2},{4,5},{5,4},{6,7},{7,6},{8,9},{9,8},{10,11... | collective-permute-start | bytes 1769480 | tf_op jit(solution)/shard_map/ppermute | solution.py:84
  206.8 55.2 %collective-permute-start.20 = (bf16[192,1536]{1,0:T(8,128)(2,1)S(1)}, bf16[192,1536]{1,0:T(8,128)(2,1)S(1)}, u32[]{:S(2)}, u32[]{:S(2)}) collective-permute-start(bf16[192,1536]{1,0:T(8,128)(2,1)S(1)} %get-tuple-element.119), channel_id=1, source_target_pairs={{0,2},{1,3},{2,0},{3,1},{4,6},{5,7},{6,4},{7,5},{8,10},{9,11},{10,... | collective-permute-start | bytes 1769480 | tf_op jit(solution)/shard_map/ppermute | solution.py:84
  210.8 132.1 %copy-start.3 = (bf16[768,1536]{1,0:T(8,128)(2,1)}, bf16[768,1536]{1,0:T(8,128)(2,1)S(1)}, u32[]{:S(2)}) copy-start(bf16[768,1536]{1,0:T(8,128)(2,1)S(1)} %multiply_convert_fusion.1) | copy-start | bytes 7077892
  262.1 8.3 %collective-permute-start.22 = (bf16[192,768]{1,0:T(8,128)(2,1)S(1)}, bf16[192,768]{1,0:T(8,128)(2,1)S(1)}, u32[]{:S(2)}, u32[]{:S(2)}) collective-permute-start(bf16[192,768]{1,0:T(8,128)(2,1)S(1)} %get-tuple-element.129), channel_id=1, source_target_pairs={{0,1},{1,0},{2,3},{3,2},{4,6},{5,7},{6,4},{7,5},{8,10},{9,11},{10,... | collective-permute-start | bytes 884744 | tf_op jit(solution)/shard_map/ppermute | solution.py:84
  263.3 11.9 %collective-permute-start.21 = (bf16[192,768]{1,0:T(8,128)(2,1)S(1)}, bf16[192,768]{1,0:T(8,128)(2,1)S(1)}, u32[]{:S(2)}, u32[]{:S(2)}) collective-permute-start(bf16[192,768]{1,0:T(8,128)(2,1)S(1)} %get-tuple-element.128), channel_id=1, source_target_pairs={{0,1},{1,0},{2,3},{3,2},{4,5},{5,4},{6,7},{7,6},{8,9},{9,8},{10,11... | collective-permute-start | bytes 884744 | tf_op jit(solution)/shard_map/ppermute | solution.py:84
  275.5 35.9 %collective-permute-start.23 = (bf16[4,192,1536]{2,1,0:T(8,128)(2,1)S(1)}, bf16[4,192,1536]{2,1,0:T(8,128)(2,1)S(1)}, u32[]{:S(2)}, u32[]{:S(2)}) collective-permute-start(bf16[4,192,1536]{2,1,0:T(8,128)(2,1)S(1)} %pad_maximum_fusion.5), channel_id=1, source_target_pairs={{0,8},{1,9},{2,10},{3,11},{4,12},{5,13},{6,14},{7,15},{8,0},{9,1},... | collective-permute-start | bytes 7077896 | tf_op jit(solution)/shard_map/ppermute | solution.py:84
  275.8 20.9 %collective-permute-start.14 = (bf16[192,2304]{1,0:T(8,128)(2,1)S(1)}, bf16[192,2304]{1,0:T(8,128)(2,1)S(1)}, u32[]{:S(2)}, u32[]{:S(2)}) collective-permute-start(bf16[192,2304]{1,0:T(8,128)(2,1)S(1)} %get-tuple-element.125), channel_id=1, source_target_pairs={{0,1},{1,0},{2,3},{3,2},{4,6},{5,7},{6,4},{7,5},{8,10},{9,11},{10,... | collective-permute-start | bytes 2654216 | tf_op jit(solution)/shard_map/ppermute | solution.py:84
  277.0 30.8 %collective-permute-start.13 = (bf16[192,2304]{1,0:T(8,128)(2,1)S(1)}, bf16[192,2304]{1,0:T(8,128)(2,1)S(1)}, u32[]{:S(2)}, u32[]{:S(2)}) collective-permute-start(bf16[192,2304]{1,0:T(8,128)(2,1)S(1)} %get-tuple-element.124), channel_id=1, source_target_pairs={{0,1},{1,0},{2,3},{3,2},{4,5},{5,4},{6,7},{7,6},{8,9},{9,8},{10,11... | collective-permute-start | bytes 2654216 | tf_op jit(solution)/shard_map/ppermute | solution.py:84
  311.4 79.1 %collective-permute-start.17 = (bf16[4,192,4608]{2,1,0:T(8,128)(2,1)}, bf16[4,192,4608]{2,1,0:T(8,128)(2,1)}, u32[]{:S(2)}, u32[]{:S(2)}) collective-permute-start(bf16[4,192,4608]{2,1,0:T(8,128)(2,1)} %pad_maximum_fusion.3), channel_id=1, source_target_pairs={{0,8},{1,9},{2,10},{3,11},{4,12},{5,13},{6,14},{7,15},{8,0},{9,1},... | collective-permute-start | bytes 21233672 | tf_op jit(solution)/shard_map/ppermute | solution.py:84
  368.0 13.6 %copy-start.4 = (bf16[768,1536]{0,1:T(8,128)(2,1)S(1)}, bf16[768,1536]{0,1:T(8,128)(2,1)}, u32[]{:S(2)}) copy-start(bf16[768,1536]{0,1:T(8,128)(2,1)} %copy.19) | copy-start | bytes 7077892
  414.9 12.1 %slice-start = ((s8[4718592]{0:T(1024)(128)(4,1)}), s8[4194304]{0:T(1024)(128)(4,1)S(1)}, s32[]{:S(2)}) async-start(s8[4718592]{0:T(1024)(128)(4,1)} %bitcast.85), calls=%async_computation | async-start | bytes 8388608
  420.0 7.1 %slice-start.1 = ((s8[4718592]{0:T(1024)(128)(4,1)}), s8[524288]{0:T(1024)(128)(4,1)S(1)}, s32[]{:S(2)}) async-start(s8[4718592]{0:T(1024)(128)(4,1)} %bitcast.85), calls=%async_computation.1 | async-start | bytes 1048576
  426.2 0.9 copy-start.8
  426.2 0.9 copy-start.10
  426.2 0.9 copy-start.12
  426.2 0.9 copy-start.14
  426.2 0.9 copy-start.16
  426.3 0.9 copy-start.18
  426.3 0.9 copy-start.20
  426.3 0.9 copy-start.22
  426.3 0.9 copy-start.24
  426.3 0.9 copy-start.26
  426.3 0.9 copy-start.28
  426.3 0.9 copy-start.30
  426.3 0.9 copy-start.32
  426.3 0.9 copy-start.34
  426.4 0.9 copy-start.36
  426.4 0.9 copy-start.38
  426.4 0.9 copy-start.40
  426.4 0.9 copy-start.42
  426.4 0.9 copy-start.44
  426.4 0.9 copy-start.46
  426.4 0.9 copy-start.48
  441.5 41.9 %copy-start.1 = (s32[5,2048]{1,0:T(8,128)S(1)}, s32[5,2048]{1,0:T(8,128)}, u32[]{:S(2)}) copy-start(s32[5,2048]{1,0:T(8,128)} %copy-done) | copy-start | bytes 122884
  441.5 36.3 %collective-permute-start.26 = (bf16[256,1536]{1,0:T(8,128)(2,1)}, bf16[256,1536]{1,0:T(8,128)(2,1)S(1)}, u32[]{:S(2)}, u32[]{:S(2)}) collective-permute-start(bf16[256,1536]{1,0:T(8,128)(2,1)} %fusion.52), channel_id=1, source_target_pairs={{0,4},{8,12},{1,5},{9,13},{3,7},{11,15},{2,6},{10,14},{4,16},{12,2... | collective-permute-start | bytes 2359304 | tf_op jit(solution)/shard_map/ppermute | solution.py:84
  479.1 11.5 %collective-permute-start.28 = (bf16[256,1536]{1,0:T(8,128)(2,1)S(1)}, bf16[256,1536]{1,0:T(8,128)(2,1)S(1)}, u32[]{:S(2)}, u32[]{:S(2)}) collective-permute-start(bf16[256,1536]{1,0:T(8,128)(2,1)S(1)} %broadcast_select_fusion.2), channel_id=1, source_target_pairs={{8,0},{1,8},{9,1},{3,9},{11,3},{2,11},{10,2},{12,4},{5,12},{13,5},... | collective-permute-start | bytes 2359304 | tf_op jit(solution)/shard_map/ppermute | solution.py:84
  481.1 30.2 %collective-permute-start.27 = (bf16[256,1536]{1,0:T(8,128)(2,1)S(1)}, bf16[256,1536]{1,0:T(8,128)(2,1)S(1)}, u32[]{:S(2)}, u32[]{:S(2)}) collective-permute-start(bf16[256,1536]{1,0:T(8,128)(2,1)S(1)} %broadcast_select_fusion.2), channel_id=1, source_target_pairs={{0,8},{8,1},{1,9},{9,3},{3,11},{11,2},{2,10},{4,12},{12,5},{5,13},... | collective-permute-start | bytes 2359304 | tf_op jit(solution)/shard_map/ppermute | solution.py:84
  486.5 107.3 %collective-permute-start.24 = (bf16[256,1536]{1,0:T(8,128)(2,1)}, bf16[256,1536]{1,0:T(8,128)(2,1)}, u32[]{:S(2)}, u32[]{:S(2)}) collective-permute-start(bf16[256,1536]{1,0:T(8,128)(2,1)} %fusion.52), channel_id=1, source_target_pairs={{0,0},{8,1},{1,2},{9,3},{3,4},{11,5},{2,6},{10,7},{4,8},{12,9},{5,... | collective-permute-start | bytes 2359304 | tf_op jit(solution)/shard_map/ppermute | solution.py:84
  567.2 11.3 %slice-start.2 = ((s8[4718592]{0:T(1024)(128)(4,1)}), s8[4194304]{0:T(1024)(128)(4,1)S(1)}, s32[]{:S(2)}) async-start(s8[4718592]{0:T(1024)(128)(4,1)} %bitcast.88), calls=%async_computation.2 | async-start | bytes 8388608
  571.7 6.8 %slice-start.3 = ((s8[4718592]{0:T(1024)(128)(4,1)}), s8[524288]{0:T(1024)(128)(4,1)S(1)}, s32[]{:S(2)}) async-start(s8[4718592]{0:T(1024)(128)(4,1)} %bitcast.88), calls=%async_computation.3 | async-start | bytes 1048576
  591.9 14.8 %collective-permute-start.29 = (bf16[256,1536]{1,0:T(8,128)(2,1)S(1)}, bf16[256,1536]{1,0:T(8,128)(2,1)S(1)}, u32[]{:S(2)}, u32[]{:S(2)}) collective-permute-start(bf16[256,1536]{1,0:T(8,128)(2,1)S(1)} %fusion.53), channel_id=1, source_target_pairs={{0,0},{8,1},{1,2},{9,3},{3,4},{11,5},{2,6},{10,7},{4,8},{12,9},{5,... | collective-permute-start | bytes 2359304 | tf_op jit(solution)/shard_map/ppermute | solution.py:84
  (55 other events, 48.2 us)

commit v2 on v1

v2 whole, which is shorter than its diff:
```python
import functools

import jax
import jax.numpy as jnp
from jax import lax
from jax.experimental import pallas as pl
from jax.experimental.pallas import tpu as pltpu
from jax.sharding import PartitionSpec as P

HEADS = 24
KERNEL = 31
EPS = 1e-05
EDGE = 16
GROUP = 32
VMEM_BYTES = 56 * 1024 * 1024
AXES = ("section", "frame")


class Layout:
    def __init__(self, sections, frames):
        self.sections, self.frames, self.half = sections, frames, frames // 2
        self.gray = [r ^ (r >> 1) for r in range(self.half)]
        if sorted(self.gray) != list(range(self.half)):
            self.gray = list(range(self.half))

    def flat(self, section, frame):
        return section * self.frames + frame

    def worker(self, section, block):
        pair, high = divmod(section, 2)
        return self.flat(2 * pair + block % 2, high * self.half + self.gray.index(block // 2))

    def each(self):
        return [(s, b) for s in range(self.sections) for b in range(self.frames)]

    def to_workers(self, step=0):
        return [
            (self.flat(s, b + step), self.worker(s, b))
            for s, b in self.each()
            if 0 <= b + step < self.frames
        ]

    def to_homes(self):
        return [(there, here) for here, there in self.to_workers()]

    def shifted(self, step):
        return [
            (self.worker(s, b), self.worker(s, b + step))
            for s, b in self.each()
            if 0 <= b + step < self.frames
        ]

    def relay(self):
        return [
            (self.worker(s, b), self.worker(s + 1, b)) for s, b in self.each() if s + 1 < self.sections
        ]

    def first(self):
        return [(self.flat(0, b), self.worker(0, b)) for b in range(self.frames)]

    def rows_to_half(self):
        moves = []
        for s, f in self.each():
            (pair, high), (core, rest) = divmod(s, 2), divmod(f, self.half)
            if core != high:
                moves.append((self.flat(s, f), self.flat(2 * pair + core, high * self.half + rest)))
        return moves

    def flipped(self, section_bit, frame_bits):
        return [(self.flat(s, f), self.flat(s ^ section_bit, f ^ frame_bits)) for s, f in self.each()]

    def diagonal(self):
        return [
            (self.flat(s, f), self.flat(s, f ^ (1 if s % 2 == f // self.half else 2)))
            for s, f in self.each()
        ]

    def groups(self):
        return [
            [self.flat(2 * k + c, h * self.half + r) for c in range(2) for r in range(self.half)]
            for k in range(self.sections // 2)
            for h in range(2)
        ]


def send(value, moves):
    return lax.ppermute(value, AXES, moves)


def gathered(layout, chunks):
    core = lax.axis_index("section") % 2
    rest = lax.axis_index("frame") % layout.half
    at_home = core == lax.axis_index("frame") // layout.half
    held = []
    for chunk in chunks:
        if held:
            chunk, held[-1] = lax.optimization_barrier((chunk, held[-1]))
        held.append(jnp.where(at_home, chunk, send(chunk, layout.rows_to_half())))
    if layout.half != 4:
        whole = [
            lax.all_gather(own, AXES, axis=0, tiled=True, axis_index_groups=layout.groups())
            for own in held
        ]
        return [(one[None],) for one in whole], jnp.zeros((1,), jnp.int32)
    pieces = []
    for own in held:
        half = own.shape[1] // 2
        along_x = send(own, layout.flipped(0, 1))
        along_z = send(own, layout.flipped(0, 2))
        low = send(along_z[:, :half], layout.flipped(0, 1))
        high = send(jnp.where(at_home, along_z[:, half:], along_x[:, half:]), layout.diagonal())
        pieces.append((own, along_x, along_z, jnp.concatenate([low, high], axis=1)))
    whole = []
    for index, piece in enumerate(pieces):
        near = jnp.stack(piece)
        if index + 1 < len(pieces):
            near, _ = lax.optimization_barrier((near, pieces[index + 1][1]))
        whole.append((near, send(near, layout.flipped(1, 0))))
    near_place = core * 4 + (jnp.arange(4) ^ rest)
    place = jnp.concatenate([near_place, near_place ^ 4])
    return whole, place.astype(jnp.int32) * chunks[0].shape[0]


def cut(total, most):
    return max(w for w in range(128, most + 1, 128) if total % w == 0)


def load_columns(offsets, pieces, target, columns, sem):
    place = 0
    for piece in pieces:
        count, height = piece.shape[:2]
        for index in range(count):
            row = pl.multiple_of(offsets[place], 16)
            place += 1
            pltpu.make_async_copy(
                piece.at[index, :, columns], target.at[pl.ds(row, height), columns], sem
            ).start()


def await_columns(target, columns, sem):
    pltpu.make_async_copy(target.at[:, columns], target.at[:, columns], sem).wait()


def normalised(lines, gain):
    mean = jnp.mean(lines, axis=-1, keepdims=True)
    centred = lines - mean
    spread = jnp.mean(centred * centred, axis=-1, keepdims=True)
    return (centred * lax.rsqrt(spread + EPS) * gain).astype(jnp.bfloat16)


def attention_kernel(
    pieces, offsets, low, own, up, gain, seg_rows, seg_keys, *rest
):
    weight, (context, matrix, normed, query, keys, values, bias, sems) = rest[:pieces], rest[pieces:]
    rows, width = own.shape
    wide, start, queries = 3 * rows, rows - EDGE, rows + 2 * EDGE
    step = cut(width, 768)
    spans = [pl.ds(at, step) for at in range(0, 3 * width, step)]
    for index, span in enumerate(spans):
        load_columns(offsets, weight, matrix, span, sems.at[index])
    for index, block in enumerate((low, own, up)):
        normed[pl.ds(index * rows, rows), :] = normalised(block[...].astype(jnp.float32), gain[...])
    tile, window = queries // 2, 2 * rows + 128
    firsts = (0, wide - window)
    for part in range(2):
        same = seg_rows[pl.ds(part * tile, tile), :] == seg_keys[:, pl.ds(firsts[part], window)]
        sheet = jnp.where(same, 0.0, -1e30)
        bias[part, pl.ds(0, tile), :] = sheet
        bias[part, pl.ds(tile, tile), :] = sheet
    per = width // step
    for index, span in enumerate(spans):
        await_columns(matrix, span, sems.at[index])
        kind, at = divmod(index, per)
        place = pl.ds(at * step, step)
        if kind == 0:
            made = jnp.dot(
                normed[pl.ds(start, queries), :], matrix[:, span], preferred_element_type=jnp.float32
            )
            query[:, place] = (made * (width // HEADS) ** (-0.5)).astype(jnp.bfloat16)
        else:
            made = jnp.dot(normed[...], matrix[:, span], preferred_element_type=jnp.float32)
            (keys if kind == 1 else values)[:, place] = made.astype(jnp.bfloat16)

    head = width // HEADS
    together = 128 // head
    lanes = lax.broadcasted_iota(jnp.int32, (tile, 128), 1) // head

    def heads(index, carry):
        place = pl.ds(pl.multiple_of(index * 128, 128), 128)
        for part in range(2):
            asked = query[pl.ds(part * tile, tile), place]
            stacked = jnp.concatenate(
                [jnp.where(lanes == one, asked, jnp.zeros_like(asked)) for one in range(together)], axis=0
            )
            seen = pl.ds(firsts[part], window)
            scores = lax.dot_general(
                stacked, keys[seen, place], (((1,), (1,)), ((), ())), preferred_element_type=jnp.float32
            )
            scores = scores + bias[part]
            expd = jnp.exp(scores - jnp.max(scores, axis=-1, keepdims=True))
            share = 1.0 / jnp.sum(expd, axis=-1, keepdims=True)
            mixed = jnp.dot(
                expd.astype(jnp.bfloat16), values[seen, place], preferred_element_type=jnp.float32
            ) * share
            result = mixed[:tile]
            for one in range(1, together):
                result = jnp.where(lanes == one, mixed[one * tile : (one + 1) * tile], result)
            context[pl.ds(part * tile, tile), place] = result.astype(jnp.bfloat16)
        return carry

    lax.fori_loop(0, width // 128, heads, 0)


def attention(offsets, weight, low, own, up, gain, seg_wide):
    rows, width = own.shape
    wide, queries = 3 * rows, rows + 2 * EDGE
    spans = 3 * width // cut(width, 768)
    whole = pl.BlockSpec(memory_space=pltpu.VMEM)
    seg_rows = seg_wide[rows - EDGE : 2 * rows + EDGE][:, None]
    return pl.pallas_call(
        functools.partial(attention_kernel, len(weight)),
        out_shape=jax.ShapeDtypeStruct((queries, width), jnp.bfloat16),
        in_specs=[pl.BlockSpec(memory_space=pltpu.SMEM)]
        + [whole] * 6
        + [pl.BlockSpec(memory_space=pl.ANY)] * len(weight),
        out_specs=whole,
        scratch_shapes=[
            pltpu.VMEM((width, 3 * width), jnp.bfloat16),
            pltpu.VMEM((wide, width), jnp.bfloat16),
            pltpu.VMEM((queries, width), jnp.bfloat16),
            pltpu.VMEM((wide, width), jnp.bfloat16),
            pltpu.VMEM((wide, width), jnp.bfloat16),
            pltpu.VMEM((2, queries, 2 * rows + 128), jnp.float32),
            pltpu.SemaphoreType.DMA((spans,)),
        ],
        compiler_params=pltpu.CompilerParams(vmem_limit_bytes=VMEM_BYTES),
        cost_estimate=pl.CostEstimate(
            flops=2 * width * width * (queries + 2 * wide) + 4 * queries * wide * width,
            bytes_accessed=6 * width * width + 8 * rows * width,
            transcendentals=HEADS * queries * wide,
        ),
        name="attention",
    )(offsets, low, own, up, gain, seg_rows, seg_wide[None, :], *weight)


def convolution_kernel(
    pieces, offsets, context, low, own, up, gain, seg_rows, masks_seg, taps, *rest
):
    weight = rest[:pieces]
    act, resid_out, matrix, resid, conv_in, gated, moved, masks, sems = rest[pieces:]
    rows, width = own.shape
    queries = rows + 2 * EDGE
    step = cut(width, 512)
    count = width // step
    outs = [pl.ds(at * step, step) for at in range(count)]
    values = [pl.ds(width + at * step, step) for at in range(count)]
    gates = [pl.ds(2 * width + at * step, step) for at in range(count)]
    order = outs + [span for both in zip(values, gates) for span in both]
    for index, span in enumerate(order):
        load_columns(offsets, weight, matrix, span, sems.at[index])
    half = KERNEL // 2
    for tap in range(KERNEL):
        same = masks_seg[:, tap : tap + 1] == seg_rows[...]
        masks[tap] = jnp.broadcast_to(jnp.where(same, 1.0, 0.0), (rows, 128))
    for index, span in enumerate(outs):
        await_columns(matrix, span, sems.at[index])
        added = jnp.dot(context[...], matrix[:, span], preferred_element_type=jnp.float32)
        resid[pl.ds(0, EDGE), span] = added[:EDGE] + low[pl.ds(rows - EDGE, EDGE), span].astype(jnp.float32)
        resid[pl.ds(EDGE, rows), span] = added[EDGE : EDGE + rows] + own[:, span].astype(jnp.float32)
        resid[pl.ds(EDGE + rows, EDGE), span] = added[EDGE + rows :] + up[pl.ds(0, EDGE), span].astype(
            jnp.float32
        )
    conv_in[...] = normalised(resid[...], gain[...])
    resid_out[...] = resid[pl.ds(EDGE, rows), :]
    for index in range(count):
        await_columns(matrix, values[index], sems.at[count + 2 * index])
        await_columns(matrix, gates[index], sems.at[count + 2 * index + 1])
        value = jnp.dot(conv_in[...], matrix[:, values[index]], preferred_element_type=jnp.float32)
        gate = jnp.dot(conv_in[...], matrix[:, gates[index]], preferred_element_type=jnp.float32)
        glu = (value * jax.nn.sigmoid(gate)).astype(jnp.bfloat16).astype(jnp.float32)
        gated[pl.ds(0, queries), :] = glu
        for shift in range(8):
            moved[shift] = gated[pl.ds(shift, queries), :]

        def lines(group, carry):
            at = pl.multiple_of(group * GROUP, GROUP)
            for lane in range(0, step, 128):
                total = jnp.zeros((GROUP, 128), jnp.float32)
                place = index * step + lane
                for tap in range(KERNEL):
                    first = EDGE - half + tap
                    part = moved[first % 8, pl.ds(at + first // 8 * 8, GROUP), lane : lane + 128]
                    part = part * masks[tap, pl.ds(at, GROUP), :]
                    total = total + part * taps[tap : tap + 1, place : place + 128]
                act[pl.ds(at, GROUP), place : place + 128] = (total * jax.nn.sigmoid(total)).astype(
                    jnp.bfloat16
                )
            return carry

        lax.fori_loop(0, rows // GROUP, lines, 0)


def convolution(offsets, weight, context, low, own, up, gain, seg_wide, taps):
    rows, width = own.shape
    queries = rows + 2 * EDGE
    step = cut(width, 512)
    whole = pl.BlockSpec(memory_space=pltpu.VMEM)
    first = rows - KERNEL // 2
    seg_taps = jnp.stack([seg_wide[first + tap : first + tap + rows] for tap in range(KERNEL)], axis=1)
    return pl.pallas_call(
        functools.partial(convolution_kernel, len(weight)),
        out_shape=(
            jax.ShapeDtypeStruct((rows, width), jnp.bfloat16),
            jax.ShapeDtypeStruct((rows, width), jnp.float32),
        ),
        in_specs=[pl.BlockSpec(memory_space=pltpu.SMEM)]
        + [whole] * 8
        + [pl.BlockSpec(memory_space=pl.ANY)] * len(weight),
        out_specs=(whole, whole),
        scratch_shapes=[
            pltpu.VMEM((width, 3 * width), jnp.bfloat16),
            pltpu.VMEM((queries, width), jnp.float32),
            pltpu.VMEM((queries, width), jnp.bfloat16),
            pltpu.VMEM((queries + 8, step), jnp.float32),
            pltpu.VMEM((8, queries, step), jnp.float32),
            pltpu.VMEM((KERNEL, rows, 128), jnp.float32),
            pltpu.SemaphoreType.DMA((3 * width // step,)),
        ],
        compiler_params=pltpu.CompilerParams(vmem_limit_bytes=VMEM_BYTES),
        cost_estimate=pl.CostEstimate(
            flops=6 * width * width * queries + 3 * KERNEL * rows * width,
            bytes_accessed=6 * width * width + 8 * rows * width,
            transcendentals=2 * rows * width,
        ),
        name="convolution",
    )(
        offsets, context, low, own, up, gain, seg_wide[rows : 2 * rows][:, None], seg_taps, taps, *weight
    )


def mixing_kernel(pieces, offsets, act, resid, *rest):
    weight, (out, matrix, sems) = rest[:pieces], rest[pieces:]
    width = act.shape[1]
    step = cut(width, 512)
    spans = [pl.ds(at, step) for at in range(0, width, step)]
    for index, span in enumerate(spans):
        load_columns(offsets, weight, matrix, span, sems.at[index])
    for index, span in enumerate(spans):
        await_columns(matrix, span, sems.at[index])
        made = jnp.dot(act[...], matrix[:, span], preferred_element_type=jnp.float32)
        out[:, span] = (resid[:, span] + made).astype(jnp.bfloat16)


def mixing(offsets, weight, act, resid):
    rows, width = act.shape
    whole = pl.BlockSpec(memory_space=pltpu.VMEM)
    return pl.pallas_call(
        functools.partial(mixing_kernel, len(weight)),
        out_shape=jax.ShapeDtypeStruct((rows, width), jnp.bfloat16),
        in_specs=[pl.BlockSpec(memory_space=pltpu.SMEM)]
        + [whole] * 2
        + [pl.BlockSpec(memory_space=pl.ANY)] * len(weight),
        out_specs=whole,
        scratch_shapes=[
            pltpu.VMEM((width, width), jnp.bfloat16),
            pltpu.SemaphoreType.DMA((width // cut(width, 512),)),
        ],
        compiler_params=pltpu.CompilerParams(vmem_limit_bytes=VMEM_BYTES),
        cost_estimate=pl.CostEstimate(
            flops=2 * width * width * rows, bytes_accessed=2 * width * width + 8 * rows * width, transcendentals=0
        ),
        name="mixing",
    )(offsets, act, resid, *weight)


def on_device(
    layout,
    newcomer_groups,
    pending_inputs,
    speaker_clip_ids,
    selfattend_scaling,
    triple_projection_matrix,
    selfattend_final_matrix,
    depthwise_scaling,
    sigmoid_expand_matrix,
    filter_taps,
    combine_channel_matrix,
):
    core = lax.axis_index("section") % 2
    high = lax.axis_index("frame") // layout.half
    section = lax.axis_index("section") // 2 * 2 + high
    sections = layout.sections
    ticks = newcomer_groups.shape[0] + 1

    present = send(pending_inputs[0], layout.to_workers())
    newcomers = [send(newcomer_groups[tick], layout.first()) for tick in range(ticks - 1)]
    ids = jnp.concatenate(
        [send(speaker_clip_ids + 1, layout.to_workers(step)) for step in (-1, 0, 1)], axis=1
    )

    def small(value):
        other = send(value, layout.flipped(1, 0))
        return jnp.where(core == high, value, other)

    gain_a, gain_c = small(selfattend_scaling), small(depthwise_scaling)
    taps = small(filter_taps[0])
    joined = jnp.concatenate([selfattend_final_matrix[0], sigmoid_expand_matrix[0]], axis=1)
    (qkv, out_glu, mix), offsets = gathered(
        layout, [triple_projection_matrix[0], joined, combine_channel_matrix[0]]
    )
    made_all = []
    for tick in range(ticks):
        batch = sections - 1 - section + tick
        seg_wide = lax.dynamic_index_in_dim(ids, batch, 0, keepdims=False)
        low = send(present, layout.shifted(1))
        up = send(present, layout.shifted(-1))
        context = attention(offsets, qkv, low, present, up, gain_a, seg_wide)
        act, resid = convolution(offsets, out_glu, context, low, present, up, gain_c, seg_wide, taps)
        made = mixing(offsets, mix, act, resid)
        made_all.append(send(made, layout.to_homes()))
        if tick + 1 < ticks:
            arrived = send(made, layout.relay())
            present = jnp.where(section == 0, newcomers[tick], arrived)
    return jnp.stack(made_all)[:, None]


def solution(mesh):
    layout = Layout(mesh.shape["section"], mesh.shape["frame"])
    in_specs = (
        P(None, "frame", None),
        P("section", "frame", None),
        P(None, "frame"),
        P("section", None),
        P("section", "frame", None),
        P("section", "frame", None),
        P("section", None),
        P("section", "frame", None),
        P("section", None, None),
        P("section", "frame", None),
    )
    out_specs = P(None, "section", "frame", None)

    def local(*args):
        return on_device(layout, *args)

    return jax.shard_map(
        local, mesh=mesh, in_specs=in_specs, out_specs=out_specs, check_vma=False
    )
```

time: 616 us -> 425 us (0.69)
  the two profiles are of different devices: /device:TPU:8 before, /device:TPU:6 now
where the time goes in v2:
time: 425 us; the launch traced here: 417 us
  waiting for transfers between devices  155 us (36%)
  Pallas kernels  118 us (28%)
  starting transfers between devices  115 us (27%)
  other arithmetic  14.7 us (3%)
  local copies, waits for them, and re-layouts  13.5 us (3%)
    ppermute x33, waiting for transfers between devices, send(): return lax.ppermute(value, AXES, moves)  155 us
    ppermute x33, starting transfers between devices, send(): return lax.ppermute(value, AXES, moves)  115 us
    pallas_call x2, Pallas kernels, attention(): pl.pallas_call(functools.partial(attention_kernel, len(weight)), out_shap...  60.4 us
    pallas_call x2, Pallas kernels, convolution(): pl.pallas_call(functools.partial(convolution_kernel, len(weight)), out_sh...  45.7 us
    pallas_call x2, Pallas kernels, mixing(): pl.pallas_call(functools.partial(mixing_kernel, len(weight)), out_shape=j...  11.6 us
  transfers between devices with their start and end apart: 33, of which 11 were waited for; matrix products, arithmetic and copies ran while one was open for 5% of the time, Pallas kernels for 28%

profile of v2, /device:TPU:6, one launch (start us, length us, event | category | flops | bytes accessed | tf_op | source)
XLA Modules:
  0.0 416.7 jit_solution(9956404320708501407)
XLA Ops:
  0.0 0.8 collective-permute-start.7
  0.8 1.7 pad_maximum_fusion.3
  3.0 0.9 collective-permute-start.12
  3.9 1.6 collective-permute-start.9
  6.3 1.6 collective-permute-start.13
  8.3 0.7 collective-permute-start.20
  9.0 35.4 %collective-permute-done.9 = bf16[192,4608]{1,0:T(8,128)(2,1)S(1)} collective-permute-done((bf16[192,4608]{1,0:T(8,128)(2,1)S(1)}, bf16[192,4608]{1,0:T(8,128)(2,1)S(1)}, u32[]{:S(2)}, u32[]{:S(2)}) %collective-permute-start.9) | collective-permute-done | bytes 1769504 | tf_op jit(solution)/shard_map/ppermute | solution.py:87
  44.5 0.6 collective-permute-start.11
  45.1 1.5 collective-permute-start.10
  46.7 0.6 collective-permute-start.21
  47.3 47.8 %collective-permute-done.17 = bf16[192,4608]{1,0:T(8,128)(2,1)S(1)} collective-permute-done((bf16[192,4608]{1,0:T(8,128)(2,1)S(1)}, bf16[192,4608]{1,0:T(8,128)(2,1)S(1)}, u32[]{:S(2)}, u32[]{:S(2)}) %collective-permute-start.17) | collective-permute-done | bytes 1769504 | tf_op jit(solution)/shard_map/ppermute | solution.py:87
  95.2 0.6 collective-permute-start.19
  95.8 1.5 collective-permute-start.18
  97.4 3.5 pad_maximum_fusion.rest_0_
  100.9 42.3 %collective-permute-start.14 = (bf16[4,192,4608]{2,1,0:T(8,128)(2,1)}, bf16[4,192,4608]{2,1,0:T(8,128)(2,1)}, u32[]{:S(2)}, u32[]{:S(2)}) collective-permute-start(bf16[4,192,4608]{2,1,0:T(8,128)(2,1)} %pad_maximum_fusion.rest_0_), channel_id=1, source_target_pairs={{0,8},{1,9},{2,10},{3,11},{4,12},{5,13},{6,14},{7,15},{8,0},{9,1},... | collective-permute-start | bytes 21233672 | tf_op jit(solution)/shard_map/ppermute | solution.py:87
  143.4 3.5 pad_maximum_fusion.1.rest_0_
  146.9 12.2 %collective-permute-start.22 = (bf16[4,192,4608]{2,1,0:T(8,128)(2,1)}, bf16[4,192,4608]{2,1,0:T(8,128)(2,1)}, u32[]{:S(2)}, u32[]{:S(2)}) collective-permute-start(bf16[4,192,4608]{2,1,0:T(8,128)(2,1)} %pad_maximum_fusion.1.rest_0_), channel_id=1, source_target_pairs={{0,8},{1,9},{2,10},{3,11},{4,12},{5,13},{6,14},{7,15},{8,0},{9,1},... | collective-permute-start | bytes 21233672 | tf_op jit(solution)/shard_map/ppermute | solution.py:87
  159.2 0.7 collective-permute-start.4
  159.8 4.5 %collective-permute-start.5 = (s32[5,256]{1,0:T(8,128)S(1)}, s32[5,256]{1,0:T(8,128)S(1)}, u32[]{:S(2)}, u32[]{:S(2)}) collective-permute-start(s32[5,256]{1,0:T(8,128)S(1)} %broadcast_add_fusion), channel_id=1, source_target_pairs={{0,0},{1,8},{2,1},{3,9},{4,3},{5,11},{6,2},{7,10},{8,4},{9,12},{10... | collective-permute-start | bytes 15368 | tf_op jit(solution)/shard_map/ppermute | solution.py:87
  164.3 1.5 collective-permute-start.23
  166.4 0.7 copy.90
  167.1 5.4 %collective-permute-start.6 = (s32[5,256]{1,0:T(8,128)S(1)}, s32[5,256]{1,0:T(8,128)S(1)}, u32[]{:S(2)}, u32[]{:S(2)}) collective-permute-start(s32[5,256]{1,0:T(8,128)S(1)} %broadcast_add_fusion), channel_id=1, source_target_pairs={{1,0},{2,8},{3,1},{4,9},{5,3},{6,11},{7,2},{9,4},{10,12},{11,5},{1... | collective-permute-start | bytes 15368 | tf_op jit(solution)/shard_map/ppermute | solution.py:87
  172.5 1.9 collective-permute-start
  174.5 4.5 %collective-permute-done.6 = s32[5,256]{1,0:T(8,128)S(1)} collective-permute-done((s32[5,256]{1,0:T(8,128)S(1)}, s32[5,256]{1,0:T(8,128)S(1)}, u32[]{:S(2)}, u32[]{:S(2)}) %collective-permute-start.6) | collective-permute-done | bytes 5152 | tf_op jit(solution)/shard_map/ppermute | solution.py:87
  179.1 0.8 copy.79.seg_rows
  179.9 0.9 fusion.2
  180.8 2.0 collective-permute-start.24
  183.0 0.8 copy.80.seg_rows
  183.8 0.7 dynamic-slice_bitcast_fusion.35
  184.5 2.1 stack.277
  186.6 0.8 copy.81.masks_seg
  187.3 0.6 constant_dynamic-slice_fusion
  187.9 5.6 %collective-permute-done.25 = bf16[192,768]{1,0:T(8,128)(2,1)S(1)} collective-permute-done((bf16[192,768]{1,0:T(8,128)(2,1)}, bf16[192,768]{1,0:T(8,128)(2,1)S(1)}, u32[]{:S(2)}, u32[]{:S(2)}) %collective-permute-start.25) | collective-permute-done | bytes 294944 | tf_op jit(solution)/shard_map/ppermute | solution.py:87
  193.5 4.4 %collective-permute-done.24 = bf16[192,768]{1,0:T(8,128)(2,1)S(1)} collective-permute-done((bf16[192,768]{1,0:T(8,128)(2,1)}, bf16[192,768]{1,0:T(8,128)(2,1)S(1)}, u32[]{:S(2)}, u32[]{:S(2)}) %collective-permute-start.24) | collective-permute-done | bytes 294944 | tf_op jit(solution)/shard_map/ppermute | solution.py:87
  198.4 0.6 copy-done.12
  199.5 0.6 broadcast_select_fusion.6.gain
  200.1 2.4 collective-permute-start.1
  202.5 3.1 collective-permute-start.2
  205.7 0.6 broadcast_select_fusion.5.gain
  206.3 0.7 broadcast_select_fusion.4.taps
  207.0 6.4 %collective-permute-done.1.low = bf16[256,1536]{1,0:T(8,128)(2,1)S(1)} collective-permute-done((bf16[256,1536]{1,0:T(8,128)(2,1)S(1)}, bf16[256,1536]{1,0:T(8,128)(2,1)S(1)}, u32[]{:S(2)}, u32[]{:S(2)}) %collective-permute-start.1) | collective-permute-done | bytes 786464 | tf_op jit(solution)/shard_map/ppermute | solution.py:87
  213.4 1.2 collective-permute-start.28
  215.2 0.9 copy-done.8
  216.0 30.2 %attention.2.context = bf16[288,1536]{1,0:T(8,128)(2,1)} custom-call(s32[8]{0:T(128)} %add_multiply_fusion.offsets, bf16[256,1536]{1,0:T(8,128)(2,1)} %copy-done.7, bf16[256,1536]{1,0:T(8,128)(2,1)} %copy-done.4, bf16[256,1536]{1,0:T(8,128)(2,1)} %copy-done.8, f32[1,1536]{1,0:T(1,128)} %broadcast_select_fusion.6.gain, s32[288,1]{1,0:T(8,128)} %copy.79.seg_rows, ...), custom_call_target="tpu_custom_call" | custom-call | flops 9965666304 | bytes 17301504 | tf_op jit(solution)/shard_map/attention/pallas_call | solution.py:220
  246.2 22.9 %convolution.2 = (bf16[256,1536]{1,0:T(8,128)(2,1)}, f32[256,1536]{1,0:T(8,128)}) custom-call(s32[8]{0:T(128)} %add_multiply_fusion.offsets, bf16[288,1536]{1,0:T(8,128)(2,1)} %attention.2.context, bf16[256,1536]{1,0:T(8,128)(2,1)} %copy-done.7, bf16[256,1536]{1,0:T(8,128)(2,1)} %copy-done.4, bf16[256,1536]{1,0:T(8,128)(2,1)} %copy-done.8, ...), custom_call_target="tpu_custom_call" | custom-call | flops 4113432576 | bytes 17301504 | tf_op jit(solution)/shard_map/convolution/pallas_call | solution.py:310
  269.2 1.4 copy-done.1
  270.6 5.8 %mixing.2 = bf16[256,1536]{1,0:T(8,128)(2,1)} custom-call(s32[8]{0:T(128)} %add_multiply_fusion.offsets, bf16[256,1536]{1,0:T(8,128)(2,1)} %get-tuple-element.21.act, f32[256,1536]{1,0:T(8,128)} %get-tuple-element.22.resid, bf16[4,192,1536]{2,1,0:T(8,128)(2,1)} %copy-done, bf16[4,192,1536]{2,1,0:T(8,128)(2,1)} %copy-done.1), custom_call_target="tpu_custom_call" | custom-call | flops 1207959552 | bytes 7864320 | tf_op jit(solution)/shard_map/mixing/pallas_call | solution.py:357
  276.4 4.3 %collective-permute-start.29 = (bf16[256,1536]{1,0:T(8,128)(2,1)}, bf16[256,1536]{1,0:T(8,128)(2,1)S(1)}, u32[]{:S(2)}, u32[]{:S(2)}) collective-permute-start(bf16[256,1536]{1,0:T(8,128)(2,1)} %mixing.2), channel_id=1, source_target_pairs={{0,4},{8,12},{1,5},{9,13},{3,7},{11,15},{2,6},{10,14},{4,16},{12,2... | collective-permute-start | bytes 2359304 | tf_op jit(solution)/shard_map/ppermute | solution.py:87
  280.7 35.7 %collective-permute-done.29 = bf16[256,1536]{1,0:T(8,128)(2,1)S(1)} collective-permute-done((bf16[256,1536]{1,0:T(8,128)(2,1)}, bf16[256,1536]{1,0:T(8,128)(2,1)S(1)}, u32[]{:S(2)}, u32[]{:S(2)}) %collective-permute-start.29) | collective-permute-done | bytes 786464 | tf_op jit(solution)/shard_map/ppermute | solution.py:87
  316.5 3.0 collective-permute-start.30
  319.5 2.6 collective-permute-start.31
  322.1 0.8 copy.82.seg_rows
  322.9 0.8 copy.83.seg_rows
  324.0 0.8 copy.84.masks_seg
  324.7 2.1 collective-permute-start.27
  326.9 3.0 collective-permute-done.30.low
  329.8 1.8 collective-permute-done.31.up
  331.6 0.9 copy-done.6
  332.4 30.2 %attention.3.context = bf16[288,1536]{1,0:T(8,128)(2,1)} custom-call(s32[8]{0:T(128)} %add_multiply_fusion.offsets, bf16[256,1536]{1,0:T(8,128)(2,1)} %copy-done.5, bf16[256,1536]{1,0:T(8,128)(2,1)} %copy-done.2, bf16[256,1536]{1,0:T(8,128)(2,1)} %copy-done.6, f32[1,1536]{1,0:T(1,128)} %broadcast_select_fusion.6.gain, s32[288,1]{1,0:T(8,128)} %copy.82.seg_rows, ...), custom_call_target="tpu_custom_call" | custom-call | flops 9965666304 | bytes 17301504 | tf_op jit(solution)/shard_map/attention/pallas_call | solution.py:220
  362.7 22.9 %convolution.3 = (bf16[256,1536]{1,0:T(8,128)(2,1)}, f32[256,1536]{1,0:T(8,128)}) custom-call(s32[8]{0:T(128)} %add_multiply_fusion.offsets, bf16[288,1536]{1,0:T(8,128)(2,1)} %attention.3.context, bf16[256,1536]{1,0:T(8,128)(2,1)} %copy-done.5, bf16[256,1536]{1,0:T(8,128)(2,1)} %copy-done.2, bf16[256,1536]{1,0:T(8,128)(2,1)} %copy-done.6, ...), custom_call_target="tpu_custom_call" | custom-call | flops 4113432576 | bytes 17301504 | tf_op jit(solution)/shard_map/convolution/pallas_call | solution.py:310
  385.6 5.8 %mixing.3 = bf16[256,1536]{1,0:T(8,128)(2,1)} custom-call(s32[8]{0:T(128)} %add_multiply_fusion.offsets, bf16[256,1536]{1,0:T(8,128)(2,1)} %get-tuple-element.23.act, f32[256,1536]{1,0:T(8,128)} %get-tuple-element.24.resid, bf16[4,192,1536]{2,1,0:T(8,128)(2,1)} %copy-done, bf16[4,192,1536]{2,1,0:T(8,128)(2,1)} %copy-done.1), custom_call_target="tpu_custom_call" | custom-call | flops 1207959552 | bytes 7864320 | tf_op jit(solution)/shard_map/mixing/pallas_call | solution.py:357
  391.4 14.0 %collective-permute-start.32 = (bf16[256,1536]{1,0:T(8,128)(2,1)}, bf16[256,1536]{1,0:T(8,128)(2,1)S(1)}, u32[]{:S(2)}, u32[]{:S(2)}) collective-permute-start(bf16[256,1536]{1,0:T(8,128)(2,1)} %mixing.3), channel_id=1, source_target_pairs={{0,0},{8,1},{1,2},{9,3},{3,4},{11,5},{2,6},{10,7},{4,8},{12,9},{5,... | collective-permute-start | bytes 2359304 | tf_op jit(solution)/shard_map/ppermute | solution.py:87
  405.4 9.8 %collective-permute-done.32 = bf16[256,1536]{1,0:T(8,128)(2,1)S(1)} collective-permute-done((bf16[256,1536]{1,0:T(8,128)(2,1)}, bf16[256,1536]{1,0:T(8,128)(2,1)S(1)}, u32[]{:S(2)}, u32[]{:S(2)}) %collective-permute-start.32) | collective-permute-done | bytes 786464 | tf_op jit(solution)/shard_map/ppermute | solution.py:87
  415.2 1.3 maximum_bitcast_fusion.2
  (78 shorter events, 5.0 us)
Async XLA Ops:
  0.0 2.5 collective-permute-start.7
  0.8 2.0 copy-start.3
  3.0 5.3 %copy-start.11 = (bf16[1,192,1536]{2,1,0:T(8,128)(2,1)S(1)}, bf16[1,192,1536]{2,1,0:T(8,128)(2,1)}, u32[]{:S(2)}) copy-start(bf16[1,192,1536]{2,1,0:T(8,128)(2,1)} %param.19) | copy-start | bytes 1769476
  3.0 3.1 collective-permute-start.12
  3.9 40.4 %collective-permute-start.9 = (bf16[192,4608]{1,0:T(8,128)(2,1)S(1)}, bf16[192,4608]{1,0:T(8,128)(2,1)S(1)}, u32[]{:S(2)}, u32[]{:S(2)}) collective-permute-start(bf16[192,4608]{1,0:T(8,128)(2,1)S(1)} %broadcast_select_fusion.1), channel_id=1, source_target_pairs={{0,2},{1,3},{2,0},{3,1},{4,6},{5,7},{6,4},{7,5},{8,10},{9,11},{10,... | collective-permute-start | bytes 5308424 | tf_op jit(solution)/shard_map/ppermute | solution.py:87
  5.6 38.8 %collective-permute-start.8 = (bf16[192,4608]{1,0:T(8,128)(2,1)S(1)}, bf16[192,4608]{1,0:T(8,128)(2,1)S(1)}, u32[]{:S(2)}, u32[]{:S(2)}) collective-permute-start(bf16[192,4608]{1,0:T(8,128)(2,1)S(1)} %broadcast_select_fusion.1), channel_id=1, source_target_pairs={{0,1},{1,0},{2,3},{3,2},{4,5},{5,4},{6,7},{7,6},{8,9},{9,8},{10,11... | collective-permute-start | bytes 5308424 | tf_op jit(solution)/shard_map/ppermute | solution.py:87
  6.3 41.0 %collective-permute-start.13 = (bf16[192,4608]{1,0:T(8,128)(2,1)S(1)}, bf16[192,4608]{1,0:T(8,128)(2,1)S(1)}, u32[]{:S(2)}, u32[]{:S(2)}) collective-permute-start(bf16[192,4608]{1,0:T(8,128)(2,1)S(1)} %broadcast_select_fusion), channel_id=1, source_target_pairs={{0,1},{1,0},{2,3},{3,2},{4,5},{5,4},{6,7},{7,6},{8,9},{9,8},{10,11... | collective-permute-start | bytes 5308424 | tf_op jit(solution)/shard_map/ppermute | solution.py:87
  7.8 87.2 %collective-permute-start.17 = (bf16[192,4608]{1,0:T(8,128)(2,1)S(1)}, bf16[192,4608]{1,0:T(8,128)(2,1)S(1)}, u32[]{:S(2)}, u32[]{:S(2)}) collective-permute-start(bf16[192,4608]{1,0:T(8,128)(2,1)S(1)} %broadcast_select_fusion), channel_id=1, source_target_pairs={{0,2},{1,3},{2,0},{3,1},{4,6},{5,7},{6,4},{7,5},{8,10},{9,11},{10,... | collective-permute-start | bytes 5308424 | tf_op jit(solution)/shard_map/ppermute | solution.py:87
  8.3 38.3 %collective-permute-start.20 = (bf16[192,1536]{1,0:T(8,128)(2,1)S(1)}, bf16[192,1536]{1,0:T(8,128)(2,1)S(1)}, u32[]{:S(2)}, u32[]{:S(2)}) collective-permute-start(bf16[192,1536]{1,0:T(8,128)(2,1)S(1)} %bitcast.175), channel_id=1, source_target_pairs={{4,8},{5,9},{6,10},{7,11},{8,4},{9,5},{10,6},{11,7},{20,24},{21,25... | collective-permute-start | bytes 1769480 | tf_op jit(solution)/shard_map/ppermute | solution.py:87
  44.5 52.8 %collective-permute-start.11 = (bf16[192,2304]{1,0:T(8,128)(2,1)S(1)}, bf16[192,2304]{1,0:T(8,128)(2,1)S(1)}, u32[]{:S(2)}, u32[]{:S(2)}) collective-permute-start(bf16[192,2304]{1,0:T(8,128)(2,1)S(1)} %get-tuple-element.30), channel_id=1, source_target_pairs={{0,1},{1,0},{2,3},{3,2},{4,6},{5,7},{6,4},{7,5},{8,10},{9,11},{10,... | collective-permute-start | bytes 2654216 | tf_op jit(solution)/shard_map/ppermute | solution.py:87
  45.1 52.2 %collective-permute-start.10 = (bf16[192,2304]{1,0:T(8,128)(2,1)S(1)}, bf16[192,2304]{1,0:T(8,128)(2,1)S(1)}, u32[]{:S(2)}, u32[]{:S(2)}) collective-permute-start(bf16[192,2304]{1,0:T(8,128)(2,1)S(1)} %get-tuple-element.29), channel_id=1, source_target_pairs={{0,1},{1,0},{2,3},{3,2},{4,5},{5,4},{6,7},{7,6},{8,9},{9,8},{10,11... | collective-permute-start | bytes 2654216 | tf_op jit(solution)/shard_map/ppermute | solution.py:87
  46.7 100.2 %collective-permute-start.21 = (bf16[192,1536]{1,0:T(8,128)(2,1)S(1)}, bf16[192,1536]{1,0:T(8,128)(2,1)S(1)}, u32[]{:S(2)}, u32[]{:S(2)}) collective-permute-start(bf16[192,1536]{1,0:T(8,128)(2,1)S(1)} %broadcast_select_fusion.3), channel_id=1, source_target_pairs={{0,1},{1,0},{2,3},{3,2},{4,5},{5,4},{6,7},{7,6},{8,9},{9,8},{10,11... | collective-permute-start | bytes 1769480 | tf_op jit(solution)/shard_map/ppermute | solution.py:87
  95.2 48.0 %collective-permute-start.19 = (bf16[192,2304]{1,0:T(8,128)(2,1)S(1)}, bf16[192,2304]{1,0:T(8,128)(2,1)S(1)}, u32[]{:S(2)}, u32[]{:S(2)}) collective-permute-start(bf16[192,2304]{1,0:T(8,128)(2,1)S(1)} %get-tuple-element.28), channel_id=1, source_target_pairs={{0,1},{1,0},{2,3},{3,2},{4,6},{5,7},{6,4},{7,5},{8,10},{9,11},{10,... | collective-permute-start | bytes 2654216 | tf_op jit(solution)/shard_map/ppermute | solution.py:87
  95.8 47.4 %collective-permute-start.18 = (bf16[192,2304]{1,0:T(8,128)(2,1)S(1)}, bf16[192,2304]{1,0:T(8,128)(2,1)S(1)}, u32[]{:S(2)}, u32[]{:S(2)}) collective-permute-start(bf16[192,2304]{1,0:T(8,128)(2,1)S(1)} %get-tuple-element.27), channel_id=1, source_target_pairs={{0,1},{1,0},{2,3},{3,2},{4,5},{5,4},{6,7},{7,6},{8,9},{9,8},{10,11... | collective-permute-start | bytes 2654216 | tf_op jit(solution)/shard_map/ppermute | solution.py:87
  100.9 114.2 %collective-permute-start.14 = (bf16[4,192,4608]{2,1,0:T(8,128)(2,1)}, bf16[4,192,4608]{2,1,0:T(8,128)(2,1)}, u32[]{:S(2)}, u32[]{:S(2)}) collective-permute-start(bf16[4,192,4608]{2,1,0:T(8,128)(2,1)} %pad_maximum_fusion.rest_0_), channel_id=1, source_target_pairs={{0,8},{1,9},{2,10},{3,11},{4,12},{5,13},{6,14},{7,15},{8,0},{9,1},... | collective-permute-start | bytes 21233672 | tf_op jit(solution)/shard_map/ppermute | solution.py:87
  143.3 15.8 %copy-start.13 = (s32[5,256]{1,0:T(8,128)S(1)}, s32[5,256]{1,0:T(8,128)}, u32[]{:S(2)}) copy-start(s32[5,256]{1,0:T(8,128)} %param.12) | copy-start | bytes 15364
  143.4 23.0 %copy-start.10 = (f32[1,31,1536]{2,0,1:T(1,128)S(1)}, f32[1,31,1536]{2,0,1:T(1,128)}, u32[]{:S(2)}) copy-start(f32[1,31,1536]{2,0,1:T(1,128)} %param.18) | copy-start | bytes 571396
  146.9 46.6 %copy-start.14 = (f32[1,1536]{1,0:T(1,128)S(1)}, f32[1,1536]{1,0:T(1,128)}, u32[]{:S(2)}) copy-start(f32[1,1536]{1,0:T(1,128)} %param.13) | copy-start | bytes 18436
  146.9 51.1 %copy-start.15 = (f32[1,1536]{1,0:T(1,128)S(1)}, f32[1,1536]{1,0:T(1,128)}, u32[]{:S(2)}) copy-start(f32[1,1536]{1,0:T(1,128)} %param.16) | copy-start | bytes 18436
  146.9 99.3 %collective-permute-start.22 = (bf16[4,192,4608]{2,1,0:T(8,128)(2,1)}, bf16[4,192,4608]{2,1,0:T(8,128)(2,1)}, u32[]{:S(2)}, u32[]{:S(2)}) collective-permute-start(bf16[4,192,4608]{2,1,0:T(8,128)(2,1)} %pad_maximum_fusion.1.rest_0_), channel_id=1, source_target_pairs={{0,8},{1,9},{2,10},{3,11},{4,12},{5,13},{6,14},{7,15},{8,0},{9,1},... | collective-permute-start | bytes 21233672 | tf_op jit(solution)/shard_map/ppermute | solution.py:87
  159.2 7.9 %collective-permute-start.4 = (s32[5,256]{1,0:T(8,128)S(1)}, s32[5,256]{1,0:T(8,128)S(1)}, u32[]{:S(2)}, u32[]{:S(2)}) collective-permute-start(s32[5,256]{1,0:T(8,128)S(1)} %broadcast_add_fusion), channel_id=1, source_target_pairs={{0,8},{1,1},{2,9},{3,3},{4,11},{5,2},{6,10},{8,12},{9,5},{10,13},{... | collective-permute-start | bytes 15368 | tf_op jit(solution)/shard_map/ppermute | solution.py:87
  159.8 12.7 %collective-permute-start.5 = (s32[5,256]{1,0:T(8,128)S(1)}, s32[5,256]{1,0:T(8,128)S(1)}, u32[]{:S(2)}, u32[]{:S(2)}) collective-permute-start(s32[5,256]{1,0:T(8,128)S(1)} %broadcast_add_fusion), channel_id=1, source_target_pairs={{0,0},{1,8},{2,1},{3,9},{4,3},{5,11},{6,2},{7,10},{8,4},{9,12},{10... | collective-permute-start | bytes 15368 | tf_op jit(solution)/shard_map/ppermute | solution.py:87
  164.3 15.6 %collective-permute-start.23 = (bf16[192,1536]{1,0:T(8,128)(2,1)S(1)}, bf16[192,1536]{1,0:T(8,128)(2,1)S(1)}, u32[]{:S(2)}, u32[]{:S(2)}) collective-permute-start(bf16[192,1536]{1,0:T(8,128)(2,1)S(1)} %broadcast_select_fusion.3), channel_id=1, source_target_pairs={{0,2},{1,3},{2,0},{3,1},{4,6},{5,7},{6,4},{7,5},{8,10},{9,11},{10,... | collective-permute-start | bytes 1769480 | tf_op jit(solution)/shard_map/ppermute | solution.py:87
  167.1 11.9 %collective-permute-start.6 = (s32[5,256]{1,0:T(8,128)S(1)}, s32[5,256]{1,0:T(8,128)S(1)}, u32[]{:S(2)}, u32[]{:S(2)}) collective-permute-start(s32[5,256]{1,0:T(8,128)S(1)} %broadcast_add_fusion), channel_id=1, source_target_pairs={{1,0},{2,8},{3,1},{4,9},{5,3},{6,11},{7,2},{9,4},{10,12},{11,5},{1... | collective-permute-start | bytes 15368 | tf_op jit(solution)/shard_map/ppermute | solution.py:87
  172.5 27.5 %collective-permute-start = (bf16[256,1536]{1,0:T(8,128)(2,1)}, bf16[256,1536]{1,0:T(8,128)(2,1)S(1)}, u32[]{:S(2)}, u32[]{:S(2)}) collective-permute-start(bf16[256,1536]{1,0:T(8,128)(2,1)} %bitcast.178), channel_id=1, source_target_pairs={{0,0},{1,8},{2,1},{3,9},{4,3},{5,11},{6,2},{7,10},{8,4},{9,12},{10... | collective-permute-start | bytes 2359304 | tf_op jit(solution)/shard_map/ppermute | solution.py:87
  180.8 12.8 %collective-permute-start.25 = (bf16[192,768]{1,0:T(8,128)(2,1)}, bf16[192,768]{1,0:T(8,128)(2,1)S(1)}, u32[]{:S(2)}, u32[]{:S(2)}) collective-permute-start(bf16[192,768]{1,0:T(8,128)(2,1)} %get-tuple-element.32), channel_id=1, source_target_pairs={{0,1},{1,0},{2,3},{3,2},{4,6},{5,7},{6,4},{7,5},{8,10},{9,11},{10,... | collective-permute-start | bytes 884744 | tf_op jit(solution)/shard_map/ppermute | solution.py:87
  180.8 17.2 %collective-permute-start.24 = (bf16[192,768]{1,0:T(8,128)(2,1)}, bf16[192,768]{1,0:T(8,128)(2,1)S(1)}, u32[]{:S(2)}, u32[]{:S(2)}) collective-permute-start(bf16[192,768]{1,0:T(8,128)(2,1)} %get-tuple-element.31), channel_id=1, source_target_pairs={{0,1},{1,0},{2,3},{3,2},{4,5},{5,4},{6,7},{7,6},{8,9},{9,8},{10,11... | collective-permute-start | bytes 884744 | tf_op jit(solution)/shard_map/ppermute | solution.py:87
  193.5 4.8 %collective-permute-start.3 = (f32[1,1536]{1,0:T(1,128)S(1)}, f32[1,1536]{1,0:T(1,128)S(1)}, u32[]{:S(2)}, u32[]{:S(2)}) collective-permute-start(f32[1,1536]{1,0:T(1,128)S(1)} %copy-done.14), channel_id=1, source_target_pairs={{0,8},{1,9},{2,10},{3,11},{4,12},{5,13},{6,14},{7,15},{8,0},{9,1},... | collective-permute-start | bytes 18440 | tf_op jit(solution)/shard_map/ppermute | solution.py:87
  198.0 1.5 collective-permute-start.15
  198.0 0.9 copy-start.12
  198.3 47.9 %copy-start = (bf16[4,192,1536]{2,1,0:T(8,128)(2,1)}, bf16[4,192,1536]{2,1,0:T(8,128)(2,1)S(1)}, u32[]{:S(2)}) copy-start(bf16[4,192,1536]{2,1,0:T(8,128)(2,1)S(1)} %pad_maximum_fusion.2.rest_0_) | copy-start | bytes 7077892
  199.0 3.5 collective-permute-start.16
  199.5 69.7 %collective-permute-start.26 = (bf16[4,192,1536]{2,1,0:T(8,128)(2,1)S(1)}, bf16[4,192,1536]{2,1,0:T(8,128)(2,1)S(1)}, u32[]{:S(2)}, u32[]{:S(2)}) collective-permute-start(bf16[4,192,1536]{2,1,0:T(8,128)(2,1)S(1)} %pad_maximum_fusion.2.rest_0_), channel_id=1, source_target_pairs={{0,8},{1,9},{2,10},{3,11},{4,12},{5,13},{6,14},{7,15},{8,0},{9,1},... | collective-permute-start | bytes 7077896 | tf_op jit(solution)/shard_map/ppermute | solution.py:87
  200.1 15.1 %copy-start.4 = (bf16[256,1536]{1,0:T(8,128)(2,1)}, bf16[256,1536]{1,0:T(8,128)(2,1)S(1)}, u32[]{:S(2)}) copy-start(bf16[256,1536]{1,0:T(8,128)(2,1)S(1)} %collective-permute-done.own) | copy-start | bytes 2359300
  200.1 13.3 %collective-permute-start.1 = (bf16[256,1536]{1,0:T(8,128)(2,1)S(1)}, bf16[256,1536]{1,0:T(8,128)(2,1)S(1)}, u32[]{:S(2)}, u32[]{:S(2)}) collective-permute-start(bf16[256,1536]{1,0:T(8,128)(2,1)S(1)} %collective-permute-done.own), channel_id=1, source_target_pairs={{0,8},{8,1},{1,9},{9,3},{3,11},{11,2},{2,10},{4,12},{12,5},{5,13},... | collective-permute-start | bytes 2359304 | tf_op jit(solution)/shard_map/ppermute | solution.py:87
  202.5 12.6 %collective-permute-start.2 = (bf16[256,1536]{1,0:T(8,128)(2,1)S(1)}, bf16[256,1536]{1,0:T(8,128)(2,1)S(1)}, u32[]{:S(2)}, u32[]{:S(2)}) collective-permute-start(bf16[256,1536]{1,0:T(8,128)(2,1)S(1)} %collective-permute-done.own), channel_id=1, source_target_pairs={{8,0},{1,8},{9,1},{3,9},{11,3},{2,11},{10,2},{12,4},{5,12},{13,5},... | collective-permute-start | bytes 2359304 | tf_op jit(solution)/shard_map/ppermute | solution.py:87
  213.4 1.8 copy-start.7
  213.4 67.3 %collective-permute-start.28 = (bf16[256,1536]{1,0:T(8,128)(2,1)}, bf16[256,1536]{1,0:T(8,128)(2,1)S(1)}, u32[]{:S(2)}, u32[]{:S(2)}) collective-permute-start(bf16[256,1536]{1,0:T(8,128)(2,1)} %bitcast.50), channel_id=1, source_target_pairs={{0,0},{1,8},{2,1},{3,9},{4,3},{5,11},{6,2},{7,10}} | collective-permute-start | bytes 2359304 | tf_op jit(solution)/shard_map/ppermute | solution.py:87
  215.1 0.9 copy-start.8
  269.2 1.4 copy-start.1
  276.4 48.4 %copy-start.9 = (bf16[256,1536]{1,0:T(8,128)(2,1)S(1)}, bf16[256,1536]{1,0:T(8,128)(2,1)}, u32[]{:S(2)}) copy-start(bf16[256,1536]{1,0:T(8,128)(2,1)} %mixing.2) | copy-start | bytes 2359300
  276.4 40.0 %collective-permute-start.29 = (bf16[256,1536]{1,0:T(8,128)(2,1)}, bf16[256,1536]{1,0:T(8,128)(2,1)S(1)}, u32[]{:S(2)}, u32[]{:S(2)}) collective-permute-start(bf16[256,1536]{1,0:T(8,128)(2,1)} %mixing.2), channel_id=1, source_target_pairs={{0,4},{8,12},{1,5},{9,13},{3,7},{11,15},{2,6},{10,14},{4,16},{12,2... | collective-permute-start | bytes 2359304 | tf_op jit(solution)/shard_map/ppermute | solution.py:87
  316.5 15.1 %copy-start.2 = (bf16[256,1536]{1,0:T(8,128)(2,1)}, bf16[256,1536]{1,0:T(8,128)(2,1)S(1)}, u32[]{:S(2)}) copy-start(bf16[256,1536]{1,0:T(8,128)(2,1)S(1)} %broadcast_select_fusion.2.own) | copy-start | bytes 2359300
  316.5 13.3 %collective-permute-start.30 = (bf16[256,1536]{1,0:T(8,128)(2,1)S(1)}, bf16[256,1536]{1,0:T(8,128)(2,1)S(1)}, u32[]{:S(2)}, u32[]{:S(2)}) collective-permute-start(bf16[256,1536]{1,0:T(8,128)(2,1)S(1)} %broadcast_select_fusion.2.own), channel_id=1, source_target_pairs={{0,8},{8,1},{1,9},{9,3},{3,11},{11,2},{2,10},{4,12},{12,5},{5,13},... | collective-permute-start | bytes 2359304 | tf_op jit(solution)/shard_map/ppermute | solution.py:87
  319.5 12.1 %collective-permute-start.31 = (bf16[256,1536]{1,0:T(8,128)(2,1)S(1)}, bf16[256,1536]{1,0:T(8,128)(2,1)S(1)}, u32[]{:S(2)}, u32[]{:S(2)}) collective-permute-start(bf16[256,1536]{1,0:T(8,128)(2,1)S(1)} %broadcast_select_fusion.2.own), channel_id=1, source_target_pairs={{8,0},{1,8},{9,1},{3,9},{11,3},{2,11},{10,2},{12,4},{5,12},{13,5},... | collective-permute-start | bytes 2359304 | tf_op jit(solution)/shard_map/ppermute | solution.py:87
  324.7 80.7 %collective-permute-start.27 = (bf16[256,1536]{1,0:T(8,128)(2,1)S(1)}, bf16[256,1536]{1,0:T(8,128)(2,1)S(1)}, u32[]{:S(2)}, u32[]{:S(2)}) collective-permute-start(bf16[256,1536]{1,0:T(8,128)(2,1)S(1)} %copy-done.9), channel_id=1, source_target_pairs={{0,0},{8,1},{1,2},{9,3},{3,4},{11,5},{2,6},{10,7},{4,8},{12,9},{5,... | collective-permute-start | bytes 2359304 | tf_op jit(solution)/shard_map/ppermute | solution.py:87
  329.8 1.8 copy-start.5
  331.6 0.9 copy-start.6
  391.4 23.8 %collective-permute-start.32 = (bf16[256,1536]{1,0:T(8,128)(2,1)}, bf16[256,1536]{1,0:T(8,128)(2,1)S(1)}, u32[]{:S(2)}, u32[]{:S(2)}) collective-permute-start(bf16[256,1536]{1,0:T(8,128)(2,1)} %mixing.3), channel_id=1, source_target_pairs={{0,0},{8,1},{1,2},{9,3},{3,4},{11,5},{2,6},{10,7},{4,8},{12,9},{5,... | collective-permute-start | bytes 2359304 | tf_op jit(solution)/shard_map/ppermute | solution.py:87

commit v3 on v2

--- a/solution.py
+++ b/solution.py
@@ -87,38 +87,49 @@
     return lax.ppermute(value, AXES, moves)
 
 
-def gathered(layout, chunks):
-    core = lax.axis_index("section") % 2
-    rest = lax.axis_index("frame") % layout.half
-    at_home = core == lax.axis_index("frame") // layout.half
-    held = []
-    for chunk in chunks:
-        if held:
-            chunk, held[-1] = lax.optimization_barrier((chunk, held[-1]))
-        held.append(jnp.where(at_home, chunk, send(chunk, layout.rows_to_half())))
-    if layout.half != 4:
-        whole = [
-            lax.all_gather(own, AXES, axis=0, tiled=True, axis_index_groups=layout.groups())
-            for own in held
-        ]
-        return [(one[None],) for one in whole], jnp.zeros((1,), jnp.int32)
-    pieces = []
-    for own in held:
-        half = own.shape[1] // 2
-        along_x = send(own, layout.flipped(0, 1))
-        along_z = send(own, layout.flipped(0, 2))
-        low = send(along_z[:, :half], layout.flipped(0, 1))
-        high = send(jnp.where(at_home, along_z[:, half:], along_x[:, half:]), layout.diagonal())
-        pieces.append((own, along_x, along_z, jnp.concatenate([low, high], axis=1)))
-    whole = []
-    for index, piece in enumerate(pieces):
-        near = jnp.stack(piece)
-        if index + 1 < len(pieces):
-            near, _ = lax.optimization_barrier((near, pieces[index + 1][1]))
-        whole.append((near, send(near, layout.flipped(1, 0))))
-    near_place = core * 4 + (jnp.arange(4) ^ rest)
-    place = jnp.concatenate([near_place, near_place ^ 4])
-    return whole, place.astype(jnp.int32) * chunks[0].shape[0]
+def behind(value, *earlier):
+    return lax.optimization_barrier((value, earlier))[0]
+
+
+class Weights:
+    def __init__(self, layout):
+        self.layout = layout
+        self.core = lax.axis_index("section") % 2
+        self.rest = lax.axis_index("frame") % layout.half
+        self.at_home = self.core == lax.axis_index("frame") // layout.half
+        self.tree = layout.half == 4
+
+    def to_half(self, chunk):
+        return jnp.where(self.at_home, chunk, send(chunk, self.layout.rows_to_half()))
+
+    def to_sides(self, own):
+        if not self.tree:
+            return own, own
+        return send(own, self.layout.flipped(0, 1)), send(own, self.layout.flipped(0, 2))
+
+    def to_diagonal(self, along_x, along_z):
+        if not self.tree:
+            return along_x, along_z
+        half = along_x.shape[1] // 2
+        low = send(along_z[:, :half], self.layout.flipped(0, 1))
+        high = jnp.where(self.at_home, along_z[:, half:], along_x[:, half:])
+        return low, send(high, self.layout.diagonal())
+
+    def offsets(self, rows):
+        if not self.tree:
+            return jnp.zeros((1,), jnp.int32)
+        near = self.core * 4 + (jnp.arange(4) ^ self.rest)
+        return jnp.concatenate([near, near ^ 4]).astype(jnp.int32) * rows
+
+    def whole(self, own, sides, diagonal, *earlier):
+        if not self.tree:
+            whole = lax.all_gather(
+                own, AXES, axis=0, tiled=True, axis_index_groups=self.layout.groups()
+            )
+            return (whole[None],)
+        own, sides, diagonal = behind((own, sides, diagonal), *earlier)
+        near = jnp.stack([own, *sides, jnp.concatenate(diagonal, axis=1)])
+        return near, send(near, self.layout.flipped(1, 0))
 
 
 def cut(total, most):
@@ -152,14 +163,17 @@
     pieces, offsets, low, own, up, gain, seg_rows, seg_keys, *rest
 ):
     weight, (context, matrix, normed, query, keys, values, bias, sems) = rest[:pieces], rest[pieces:]
-    rows, width = own.shape
-    wide, start, queries = 3 * rows, rows - EDGE, rows + 2 * EDGE
+    queries, width = context.shape
+    rows = queries - 2 * EDGE
+    wide, start = 3 * rows, rows - EDGE
     step = cut(width, 768)
     spans = [pl.ds(at, step) for at in range(0, 3 * width, step)]
     for index, span in enumerate(spans):
         load_columns(offsets, weight, matrix, span, sems.at[index])
     for index, block in enumerate((low, own, up)):
-        normed[pl.ds(index * rows, rows), :] = normalised(block[...].astype(jnp.float32), gain[...])
+        normed[pl.ds(index * rows, rows), :] = normalised(
+            block[pl.ds(0, rows), :].astype(jnp.float32), gain[...]
+        )
     tile, window = queries // 2, 2 * rows + 128
     firsts = (0, wide - window)
     for part in range(2):
@@ -212,7 +226,7 @@
 
 
 def attention(offsets, weight, low, own, up, gain, seg_wide):
-    rows, width = own.shape
+    rows, width = seg_wide.shape[0] // 3, own.shape[1]
     wide, queries = 3 * rows, rows + 2 * EDGE
     spans = 3 * width // cut(width, 768)
     whole = pl.BlockSpec(memory_space=pltpu.VMEM)
@@ -248,7 +262,7 @@
 ):
     weight = rest[:pieces]
     act, resid_out, matrix, resid, conv_in, gated, moved, masks, sems = rest[pieces:]
-    rows, width = own.shape
+    rows, width = act.shape
     queries = rows + 2 * EDGE
     step = cut(width, 512)
     count = width // step
@@ -266,7 +280,7 @@
         await_columns(matrix, span, sems.at[index])
         added = jnp.dot(context[...], matrix[:, span], preferred_element_type=jnp.float32)
         resid[pl.ds(0, EDGE), span] = added[:EDGE] + low[pl.ds(rows - EDGE, EDGE), span].astype(jnp.float32)
-        resid[pl.ds(EDGE, rows), span] = added[EDGE : EDGE + rows] + own[:, span].astype(jnp.float32)
+        resid[pl.ds(EDGE, rows), span] = added[EDGE : EDGE + rows] + own[pl.ds(0, rows), span].astype(jnp.float32)
         resid[pl.ds(EDGE + rows, EDGE), span] = added[EDGE + rows :] + up[pl.ds(0, EDGE), span].astype(
             jnp.float32
         )
@@ -301,7 +315,7 @@
 
 
 def convolution(offsets, weight, context, low, own, up, gain, seg_wide, taps):
-    rows, width = own.shape
+    rows, width = seg_wide.shape[0] // 3, own.shape[1]
     queries = rows + 2 * EDGE
     step = cut(width, 512)
     whole = pl.BlockSpec(memory_space=pltpu.VMEM)
@@ -392,35 +406,56 @@
     sections = layout.sections
     ticks = newcomer_groups.shape[0] + 1
 
-    present = send(pending_inputs[0], layout.to_workers())
-    newcomers = [send(newcomer_groups[tick], layout.first()) for tick in range(ticks - 1)]
-    ids = jnp.concatenate(
-        [send(speaker_clip_ids + 1, layout.to_workers(step)) for step in (-1, 0, 1)], axis=1
-    )
-
-    def small(value):
-        other = send(value, layout.flipped(1, 0))
-        return jnp.where(core == high, value, other)
-
-    gain_a, gain_c = small(selfattend_scaling), small(depthwise_scaling)
-    taps = small(filter_taps[0])
-    joined = jnp.concatenate([selfattend_final_matrix[0], sigmoid_expand_matrix[0]], axis=1)
-    (qkv, out_glu, mix), offsets = gathered(
-        layout, [triple_projection_matrix[0], joined, combine_channel_matrix[0]]
-    )
+    rows, width = pending_inputs.shape[1:]
+    batches = speaker_clip_ids.shape[0]
+    weights = Weights(layout)
+    offsets = weights.offsets(combine_channel_matrix.shape[1])
+
+    small = jnp.concatenate([selfattend_scaling, depthwise_scaling, filter_taps[0]], axis=0)
+    small = jnp.where(core == high, small, send(small, layout.flipped(1, 0)))
+    gain_a, gain_c, taps = small[0:1], small[1:2], small[2:]
+
+    ids = (speaker_clip_ids + 1).astype(jnp.bfloat16)
+    ids = jnp.pad(ids, ((0, -batches % 16), (0, width - rows)))
+    own_1 = weights.to_half(behind(triple_projection_matrix[0], small))
+    packed = jnp.concatenate([pending_inputs[0], ids], axis=0)
+    packed = send(behind(packed, own_1), layout.to_workers())
+    expand = jnp.concatenate([selfattend_final_matrix[0], sigmoid_expand_matrix[0]], axis=1)
+    own_2 = weights.to_half(behind(expand, own_1))
+    own_3 = weights.to_half(behind(combine_channel_matrix[0], own_2))
+    sides_1 = weights.to_sides(own_1)
+    sides_2 = weights.to_sides(behind(own_2, sides_1))
+    packed_out = behind(packed, sides_1)
+    packed = (send(packed_out, layout.shifted(1)), packed, send(packed_out, layout.shifted(-1)))
+    diagonal_1 = weights.to_diagonal(*sides_1)
+    qkv = weights.whole(own_1, sides_1, diagonal_1, packed, own_3)
+    packed = behind(packed, own_3)
+
+    ids = jnp.concatenate([part[rows : rows + batches, :rows] for part in packed], axis=1)
+    ids = ids.astype(jnp.int32)
+    low, present, up = packed
+
     made_all = []
     for tick in range(ticks):
         batch = sections - 1 - section + tick
         seg_wide = lax.dynamic_index_in_dim(ids, batch, 0, keepdims=False)
-        low = send(present, layout.shifted(1))
-        up = send(present, layout.shifted(-1))
         context = attention(offsets, qkv, low, present, up, gain_a, seg_wide)
-        act, resid = convolution(offsets, out_glu, context, low, present, up, gain_c, seg_wide, taps)
+        if tick == 0:
+            diagonal_2 = weights.to_diagonal(*behind(sides_2, context))
+            sides_3 = weights.to_sides(behind(own_3, sides_2, context))
+            out_expand = weights.whole(own_2, sides_2, diagonal_2)
+            diagonal_3 = weights.to_diagonal(*behind(sides_3, diagonal_2))
+            newcomers = behind(newcomer_groups, diagonal_2)
+            newcomers = [send(newcomers[coming], layout.first()) for coming in range(ticks - 1)]
+        act, resid = convolution(offsets, out_expand, context, low, present, up, gain_c, seg_wide, taps)
+        if tick == 0:
+            mix = weights.whole(own_3, sides_3, diagonal_3, act)
         made = mixing(offsets, mix, act, resid)
         made_all.append(send(made, layout.to_homes()))
         if tick + 1 < ticks:
             arrived = send(made, layout.relay())
             present = jnp.where(section == 0, newcomers[tick], arrived)
+            low, up = send(present, layout.shifted(1)), send(present, layout.shifted(-1))
     return jnp.stack(made_all)[:, None]
 
 

time: 425 us -> 423 us (level)
  waiting for transfers between devices: 155 us -> 146 us
  local copies, waits for them, and re-layouts: 13.5 us -> 20.2 us
    ppermute x33 -> x28, waiting for transfers between devices: 155 us -> 146 us  [send(): return lax.ppermute(value, AXES, moves)]
    slice x0 -> x5, local copies, waits for them, and re-layouts: none -> 5.14 us  [the longest x2 3.12 us: on_device(): gain_a, gain_c, taps = (small[0:1], small[1:2], small[2:])]
    ppermute x33 -> x28, starting transfers between devices: 115 us -> 115 us  [send(): return lax.ppermute(value, AXES, moves)]
  transfers between devices with their start and end apart: 33 -> 28, of which waited for: 11 -> 15; matrix products, arithmetic and copies ran while one was open for 5% -> 4% of each run, Pallas kernels for 28% -> 28%
where the time goes in v3:
time: 423 us; the launch traced here: 419 us
  waiting for transfers between devices  146 us (35%)
  Pallas kernels  118 us (28%)
  starting transfers between devices  115 us (27%)
  local copies, waits for them, and re-layouts  20.2 us (5%)
  other arithmetic  18.8 us (4%)
    ppermute x28, waiting for transfers between devices, send(): return lax.ppermute(value, AXES, moves)  146 us
    ppermute x28, starting transfers between devices, send(): return lax.ppermute(value, AXES, moves)  115 us
    pallas_call x2, Pallas kernels, attention(): pl.pallas_call(functools.partial(attention_kernel, len(weight)), out_shap...  60.3 us
    pallas_call x2, Pallas kernels, convolution(): pl.pallas_call(functools.partial(convolution_kernel, len(weight)), out_sh...  45.8 us
    pallas_call x2, Pallas kernels, mixing(): pl.pallas_call(functools.partial(mixing_kernel, len(weight)), out_shape=j...  11.6 us
    another operation x6, other arithmetic, whole(): near = jnp.stack([own, *sides, jnp.concatenate(diagonal, axis=1)])  10.4 us
  transfers between devices with their start and end apart: 28, of which 15 were waited for; matrix products, arithmetic and copies ran while one was open for 4% of the time, Pallas kernels for 28%

profile of v3, /device:TPU:6, one launch (start us, length us, event | category | flops | bytes accessed | tf_op | source)
XLA Modules:
  0.0 418.8 jit_solution(11087324175909742084)
XLA Ops:
  0.0 1.0 copy.88
  1.0 0.8 pad_maximum_fusion.4
  1.9 1.5 collective-permute-done
  3.4 1.4 broadcast_select_fusion.4
  4.8 0.8 collective-permute-start.1
  5.6 1.3 pad_maximum_fusion.3
  7.4 0.8 collective-permute-start.7
  8.2 1.6 collective-permute-start.4
  10.5 47.9 %collective-permute-start.2 = (bf16[272,1536]{1,0:T(8,128)(2,1)S(1)}, bf16[272,1536]{1,0:T(8,128)(2,1)S(1)}, u32[]{:S(2)}, u32[]{:S(2)}) collective-permute-start(bf16[272,1536]{1,0:T(8,128)(2,1)S(1)} %fusion.1), channel_id=1, source_target_pairs={{0,0},{1,8},{2,1},{3,9},{4,3},{5,11},{6,2},{7,10},{8,4},{9,12},{10... | collective-permute-start | bytes 2506760 | tf_op jit(solution)/shard_map/ppermute | solution.py:87
  59.6 2.0 collective-permute-start.9
  61.6 15.8 %collective-permute-done.2.own = bf16[272,1536]{1,0:T(8,128)(2,1)S(1)} collective-permute-done((bf16[272,1536]{1,0:T(8,128)(2,1)S(1)}, bf16[272,1536]{1,0:T(8,128)(2,1)S(1)}, u32[]{:S(2)}, u32[]{:S(2)}) %collective-permute-start.2) | collective-permute-done | bytes 835616 | tf_op jit(solution)/shard_map/ppermute | solution.py:87
  77.4 27.8 %collective-permute-start.6 = (bf16[272,1536]{1,0:T(8,128)(2,1)S(1)}, bf16[272,1536]{1,0:T(8,128)(2,1)S(1)}, u32[]{:S(2)}, u32[]{:S(2)}) collective-permute-start(bf16[272,1536]{1,0:T(8,128)(2,1)S(1)} %collective-permute-done.2.own), channel_id=1, source_target_pairs={{8,0},{1,8},{9,1},{3,9},{11,3},{2,11},{10,2},{12,4},{5,12},{13,5},... | collective-permute-start | bytes 2506760 | tf_op jit(solution)/shard_map/ppermute | solution.py:87
  105.2 2.4 collective-permute-start.5
  107.6 0.9 broadcast_select_fusion.3
  108.6 12.3 %collective-permute-done.6.up = bf16[272,1536]{1,0:T(8,128)(2,1)S(1)} collective-permute-done((bf16[272,1536]{1,0:T(8,128)(2,1)S(1)}, bf16[272,1536]{1,0:T(8,128)(2,1)S(1)}, u32[]{:S(2)}, u32[]{:S(2)}) %collective-permute-start.6) | collective-permute-done | bytes 835616 | tf_op jit(solution)/shard_map/ppermute | solution.py:87
  120.8 2.1 collective-permute-done.5.low
  122.9 0.9 copy-done.7
  124.0 3.5 pad_maximum_fusion.rest_0_
  127.5 9.5 %collective-permute-start.11 = (bf16[4,192,4608]{2,1,0:T(8,128)(2,1)}, bf16[4,192,4608]{2,1,0:T(8,128)(2,1)}, u32[]{:S(2)}, u32[]{:S(2)}) collective-permute-start(bf16[4,192,4608]{2,1,0:T(8,128)(2,1)} %pad_maximum_fusion.rest_0_), channel_id=1, source_target_pairs={{0,8},{1,9},{2,10},{3,11},{4,12},{5,13},{6,14},{7,15},{8,0},{9,1},... | collective-permute-start | bytes 21233672 | tf_op jit(solution)/shard_map/ppermute | solution.py:87
  137.0 1.2 collective-permute-start.13
  138.2 1.6 collective-permute-start.12
  140.4 1.5 fusion.2
  144.6 0.8 copy.79.seg_rows
  145.4 1.4 constant_dynamic-slice_fusion
  146.8 1.4 collective-permute-done.11.rest_1_
  148.2 30.1 %attention.2.context = bf16[288,1536]{1,0:T(8,128)(2,1)} custom-call(s32[8]{0:T(128)} %add_multiply_fusion.offsets, bf16[272,1536]{1,0:T(8,128)(2,1)} %copy-done.7, bf16[272,1536]{1,0:T(8,128)(2,1)} %copy-done.5, bf16[272,1536]{1,0:T(8,128)(2,1)} %copy-done.6, f32[1,1536]{1,0:T(1,128)} %get-tuple-element.82.gain, s32[288,1]{1,0:T(8,128)} %copy.79.seg_rows, ...), custom_call_target="tpu_custom_call" | custom-call | flops 9965666304 | bytes 17301504 | tf_op jit(solution)/shard_map/attention/pallas_call | solution.py:234
  179.0 1.3 slice_select_fusion.1
  180.3 1.6 collective-permute-start.15
  182.4 20.2 %collective-permute-done.15 = bf16[192,2304]{1,0:T(8,128)(2,1)S(1)} collective-permute-done((bf16[192,2304]{1,0:T(8,128)(2,1)S(1)}, bf16[192,2304]{1,0:T(8,128)(2,1)S(1)}, u32[]{:S(2)}, u32[]{:S(2)}) %collective-permute-start.15) | collective-permute-done | bytes 884768 | tf_op jit(solution)/shard_map/ppermute | solution.py:87
  202.6 9.5 %collective-permute-done.14 = bf16[192,2304]{1,0:T(8,128)(2,1)S(1)} collective-permute-done((bf16[192,2304]{1,0:T(8,128)(2,1)S(1)}, bf16[192,2304]{1,0:T(8,128)(2,1)S(1)}, u32[]{:S(2)}, u32[]{:S(2)}) %collective-permute-start.14) | collective-permute-done | bytes 884768 | tf_op jit(solution)/shard_map/ppermute | solution.py:87
  212.2 5.3 %pad_maximum_fusion.1.rest_0_ = bf16[4,192,4608]{2,1,0:T(8,128)(2,1)} fusion(bf16[1,192,4608]{2,1,0:T(8,128)(2,1)S(1)} %maximum_bitcast_fusion.1, bf16[1,192,4608]{2,1,0:T(8,128)(2,1)S(1)} %bitcast.159, bf16[1,192,4608]{2,1,0:T(8,128)(2,1)} %bitcast.42, bf16[1,192,4608]{2,1,0:T(8,128)(2,1)S(1)} %bitcast.158), kind=kLoop, calls=%fused_computation.1 | loop fusion | flops 10616832 | bytes 14155776 | tf_op jit(solution)/shard_map/stack | solution.py:131
  217.6 0.8 collective-permute-start.18
  218.4 1.2 collective-permute-start.17
  219.6 1.6 slice.387.taps
  221.2 1.9 dynamic-slice_bitcast_fusion.19
  223.1 0.8 copy.80.seg_rows
  223.9 1.4 dynamic-slice_bitcast_fusion.35
  225.4 0.8 copy.81.masks_seg
  226.2 7.4 %collective-permute-done.18 = bf16[192,1536]{1,0:T(8,128)(2,1)S(1)} collective-permute-done((bf16[192,1536]{1,0:T(8,128)(2,1)}, bf16[192,1536]{1,0:T(8,128)(2,1)S(1)}, u32[]{:S(2)}, u32[]{:S(2)}) %collective-permute-start.18) | collective-permute-done | bytes 589856 | tf_op jit(solution)/shard_map/ppermute | solution.py:87
  234.1 1.2 collective-permute-start.20
  235.3 0.9 collective-permute-start.19
  236.2 22.9 %convolution.2 = (bf16[256,1536]{1,0:T(8,128)(2,1)}, f32[256,1536]{1,0:T(8,128)}) custom-call(s32[8]{0:T(128)} %add_multiply_fusion.offsets, bf16[288,1536]{1,0:T(8,128)(2,1)} %attention.2.context, bf16[272,1536]{1,0:T(8,128)(2,1)} %copy-done.7, bf16[272,1536]{1,0:T(8,128)(2,1)} %copy-done.5, bf16[272,1536]{1,0:T(8,128)(2,1)} %copy-done.6, ...), custom_call_target="tpu_custom_call" | custom-call | flops 4113432576 | bytes 17301504 | tf_op jit(solution)/shard_map/convolution/pallas_call | solution.py:324
  259.2 1.4 pad_maximum_fusion.2.rest_0_
  260.6 0.7 collective-permute-start.23
  261.3 3.8 collective-permute-done.21.rest_1_
  265.2 1.4 copy-done.1
  266.5 5.8 %mixing.2 = bf16[256,1536]{1,0:T(8,128)(2,1)} custom-call(s32[8]{0:T(128)} %add_multiply_fusion.offsets, bf16[256,1536]{1,0:T(8,128)(2,1)} %get-tuple-element.60.act, f32[256,1536]{1,0:T(8,128)} %get-tuple-element.61.resid, bf16[4,192,1536]{2,1,0:T(8,128)(2,1)} %copy-done, bf16[4,192,1536]{2,1,0:T(8,128)(2,1)} %copy-done.1), custom_call_target="tpu_custom_call" | custom-call | flops 1207959552 | bytes 7864320 | tf_op jit(solution)/shard_map/mixing/pallas_call | solution.py:371
  272.4 2.8 collective-permute-start.24
  275.1 42.4 %collective-permute-done.24 = bf16[256,1536]{1,0:T(8,128)(2,1)S(1)} collective-permute-done((bf16[256,1536]{1,0:T(8,128)(2,1)}, bf16[256,1536]{1,0:T(8,128)(2,1)S(1)}, u32[]{:S(2)}, u32[]{:S(2)}) %collective-permute-start.24) | collective-permute-done | bytes 786464 | tf_op jit(solution)/shard_map/ppermute | solution.py:87
  317.7 1.9 collective-permute-start.26
  319.6 2.4 collective-permute-start.25
  322.0 0.8 copy.83.seg_rows
  323.1 0.8 copy.84.masks_seg
  323.8 0.8 copy.82.seg_rows
  324.6 2.1 collective-permute-start.22
  326.8 2.3 collective-permute-done.26.up
  329.1 6.5 %collective-permute-done.25.low = bf16[256,1536]{1,0:T(8,128)(2,1)S(1)} collective-permute-done((bf16[256,1536]{1,0:T(8,128)(2,1)S(1)}, bf16[256,1536]{1,0:T(8,128)(2,1)S(1)}, u32[]{:S(2)}, u32[]{:S(2)}) %collective-permute-start.25) | collective-permute-done | bytes 786464 | tf_op jit(solution)/shard_map/ppermute | solution.py:87
  335.6 0.9 copy-done.9
  336.5 30.3 %attention.3.context = bf16[288,1536]{1,0:T(8,128)(2,1)} custom-call(s32[8]{0:T(128)} %add_multiply_fusion.offsets, bf16[256,1536]{1,0:T(8,128)(2,1)} %copy-done.9, bf16[256,1536]{1,0:T(8,128)(2,1)} %copy-done.2, bf16[256,1536]{1,0:T(8,128)(2,1)} %copy-done.8, f32[1,1536]{1,0:T(1,128)} %get-tuple-element.82.gain, s32[288,1]{1,0:T(8,128)} %copy.82.seg_rows, ...), custom_call_target="tpu_custom_call" | custom-call | flops 9965666304 | bytes 17301504 | tf_op jit(solution)/shard_map/attention/pallas_call | solution.py:234
  366.7 22.9 %convolution.3 = (bf16[256,1536]{1,0:T(8,128)(2,1)}, f32[256,1536]{1,0:T(8,128)}) custom-call(s32[8]{0:T(128)} %add_multiply_fusion.offsets, bf16[288,1536]{1,0:T(8,128)(2,1)} %attention.3.context, bf16[256,1536]{1,0:T(8,128)(2,1)} %copy-done.9, bf16[256,1536]{1,0:T(8,128)(2,1)} %copy-done.2, bf16[256,1536]{1,0:T(8,128)(2,1)} %copy-done.8, ...), custom_call_target="tpu_custom_call" | custom-call | flops 4113432576 | bytes 17301504 | tf_op jit(solution)/shard_map/convolution/pallas_call | solution.py:324
  389.6 5.8 %mixing.3 = bf16[256,1536]{1,0:T(8,128)(2,1)} custom-call(s32[8]{0:T(128)} %add_multiply_fusion.offsets, bf16[256,1536]{1,0:T(8,128)(2,1)} %get-tuple-element.71.act, f32[256,1536]{1,0:T(8,128)} %get-tuple-element.72.resid, bf16[4,192,1536]{2,1,0:T(8,128)(2,1)} %copy-done, bf16[4,192,1536]{2,1,0:T(8,128)(2,1)} %copy-done.1), custom_call_target="tpu_custom_call" | custom-call | flops 1207959552 | bytes 7864320 | tf_op jit(solution)/shard_map/mixing/pallas_call | solution.py:371
  395.4 1.9 collective-permute-start.27
  397.3 19.9 %collective-permute-done.27 = bf16[256,1536]{1,0:T(8,128)(2,1)S(1)} collective-permute-done((bf16[256,1536]{1,0:T(8,128)(2,1)}, bf16[256,1536]{1,0:T(8,128)(2,1)S(1)}, u32[]{:S(2)}, u32[]{:S(2)}) %collective-permute-start.27) | collective-permute-done | bytes 786464 | tf_op jit(solution)/shard_map/ppermute | solution.py:87
  417.2 1.3 maximum_bitcast_fusion.2
  (71 shorter events, 8.2 us)
Async XLA Ops:
  0.0 5.6 %copy-start.4 = (bf16[1,192,3072]{2,1,0:T(8,128)(2,1)S(1)}, bf16[1,192,3072]{2,1,0:T(8,128)(2,1)}, u32[]{:S(2)}) copy-start(bf16[1,192,3072]{2,1,0:T(8,128)(2,1)} %param.17) | copy-start | bytes 3538948
  1.8 1.6 collective-permute-start
  4.8 2.1 collective-permute-start.1
  5.6 1.7 copy-start.3
  6.9 3.5 copy-start.15
  6.9 3.5 copy-start.10
  7.4 50.9 %collective-permute-start.7 = (bf16[192,4608]{1,0:T(8,128)(2,1)S(1)}, bf16[192,4608]{1,0:T(8,128)(2,1)S(1)}, u32[]{:S(2)}, u32[]{:S(2)}) collective-permute-start(bf16[192,4608]{1,0:T(8,128)(2,1)S(1)} %pad_maximum_fusion.3), channel_id=1, source_target_pairs={{4,8},{5,9},{6,10},{7,11},{8,4},{9,5},{10,6},{11,7},{20,24},{21,25... | collective-permute-start | bytes 5308424 | tf_op jit(solution)/shard_map/ppermute | solution.py:87
  8.2 51.1 %collective-permute-start.4 = (bf16[192,4608]{1,0:T(8,128)(2,1)S(1)}, bf16[192,4608]{1,0:T(8,128)(2,1)S(1)}, u32[]{:S(2)}, u32[]{:S(2)}) collective-permute-start(bf16[192,4608]{1,0:T(8,128)(2,1)S(1)} %broadcast_select_fusion.1), channel_id=1, source_target_pairs={{0,2},{1,3},{2,0},{3,1},{4,6},{5,7},{6,4},{7,5},{8,10},{9,11},{10,... | collective-permute-start | bytes 5308424 | tf_op jit(solution)/shard_map/ppermute | solution.py:87
  9.9 49.4 %collective-permute-start.3 = (bf16[192,4608]{1,0:T(8,128)(2,1)S(1)}, bf16[192,4608]{1,0:T(8,128)(2,1)S(1)}, u32[]{:S(2)}, u32[]{:S(2)}) collective-permute-start(bf16[192,4608]{1,0:T(8,128)(2,1)S(1)} %broadcast_select_fusion.1), channel_id=1, source_target_pairs={{0,1},{1,0},{2,3},{3,2},{4,5},{5,4},{6,7},{7,6},{8,9},{9,8},{10,11... | collective-permute-start | bytes 5308424 | tf_op jit(solution)/shard_map/ppermute | solution.py:87
  10.5 48.1 %copy-start.12 = (bf16[1,192,1536]{2,1,0:T(8,128)(2,1)S(1)}, bf16[1,192,1536]{2,1,0:T(8,128)(2,1)}, u32[]{:S(2)}) copy-start(bf16[1,192,1536]{2,1,0:T(8,128)(2,1)} %param.19) | copy-start | bytes 1769476
  10.5 66.9 %collective-permute-start.2 = (bf16[272,1536]{1,0:T(8,128)(2,1)S(1)}, bf16[272,1536]{1,0:T(8,128)(2,1)S(1)}, u32[]{:S(2)}, u32[]{:S(2)}) collective-permute-start(bf16[272,1536]{1,0:T(8,128)(2,1)S(1)} %fusion.1), channel_id=1, source_target_pairs={{0,0},{1,8},{2,1},{3,9},{4,3},{5,11},{6,2},{7,10},{8,4},{9,12},{10... | collective-permute-start | bytes 2506760 | tf_op jit(solution)/shard_map/ppermute | solution.py:87
  58.6 49.0 %collective-permute-start.8 = (bf16[192,1536]{1,0:T(8,128)(2,1)S(1)}, bf16[192,1536]{1,0:T(8,128)(2,1)S(1)}, u32[]{:S(2)}, u32[]{:S(2)}) collective-permute-start(bf16[192,1536]{1,0:T(8,128)(2,1)S(1)} %bitcast.174), channel_id=1, source_target_pairs={{4,8},{5,9},{6,10},{7,11},{8,4},{9,5},{10,6},{11,7},{20,24},{21,25... | collective-permute-start | bytes 1769480 | tf_op jit(solution)/shard_map/ppermute | solution.py:87
  59.5 63.5 %collective-permute-start.10 = (bf16[192,2304]{1,0:T(8,128)(2,1)S(1)}, bf16[192,2304]{1,0:T(8,128)(2,1)S(1)}, u32[]{:S(2)}, u32[]{:S(2)}) collective-permute-start(bf16[192,2304]{1,0:T(8,128)(2,1)S(1)} %get-tuple-element.77), channel_id=1, source_target_pairs={{0,1},{1,0},{2,3},{3,2},{4,6},{5,7},{6,4},{7,5},{8,10},{9,11},{10,... | collective-permute-start | bytes 2654216 | tf_op jit(solution)/shard_map/ppermute | solution.py:87
  59.6 64.3 %collective-permute-start.9 = (bf16[192,2304]{1,0:T(8,128)(2,1)S(1)}, bf16[192,2304]{1,0:T(8,128)(2,1)S(1)}, u32[]{:S(2)}, u32[]{:S(2)}) collective-permute-start(bf16[192,2304]{1,0:T(8,128)(2,1)S(1)} %get-tuple-element.78), channel_id=1, source_target_pairs={{0,1},{1,0},{2,3},{3,2},{4,5},{5,4},{6,7},{7,6},{8,9},{9,8},{10,11... | collective-permute-start | bytes 2654216 | tf_op jit(solution)/shard_map/ppermute | solution.py:87
  77.4 46.5 %copy-start.5 = (bf16[272,1536]{1,0:T(8,128)(2,1)}, bf16[272,1536]{1,0:T(8,128)(2,1)S(1)}, u32[]{:S(2)}) copy-start(bf16[272,1536]{1,0:T(8,128)(2,1)S(1)} %collective-permute-done.2.own) | copy-start | bytes 2506756
  77.4 43.4 %collective-permute-start.6 = (bf16[272,1536]{1,0:T(8,128)(2,1)S(1)}, bf16[272,1536]{1,0:T(8,128)(2,1)S(1)}, u32[]{:S(2)}, u32[]{:S(2)}) collective-permute-start(bf16[272,1536]{1,0:T(8,128)(2,1)S(1)} %collective-permute-done.2.own), channel_id=1, source_target_pairs={{8,0},{1,8},{9,1},{3,9},{11,3},{2,11},{10,2},{12,4},{5,12},{13,5},... | collective-permute-start | bytes 2506760 | tf_op jit(solution)/shard_map/ppermute | solution.py:87
  105.2 17.8 %collective-permute-start.5 = (bf16[272,1536]{1,0:T(8,128)(2,1)S(1)}, bf16[272,1536]{1,0:T(8,128)(2,1)S(1)}, u32[]{:S(2)}, u32[]{:S(2)}) collective-permute-start(bf16[272,1536]{1,0:T(8,128)(2,1)S(1)} %collective-permute-done.2.own), channel_id=1, source_target_pairs={{0,8},{8,1},{1,9},{9,3},{3,11},{11,2},{2,10},{4,12},{12,5},{5,13},... | collective-permute-start | bytes 2506760 | tf_op jit(solution)/shard_map/ppermute | solution.py:87
  120.8 2.1 copy-start.6
  122.9 0.9 copy-start.7
  127.5 20.8 %collective-permute-start.11 = (bf16[4,192,4608]{2,1,0:T(8,128)(2,1)}, bf16[4,192,4608]{2,1,0:T(8,128)(2,1)}, u32[]{:S(2)}, u32[]{:S(2)}) collective-permute-start(bf16[4,192,4608]{2,1,0:T(8,128)(2,1)} %pad_maximum_fusion.rest_0_), channel_id=1, source_target_pairs={{0,8},{1,9},{2,10},{3,11},{4,12},{5,13},{6,14},{7,15},{8,0},{9,1},... | collective-permute-start | bytes 21233672 | tf_op jit(solution)/shard_map/ppermute | solution.py:87
  137.0 41.3 %collective-permute-start.13 = (bf16[192,4608]{1,0:T(8,128)(2,1)S(1)}, bf16[192,4608]{1,0:T(8,128)(2,1)S(1)}, u32[]{:S(2)}, u32[]{:S(2)}) collective-permute-start(bf16[192,4608]{1,0:T(8,128)(2,1)S(1)} %broadcast_select_fusion), channel_id=1, source_target_pairs={{0,2},{1,3},{2,0},{3,1},{4,6},{5,7},{6,4},{7,5},{8,10},{9,11},{10,... | collective-permute-start | bytes 5308424 | tf_op jit(solution)/shard_map/ppermute | solution.py:87
  138.2 40.8 %collective-permute-start.12 = (bf16[192,4608]{1,0:T(8,128)(2,1)S(1)}, bf16[192,4608]{1,0:T(8,128)(2,1)}, u32[]{:S(2)}, u32[]{:S(2)}) collective-permute-start(bf16[192,4608]{1,0:T(8,128)(2,1)S(1)} %broadcast_select_fusion), channel_id=1, source_target_pairs={{0,1},{1,0},{2,3},{3,2},{4,5},{5,4},{6,7},{7,6},{8,9},{9,8},{10,11... | collective-permute-start | bytes 5308424 | tf_op jit(solution)/shard_map/ppermute | solution.py:87
  143.9 0.6 copy-start.13
  180.3 22.3 %collective-permute-start.15 = (bf16[192,2304]{1,0:T(8,128)(2,1)S(1)}, bf16[192,2304]{1,0:T(8,128)(2,1)S(1)}, u32[]{:S(2)}, u32[]{:S(2)}) collective-permute-start(bf16[192,2304]{1,0:T(8,128)(2,1)S(1)} %get-tuple-element.75), channel_id=1, source_target_pairs={{0,1},{1,0},{2,3},{3,2},{4,6},{5,7},{6,4},{7,5},{8,10},{9,11},{10,... | collective-permute-start | bytes 2654216 | tf_op jit(solution)/shard_map/ppermute | solution.py:87
  181.9 30.2 %collective-permute-start.14 = (bf16[192,2304]{1,0:T(8,128)(2,1)S(1)}, bf16[192,2304]{1,0:T(8,128)(2,1)S(1)}, u32[]{:S(2)}, u32[]{:S(2)}) collective-permute-start(bf16[192,2304]{1,0:T(8,128)(2,1)S(1)} %get-tuple-element.76), channel_id=1, source_target_pairs={{0,1},{1,0},{2,3},{3,2},{4,5},{5,4},{6,7},{7,6},{8,9},{9,8},{10,11... | collective-permute-start | bytes 2654216 | tf_op jit(solution)/shard_map/ppermute | solution.py:87
  217.5 18.7 %collective-permute-start.16 = (bf16[4,192,4608]{2,1,0:T(8,128)(2,1)}, bf16[4,192,4608]{2,1,0:T(8,128)(2,1)}, u32[]{:S(2)}, u32[]{:S(2)}) collective-permute-start(bf16[4,192,4608]{2,1,0:T(8,128)(2,1)} %pad_maximum_fusion.1.rest_0_), channel_id=1, source_target_pairs={{0,8},{1,9},{2,10},{3,11},{4,12},{5,13},{6,14},{7,15},{8,0},{9,1},... | collective-permute-start | bytes 21233672 | tf_op jit(solution)/shard_map/ppermute | solution.py:87
  217.6 16.0 %collective-permute-start.18 = (bf16[192,1536]{1,0:T(8,128)(2,1)}, bf16[192,1536]{1,0:T(8,128)(2,1)S(1)}, u32[]{:S(2)}, u32[]{:S(2)}) collective-permute-start(bf16[192,1536]{1,0:T(8,128)(2,1)} %broadcast_select_fusion.3), channel_id=1, source_target_pairs={{0,2},{1,3},{2,0},{3,1},{4,6},{5,7},{6,4},{7,5},{8,10},{9,11},{10,... | collective-permute-start | bytes 1769480 | tf_op jit(solution)/shard_map/ppermute | solution.py:87
  218.4 15.6 %collective-permute-start.17 = (bf16[192,1536]{1,0:T(8,128)(2,1)}, bf16[192,1536]{1,0:T(8,128)(2,1)S(1)}, u32[]{:S(2)}, u32[]{:S(2)}) collective-permute-start(bf16[192,1536]{1,0:T(8,128)(2,1)} %broadcast_select_fusion.3), channel_id=1, source_target_pairs={{0,1},{1,0},{2,3},{3,2},{4,5},{5,4},{6,7},{7,6},{8,9},{9,8},{10,11... | collective-permute-start | bytes 1769480 | tf_op jit(solution)/shard_map/ppermute | solution.py:87
  234.1 25.0 %collective-permute-start.20 = (bf16[192,768]{1,0:T(8,128)(2,1)S(1)}, bf16[192,768]{1,0:T(8,128)(2,1)S(1)}, u32[]{:S(2)}, u32[]{:S(2)}) collective-permute-start(bf16[192,768]{1,0:T(8,128)(2,1)S(1)} %get-tuple-element.79), channel_id=1, source_target_pairs={{0,1},{1,0},{2,3},{3,2},{4,6},{5,7},{6,4},{7,5},{8,10},{9,11},{10,... | collective-permute-start | bytes 884744 | tf_op jit(solution)/shard_map/ppermute | solution.py:87
  235.3 23.8 %collective-permute-start.19 = (bf16[192,768]{1,0:T(8,128)(2,1)S(1)}, bf16[192,768]{1,0:T(8,128)(2,1)S(1)}, u32[]{:S(2)}, u32[]{:S(2)}) collective-permute-start(bf16[192,768]{1,0:T(8,128)(2,1)S(1)} %get-tuple-element.80), channel_id=1, source_target_pairs={{0,1},{1,0},{2,3},{3,2},{4,5},{5,4},{6,7},{7,6},{8,9},{9,8},{10,11... | collective-permute-start | bytes 884744 | tf_op jit(solution)/shard_map/ppermute | solution.py:87
  260.5 4.6 %copy-start = (bf16[4,192,1536]{2,1,0:T(8,128)(2,1)}, bf16[4,192,1536]{2,1,0:T(8,128)(2,1)S(1)}, u32[]{:S(2)}) copy-start(bf16[4,192,1536]{2,1,0:T(8,128)(2,1)S(1)} %pad_maximum_fusion.2.rest_0_) | copy-start | bytes 7077892
  260.6 4.6 %collective-permute-start.21 = (bf16[4,192,1536]{2,1,0:T(8,128)(2,1)S(1)}, bf16[4,192,1536]{2,1,0:T(8,128)(2,1)S(1)}, u32[]{:S(2)}, u32[]{:S(2)}) collective-permute-start(bf16[4,192,1536]{2,1,0:T(8,128)(2,1)S(1)} %pad_maximum_fusion.2.rest_0_), channel_id=1, source_target_pairs={{0,8},{1,9},{2,10},{3,11},{4,12},{5,13},{6,14},{7,15},{8,0},{9,1},... | collective-permute-start | bytes 7077896 | tf_op jit(solution)/shard_map/ppermute | solution.py:87
  260.6 14.5 %collective-permute-start.23 = (bf16[256,1536]{1,0:T(8,128)(2,1)}, bf16[256,1536]{1,0:T(8,128)(2,1)S(1)}, u32[]{:S(2)}, u32[]{:S(2)}) collective-permute-start(bf16[256,1536]{1,0:T(8,128)(2,1)} %bitcast.50), channel_id=1, source_target_pairs={{0,0},{1,8},{2,1},{3,9},{4,3},{5,11},{6,2},{7,10}} | collective-permute-start | bytes 2359304 | tf_op jit(solution)/shard_map/ppermute | solution.py:87
  265.2 1.4 copy-start.1
  272.3 50.5 %copy-start.14 = (s32[5,768]{1,0:T(8,128)S(1)}, s32[5,768]{1,0:T(8,128)}, u32[]{:S(2)}) copy-start(s32[5,768]{1,0:T(8,128)} %copy-done.13) | copy-start | bytes 46084
  272.3 52.3 %copy-start.11 = (bf16[256,1536]{1,0:T(8,128)(2,1)S(1)}, bf16[256,1536]{1,0:T(8,128)(2,1)}, u32[]{:S(2)}) copy-start(bf16[256,1536]{1,0:T(8,128)(2,1)} %mixing.2) | copy-start | bytes 2359300
  272.4 45.2 %collective-permute-start.24 = (bf16[256,1536]{1,0:T(8,128)(2,1)}, bf16[256,1536]{1,0:T(8,128)(2,1)S(1)}, u32[]{:S(2)}, u32[]{:S(2)}) collective-permute-start(bf16[256,1536]{1,0:T(8,128)(2,1)} %mixing.2), channel_id=1, source_target_pairs={{0,4},{8,12},{1,5},{9,13},{3,7},{11,15},{2,6},{10,14},{4,16},{12,2... | collective-permute-start | bytes 2359304 | tf_op jit(solution)/shard_map/ppermute | solution.py:87
  317.6 17.9 %copy-start.2 = (bf16[256,1536]{1,0:T(8,128)(2,1)}, bf16[256,1536]{1,0:T(8,128)(2,1)S(1)}, u32[]{:S(2)}) copy-start(bf16[256,1536]{1,0:T(8,128)(2,1)S(1)} %broadcast_select_fusion.2.own) | copy-start | bytes 2359300
  317.7 11.4 %collective-permute-start.26 = (bf16[256,1536]{1,0:T(8,128)(2,1)S(1)}, bf16[256,1536]{1,0:T(8,128)(2,1)S(1)}, u32[]{:S(2)}, u32[]{:S(2)}) collective-permute-start(bf16[256,1536]{1,0:T(8,128)(2,1)S(1)} %broadcast_select_fusion.2.own), channel_id=1, source_target_pairs={{8,0},{1,8},{9,1},{3,9},{11,3},{2,11},{10,2},{12,4},{5,12},{13,5},... | collective-permute-start | bytes 2359304 | tf_op jit(solution)/shard_map/ppermute | solution.py:87
  319.6 16.0 %collective-permute-start.25 = (bf16[256,1536]{1,0:T(8,128)(2,1)S(1)}, bf16[256,1536]{1,0:T(8,128)(2,1)S(1)}, u32[]{:S(2)}, u32[]{:S(2)}) collective-permute-start(bf16[256,1536]{1,0:T(8,128)(2,1)S(1)} %broadcast_select_fusion.2.own), channel_id=1, source_target_pairs={{0,8},{8,1},{1,9},{9,3},{3,11},{11,2},{2,10},{4,12},{12,5},{5,13},... | collective-permute-start | bytes 2359304 | tf_op jit(solution)/shard_map/ppermute | solution.py:87
  324.6 72.7 %collective-permute-start.22 = (bf16[256,1536]{1,0:T(8,128)(2,1)S(1)}, bf16[256,1536]{1,0:T(8,128)(2,1)S(1)}, u32[]{:S(2)}, u32[]{:S(2)}) collective-permute-start(bf16[256,1536]{1,0:T(8,128)(2,1)S(1)} %copy-done.11), channel_id=1, source_target_pairs={{0,0},{8,1},{1,2},{9,3},{3,4},{11,5},{2,6},{10,7},{4,8},{12,9},{5,... | collective-permute-start | bytes 2359304 | tf_op jit(solution)/shard_map/ppermute | solution.py:87
  329.1 6.5 %copy-start.8 = (bf16[256,1536]{1,0:T(8,128)(2,1)}, bf16[256,1536]{1,0:T(8,128)(2,1)S(1)}, u32[]{:S(2)}) copy-start(bf16[256,1536]{1,0:T(8,128)(2,1)S(1)} %collective-permute-done.26.up) | copy-start | bytes 2359300
  335.6 0.9 copy-start.9
  395.4 21.8 %collective-permute-start.27 = (bf16[256,1536]{1,0:T(8,128)(2,1)}, bf16[256,1536]{1,0:T(8,128)(2,1)S(1)}, u32[]{:S(2)}, u32[]{:S(2)}) collective-permute-start(bf16[256,1536]{1,0:T(8,128)(2,1)} %mixing.3), channel_id=1, source_target_pairs={{0,0},{8,1},{1,2},{9,3},{3,4},{11,5},{2,6},{10,7},{4,8},{12,9},{5,... | collective-permute-start | bytes 2359304 | tf_op jit(solution)/shard_map/ppermute | solution.py:87

commit v4 on v3

--- a/solution.py
+++ b/solution.py
@@ -13,6 +13,7 @@
 EDGE = 16
 GROUP = 32
 VMEM_BYTES = 56 * 1024 * 1024
+TICK_VMEM_BYTES = 60 * 1024 * 1024
 AXES = ("section", "frame")
 
 
@@ -159,10 +160,14 @@
     return (centred * lax.rsqrt(spread + EPS) * gain).astype(jnp.bfloat16)
 
 
-def attention_kernel(
-    pieces, offsets, low, own, up, gain, seg_rows, seg_keys, *rest
+def attention_kernel(pieces, offsets, low, own, up, gain, seg_rows, seg_keys, *rest):
+    attend(offsets, rest[:pieces], low, own, up, gain, seg_rows, seg_keys, *rest[pieces:])
+
+
+def attend(
+    offsets, weight, low, own, up, gain, seg_rows, seg_keys,
+    context, matrix, normed, query, keys, values, bias, sems, asked_all=None, projected=None,
 ):
-    weight, (context, matrix, normed, query, keys, values, bias, sems) = rest[:pieces], rest[pieces:]
     queries, width = context.shape
     rows = queries - 2 * EDGE
     wide, start = 3 * rows, rows - EDGE
@@ -170,6 +175,8 @@
     spans = [pl.ds(at, step) for at in range(0, 3 * width, step)]
     for index, span in enumerate(spans):
         load_columns(offsets, weight, matrix, span, sems.at[index])
+    if asked_all is not None:
+        asked_all()
     for index, block in enumerate((low, own, up)):
         normed[pl.ds(index * rows, rows), :] = normalised(
             block[pl.ds(0, rows), :].astype(jnp.float32), gain[...]
@@ -195,9 +202,12 @@
             made = jnp.dot(normed[...], matrix[:, span], preferred_element_type=jnp.float32)
             (keys if kind == 1 else values)[:, place] = made.astype(jnp.bfloat16)
 
+    if projected is not None:
+        projected()
     head = width // HEADS
     together = 128 // head
     lanes = lax.broadcasted_iota(jnp.int32, (tile, 128), 1) // head
+    ones = jnp.ones((window, 128), jnp.bfloat16)
 
     def heads(index, carry):
         place = pl.ds(pl.multiple_of(index * 128, 128), 128)
@@ -212,17 +222,16 @@
             )
             scores = scores + bias[part]
             expd = jnp.exp(scores - jnp.max(scores, axis=-1, keepdims=True))
-            share = 1.0 / jnp.sum(expd, axis=-1, keepdims=True)
-            mixed = jnp.dot(
-                expd.astype(jnp.bfloat16), values[seen, place], preferred_element_type=jnp.float32
-            ) * share
+            shown = jnp.concatenate([values[seen, place], ones], axis=1)
+            mixed = jnp.dot(expd.astype(jnp.bfloat16), shown, preferred_element_type=jnp.float32)
+            mixed = mixed[:, :128] / mixed[:, 128:]
             result = mixed[:tile]
             for one in range(1, together):
                 result = jnp.where(lanes == one, mixed[one * tile : (one + 1) * tile], result)
             context[pl.ds(part * tile, tile), place] = result.astype(jnp.bfloat16)
         return carry
 
-    lax.fori_loop(0, width // 128, heads, 0)
+    lax.fori_loop(0, width // 128, heads, 0, unroll=2)
 
 
 def attention(offsets, weight, low, own, up, gain, seg_wide):
@@ -260,18 +269,33 @@
 def convolution_kernel(
     pieces, offsets, context, low, own, up, gain, seg_rows, masks_seg, taps, *rest
 ):
-    weight = rest[:pieces]
-    act, resid_out, matrix, resid, conv_in, gated, moved, masks, sems = rest[pieces:]
+    weight, (act, resid_out, matrix, resid, *scratch) = rest[:pieces], rest[pieces:]
+    ask_for_expansion(offsets, weight, matrix, scratch[-1])
+    convolve(context, low, own, up, gain, seg_rows, masks_seg, taps, act, matrix, resid, *scratch)
+    resid_out[...] = resid[pl.ds(EDGE, act.shape[0]), :]
+
+
+def expansion_spans(width):
+    step = cut(width, 512)
+    outs, values, gates = (
+        [pl.ds(part * width + at, step) for at in range(0, width, step)] for part in range(3)
+    )
+    return outs, values, gates, outs + [span for both in zip(values, gates) for span in both]
+
+
+def ask_for_expansion(offsets, weight, matrix, sems):
+    for index, span in enumerate(expansion_spans(matrix.shape[0])[3]):
+        load_columns(offsets, weight, matrix, span, sems.at[index])
+
+
+def convolve(
+    context, low, own, up, gain, seg_rows, masks_seg, taps, act, matrix, resid, conv_in, gated, moved, masks, sems
+):
     rows, width = act.shape
     queries = rows + 2 * EDGE
     step = cut(width, 512)
     count = width // step
-    outs = [pl.ds(at * step, step) for at in range(count)]
-    values = [pl.ds(width + at * step, step) for at in range(count)]
-    gates = [pl.ds(2 * width + at * step, step) for at in range(count)]
-    order = outs + [span for both in zip(values, gates) for span in both]
-    for index, span in enumerate(order):
-        load_columns(offsets, weight, matrix, span, sems.at[index])
+    outs, values, gates, _ = expansion_spans(width)
     half = KERNEL // 2
     for tap in range(KERNEL):
         same = masks_seg[:, tap : tap + 1] == seg_rows[...]
@@ -285,7 +309,6 @@
             jnp.float32
         )
     conv_in[...] = normalised(resid[...], gain[...])
-    resid_out[...] = resid[pl.ds(EDGE, rows), :]
     for index in range(count):
         await_columns(matrix, values[index], sems.at[count + 2 * index])
         await_columns(matrix, gates[index], sems.at[count + 2 * index + 1])
@@ -298,14 +321,17 @@
 
         def lines(group, carry):
             at = pl.multiple_of(group * GROUP, GROUP)
-            for lane in range(0, step, 128):
-                total = jnp.zeros((GROUP, 128), jnp.float32)
+            lanes = range(0, step, 128)
+            totals = [jnp.zeros((GROUP, 128), jnp.float32) for _ in lanes]
+            for tap in range(KERNEL):
+                first = EDGE - half + tap
+                mask = masks[tap, pl.ds(at, GROUP), :]
+                for number, lane in enumerate(lanes):
+                    place = index * step + lane
+                    part = moved[first % 8, pl.ds(at + first // 8 * 8, GROUP), lane : lane + 128]
+                    totals[number] += part * mask * taps[tap : tap + 1, place : place + 128]
+            for total, lane in zip(totals, lanes):
                 place = index * step + lane
-                for tap in range(KERNEL):
-                    first = EDGE - half + tap
-                    part = moved[first % 8, pl.ds(at + first // 8 * 8, GROUP), lane : lane + 128]
-                    part = part * masks[tap, pl.ds(at, GROUP), :]
-                    total = total + part * taps[tap : tap + 1, place : place + 128]
                 act[pl.ds(at, GROUP), place : place + 128] = (total * jax.nn.sigmoid(total)).astype(
                     jnp.bfloat16
                 )
@@ -387,6 +413,77 @@
     )(offsets, act, resid, *weight)
 
 
+def tick_kernel(counts, offsets, low, own, up, gain_a, gain_c, seg_queries, seg_keys, seg_rows, masks_seg, taps, *rest):
+    first, second, third = counts
+    qkv, rest = rest[:first], rest[first:]
+    expand, rest = rest[:second], rest[second:]
+    mix, rest = rest[:third], rest[third:]
+    out, context, matrix, normed, query, keys, values, bias, sems, act, expansion, resid, *scratch, mix_sems = rest
+    rows, width = out.shape
+    step = cut(width, 512)
+    spans = [pl.ds(at, step) for at in range(0, width, step)]
+
+    def ask_for_mix():
+        for index, span in enumerate(spans):
+            load_columns(offsets, mix, matrix, span, mix_sems.at[index])
+
+    attend(
+        offsets, qkv, low, own, up, gain_a, seg_queries, seg_keys,
+        context, matrix, normed, query, keys, values, bias, sems,
+        lambda: ask_for_expansion(offsets, expand, expansion, scratch[-1]), ask_for_mix,
+    )
+    convolve(context, low, own, up, gain_c, seg_rows, masks_seg, taps, act, expansion, resid, *scratch)
+    for index, span in enumerate(spans):
+        await_columns(matrix, span, mix_sems.at[index])
+        made = jnp.dot(act[...], matrix[:, span], preferred_element_type=jnp.float32)
+        out[:, span] = (resid[pl.ds(EDGE, rows), span] + made).astype(jnp.bfloat16)
+
+
+def whole_tick(offsets, qkv, expand, mix, low, own, up, gain_a, gain_c, seg_wide, taps):
+    rows, width = seg_wide.shape[0] // 3, own.shape[1]
+    wide, queries, step = 3 * rows, rows + 2 * EDGE, cut(width, 512)
+    whole = pl.BlockSpec(memory_space=pltpu.VMEM)
+    first = rows - KERNEL // 2
+    seg_taps = jnp.stack([seg_wide[first + tap : first + tap + rows] for tap in range(KERNEL)], axis=1)
+    pieces = (*qkv, *expand, *mix)
+    return pl.pallas_call(
+        functools.partial(tick_kernel, (len(qkv), len(expand), len(mix))),
+        out_shape=jax.ShapeDtypeStruct((rows, width), jnp.bfloat16),
+        in_specs=[pl.BlockSpec(memory_space=pltpu.SMEM)]
+        + [whole] * 10
+        + [pl.BlockSpec(memory_space=pl.ANY)] * len(pieces),
+        out_specs=whole,
+        scratch_shapes=[
+            pltpu.VMEM((queries, width), jnp.bfloat16),
+            pltpu.VMEM((width, 3 * width), jnp.bfloat16),
+            pltpu.VMEM((wide, width), jnp.bfloat16),
+            pltpu.VMEM((queries, width), jnp.bfloat16),
+            pltpu.VMEM((wide, width), jnp.bfloat16),
+            pltpu.VMEM((wide, width), jnp.bfloat16),
+            pltpu.VMEM((2, queries, 2 * rows + 128), jnp.float32),
+            pltpu.SemaphoreType.DMA((3 * width // cut(width, 768),)),
+            pltpu.VMEM((rows, width), jnp.bfloat16),
+            pltpu.VMEM((width, 3 * width), jnp.bfloat16),
+            pltpu.VMEM((queries, width), jnp.float32),
+            pltpu.VMEM((queries, width), jnp.bfloat16),
+            pltpu.VMEM((queries + 8, step), jnp.float32),
+            pltpu.VMEM((8, queries, step), jnp.float32),
+            pltpu.VMEM((KERNEL, rows, 128), jnp.float32),
+            pltpu.SemaphoreType.DMA((3 * width // step,)),
+            pltpu.SemaphoreType.DMA((width // step,)),
+        ],
+        compiler_params=pltpu.CompilerParams(vmem_limit_bytes=TICK_VMEM_BYTES),
+        cost_estimate=pl.CostEstimate(
+            flops=2 * width * width * (5 * queries + 2 * wide), bytes_accessed=14 * width * width, transcendentals=0
+        ),
+        name="tick",
+    )(
+        offsets, low, own, up, gain_a, gain_c,
+        seg_wide[rows - EDGE : 2 * rows + EDGE][:, None], seg_wide[None, :],
+        seg_wide[rows : 2 * rows][:, None], seg_taps, taps, *pieces,
+    )
+
+
 def on_device(
     layout,
     newcomer_groups,
@@ -439,18 +536,19 @@
     for tick in range(ticks):
         batch = sections - 1 - section + tick
         seg_wide = lax.dynamic_index_in_dim(ids, batch, 0, keepdims=False)
-        context = attention(offsets, qkv, low, present, up, gain_a, seg_wide)
-        if tick == 0:
+        if tick > 0:
+            made = whole_tick(offsets, qkv, out_expand, mix, low, present, up, gain_a, gain_c, seg_wide, taps)
+        else:
+            context = attention(offsets, qkv, low, present, up, gain_a, seg_wide)
             diagonal_2 = weights.to_diagonal(*behind(sides_2, context))
             sides_3 = weights.to_sides(behind(own_3, sides_2, context))
             out_expand = weights.whole(own_2, sides_2, diagonal_2)
             diagonal_3 = weights.to_diagonal(*behind(sides_3, diagonal_2))
             newcomers = behind(newcomer_groups, diagonal_2)
             newcomers = [send(newcomers[coming], layout.first()) for coming in range(ticks - 1)]
-        act, resid = convolution(offsets, out_expand, context, low, present, up, gain_c, seg_wide, taps)
-        if tick == 0:
+            act, resid = convolution(offsets, out_expand, context, low, present, up, gain_c, seg_wide, taps)
             mix = weights.whole(own_3, sides_3, diagonal_3, act)
-        made = mixing(offsets, mix, act, resid)
+            made = mixing(offsets, mix, act, resid)
         made_all.append(send(made, layout.to_homes()))
         if tick + 1 < ticks:
             arrived = send(made, layout.relay())

time: 423 us -> 412 us (0.974)
  Pallas kernels: 118 us -> 105 us
    pallas_call x0 -> x1, Pallas kernels: none -> 49.7 us  [whole_tick(): pl.pallas_call(functools.partial(tick_kernel, (len(qkv), len(expand), len...]
    pallas_call x2 -> x1, Pallas kernels: 60.3 us -> 26.9 us  [attention(): pl.pallas_call(functools.partial(attention_kernel, len(weight)), out_shap...]
    pallas_call x2 -> x1, Pallas kernels: 45.8 us -> 23 us  [convolution(): pl.pallas_call(functools.partial(convolution_kernel, len(weight)), out_sh...]
    pallas_call x2 -> x1, Pallas kernels: 11.6 us -> 5.77 us  [mixing(): pl.pallas_call(functools.partial(mixing_kernel, len(weight)), out_shape=j...]
  transfers between devices with their start and end apart: 28 -> 28, of which waited for: 15 -> 16; matrix products, arithmetic and copies ran while one was open for 4% -> 4% of each run, Pallas kernels for 28% -> 26%
where the time goes in v4:
time: 412 us; the launch traced here: 408 us
  waiting for transfers between devices  148 us (36%)
  starting transfers between devices  116 us (28%)
  Pallas kernels  105 us (25%)
  local copies, waits for them, and re-layouts  19.2 us (5%)
  other arithmetic  19 us (5%)
    ppermute x28, waiting for transfers between devices, send(): return lax.ppermute(value, AXES, moves)  148 us
    ppermute x28, starting transfers between devices, send(): return lax.ppermute(value, AXES, moves)  116 us
    pallas_call x1, Pallas kernels, whole_tick(): pl.pallas_call(functools.partial(tick_kernel, (len(qkv), len(expand), len...  49.7 us
    pallas_call x1, Pallas kernels, attention(): pl.pallas_call(functools.partial(attention_kernel, len(weight)), out_shap...  26.9 us
    pallas_call x1, Pallas kernels, convolution(): pl.pallas_call(functools.partial(convolution_kernel, len(weight)), out_sh...  23 us
    another operation x6, other arithmetic, whole(): near = jnp.stack([own, *sides, jnp.concatenate(diagonal, axis=1)])  10.7 us
  transfers between devices with their start and end apart: 28, of which 16 were waited for; matrix products, arithmetic and copies ran while one was open for 4% of the time, Pallas kernels for 26%

profile of v4, /device:TPU:6, one launch (start us, length us, event | category | flops | bytes accessed | tf_op | source)
XLA Modules:
  0.0 407.8 jit_solution(1174166909396405807)
XLA Ops:
  0.0 1.0 copy.88
  1.0 0.8 pad_maximum_fusion.4
  1.9 1.5 collective-permute-done
  3.4 1.4 broadcast_select_fusion.4
  4.8 0.8 collective-permute-start.1
  5.6 1.3 pad_maximum_fusion.3
  7.4 0.8 collective-permute-start.7
  8.2 1.6 collective-permute-start.4
  10.5 47.9 %collective-permute-start.2 = (bf16[272,1536]{1,0:T(8,128)(2,1)S(1)}, bf16[272,1536]{1,0:T(8,128)(2,1)S(1)}, u32[]{:S(2)}, u32[]{:S(2)}) collective-permute-start(bf16[272,1536]{1,0:T(8,128)(2,1)S(1)} %fusion.1), channel_id=1, source_target_pairs={{0,0},{1,8},{2,1},{3,9},{4,3},{5,11},{6,2},{7,10},{8,4},{9,12},{10... | collective-permute-start | bytes 2506760 | tf_op jit(solution)/shard_map/ppermute | solution.py:88
  58.6 0.7 collective-permute-start.8
  59.6 2.0 collective-permute-start.9
  61.6 15.8 %collective-permute-done.2.own = bf16[272,1536]{1,0:T(8,128)(2,1)S(1)} collective-permute-done((bf16[272,1536]{1,0:T(8,128)(2,1)S(1)}, bf16[272,1536]{1,0:T(8,128)(2,1)S(1)}, u32[]{:S(2)}, u32[]{:S(2)}) %collective-permute-start.2) | collective-permute-done | bytes 835616 | tf_op jit(solution)/shard_map/ppermute | solution.py:88
  77.4 27.8 %collective-permute-start.6 = (bf16[272,1536]{1,0:T(8,128)(2,1)S(1)}, bf16[272,1536]{1,0:T(8,128)(2,1)S(1)}, u32[]{:S(2)}, u32[]{:S(2)}) collective-permute-start(bf16[272,1536]{1,0:T(8,128)(2,1)S(1)} %collective-permute-done.2.own), channel_id=1, source_target_pairs={{8,0},{1,8},{9,1},{3,9},{11,3},{2,11},{10,2},{12,4},{5,12},{13,5},... | collective-permute-start | bytes 2506760 | tf_op jit(solution)/shard_map/ppermute | solution.py:88
  105.2 1.9 collective-permute-start.5
  107.1 0.9 broadcast_select_fusion.3
  108.0 12.8 %collective-permute-done.6.up = bf16[272,1536]{1,0:T(8,128)(2,1)S(1)} collective-permute-done((bf16[272,1536]{1,0:T(8,128)(2,1)S(1)}, bf16[272,1536]{1,0:T(8,128)(2,1)S(1)}, u32[]{:S(2)}, u32[]{:S(2)}) %collective-permute-start.6) | collective-permute-done | bytes 835616 | tf_op jit(solution)/shard_map/ppermute | solution.py:88
  120.8 2.1 collective-permute-done.5.low
  122.9 0.9 copy-done.6
  123.9 3.7 pad_maximum_fusion.rest_0_
  127.6 9.5 %collective-permute-start.11 = (bf16[4,192,4608]{2,1,0:T(8,128)(2,1)}, bf16[4,192,4608]{2,1,0:T(8,128)(2,1)}, u32[]{:S(2)}, u32[]{:S(2)}) collective-permute-start(bf16[4,192,4608]{2,1,0:T(8,128)(2,1)} %pad_maximum_fusion.rest_0_), channel_id=1, source_target_pairs={{0,8},{1,9},{2,10},{3,11},{4,12},{5,13},{6,14},{7,15},{8,0},{9,1},... | collective-permute-start | bytes 21233672 | tf_op jit(solution)/shard_map/ppermute | solution.py:88
  137.2 1.2 collective-permute-start.13
  138.3 1.6 collective-permute-start.12
  140.5 1.5 fusion.2
  144.7 0.8 copy.79.seg_rows
  145.5 1.4 constant_dynamic-slice_fusion
  146.9 1.5 collective-permute-done.11.rest_1_
  148.4 26.9 %attention.1.context = bf16[288,1536]{1,0:T(8,128)(2,1)} custom-call(s32[8]{0:T(128)} %add_multiply_fusion.offsets, bf16[272,1536]{1,0:T(8,128)(2,1)} %copy-done.6, bf16[272,1536]{1,0:T(8,128)(2,1)} %copy-done.4, bf16[272,1536]{1,0:T(8,128)(2,1)} %copy-done.5, f32[1,1536]{1,0:T(1,128)} %get-tuple-element.78.gain.gain_a, s32[288,1]{1,0:T(8,128)} %copy.79.seg_rows, ...), custom_call_target="tpu_custom_call" | custom-call | flops 9965666304 | bytes 17301504 | tf_op jit(solution)/shard_map/attention/pallas_call | solution.py:243
  175.3 2.4 collective-permute-done.13
  177.8 1.4 collective-permute-done.12
  179.1 1.3 slice_select_fusion.1
  180.5 1.6 collective-permute-start.15
  182.5 19.2 %collective-permute-done.15 = bf16[192,2304]{1,0:T(8,128)(2,1)S(1)} collective-permute-done((bf16[192,2304]{1,0:T(8,128)(2,1)S(1)}, bf16[192,2304]{1,0:T(8,128)(2,1)S(1)}, u32[]{:S(2)}, u32[]{:S(2)}) %collective-permute-start.15) | collective-permute-done | bytes 884768 | tf_op jit(solution)/shard_map/ppermute | solution.py:88
  201.7 9.5 %collective-permute-done.14 = bf16[192,2304]{1,0:T(8,128)(2,1)S(1)} collective-permute-done((bf16[192,2304]{1,0:T(8,128)(2,1)S(1)}, bf16[192,2304]{1,0:T(8,128)(2,1)S(1)}, u32[]{:S(2)}, u32[]{:S(2)}) %collective-permute-start.14) | collective-permute-done | bytes 884768 | tf_op jit(solution)/shard_map/ppermute | solution.py:88
  211.3 5.3 %pad_maximum_fusion.1.rest_0_.rest_2_ = bf16[4,192,4608]{2,1,0:T(8,128)(2,1)} fusion(bf16[1,192,4608]{2,1,0:T(8,128)(2,1)S(1)} %maximum_bitcast_fusion.1, bf16[1,192,4608]{2,1,0:T(8,128)(2,1)S(1)} %bitcast.159, bf16[1,192,4608]{2,1,0:T(8,128)(2,1)} %bitcast.42, bf16[1,192,4608]{2,1,0:T(8,128)(2,1)S(1)} %bitcast.158), kind=kLoop, calls=%fused_computation.1 | loop fusion | flops 10616832 | bytes 14155776 | tf_op jit(solution)/shard_map/stack | solution.py:132
  216.7 1.4 collective-permute-start.18
  218.1 1.6 collective-permute-start.17
  219.7 1.6 slice.387.taps
  221.3 1.9 dynamic-slice_bitcast_fusion.19
  223.2 0.8 copy.80.seg_rows
  224.0 1.4 dynamic-slice_bitcast_fusion.35
  225.5 0.8 copy.81.masks_seg
  226.2 6.4 %collective-permute-done.18 = bf16[192,1536]{1,0:T(8,128)(2,1)S(1)} collective-permute-done((bf16[192,1536]{1,0:T(8,128)(2,1)}, bf16[192,1536]{1,0:T(8,128)(2,1)S(1)}, u32[]{:S(2)}, u32[]{:S(2)}) %collective-permute-start.18) | collective-permute-done | bytes 589856 | tf_op jit(solution)/shard_map/ppermute | solution.py:88
  232.6 1.1 collective-permute-done.17
  233.8 1.6 collective-permute-start.20
  235.9 23.0 %convolution.1 = (bf16[256,1536]{1,0:T(8,128)(2,1)}, f32[256,1536]{1,0:T(8,128)}) custom-call(s32[8]{0:T(128)} %add_multiply_fusion.offsets, bf16[288,1536]{1,0:T(8,128)(2,1)} %attention.1.context, bf16[272,1536]{1,0:T(8,128)(2,1)} %copy-done.6, bf16[272,1536]{1,0:T(8,128)(2,1)} %copy-done.4, bf16[272,1536]{1,0:T(8,128)(2,1)} %copy-done.5, ...), custom_call_target="tpu_custom_call" | custom-call | flops 4113432576 | bytes 17301504 | tf_op jit(solution)/shard_map/convolution/pallas_call | solution.py:350
  259.0 1.4 pad_maximum_fusion.2.rest_0_.rest_4_
  260.5 0.7 collective-permute-start.23
  261.2 3.8 collective-permute-done.21.rest_1_.rest_5_
  265.0 1.4 copy-done.1
  266.4 5.8 %mixing.1 = bf16[256,1536]{1,0:T(8,128)(2,1)} custom-call(s32[8]{0:T(128)} %add_multiply_fusion.offsets, bf16[256,1536]{1,0:T(8,128)(2,1)} %get-tuple-element.58.act, f32[256,1536]{1,0:T(8,128)} %get-tuple-element.59.resid, bf16[4,192,1536]{2,1,0:T(8,128)(2,1)} %copy-done, bf16[4,192,1536]{2,1,0:T(8,128)(2,1)} %copy-done.1), custom_call_target="tpu_custom_call" | custom-call | flops 1207959552 | bytes 7864320 | tf_op jit(solution)/shard_map/mixing/pallas_call | solution.py:397
  272.2 2.7 collective-permute-start.24
  274.9 41.9 %collective-permute-done.24 = bf16[256,1536]{1,0:T(8,128)(2,1)S(1)} collective-permute-done((bf16[256,1536]{1,0:T(8,128)(2,1)}, bf16[256,1536]{1,0:T(8,128)(2,1)S(1)}, u32[]{:S(2)}, u32[]{:S(2)}) %collective-permute-start.24) | collective-permute-done | bytes 786464 | tf_op jit(solution)/shard_map/ppermute | solution.py:88
  316.8 1.9 collective-permute-start.26
  318.8 2.4 collective-permute-start.25
  321.2 0.8 copy.83.seg_rows
  322.3 0.8 copy.84.masks_seg
  323.0 0.8 copy.82.seg_queries
  323.8 2.3 collective-permute-start.22
  326.1 2.1 collective-permute-done.26.up
  328.3 6.6 %collective-permute-done.25.low = bf16[256,1536]{1,0:T(8,128)(2,1)} collective-permute-done((bf16[256,1536]{1,0:T(8,128)(2,1)S(1)}, bf16[256,1536]{1,0:T(8,128)(2,1)}, u32[]{:S(2)}, u32[]{:S(2)}) %collective-permute-start.25) | collective-permute-done | bytes 786464 | tf_op jit(solution)/shard_map/ppermute | solution.py:88
  334.9 49.7 %tick.1 = bf16[256,1536]{1,0:T(8,128)(2,1)} custom-call(s32[8]{0:T(128)} %add_multiply_fusion.offsets, bf16[256,1536]{1,0:T(8,128)(2,1)} %collective-permute-done.25.low, bf16[256,1536]{1,0:T(8,128)(2,1)} %copy-done.7, bf16[256,1536]{1,0:T(8,128)(2,1)} %copy-done.14, f32[1,1536]{1,0:T(1,128)} %get-tuple-element.78.gain.gain_a, ...), custom_call_target="tpu_custom_call" | custom-call | flops 14042529792 | bytes 33030144 | tf_op jit(solution)/shard_map/tick/pallas_call | solution.py:449
  384.6 1.9 collective-permute-start.27
  386.5 19.8 %collective-permute-done.27 = bf16[256,1536]{1,0:T(8,128)(2,1)S(1)} collective-permute-done((bf16[256,1536]{1,0:T(8,128)(2,1)}, bf16[256,1536]{1,0:T(8,128)(2,1)S(1)}, u32[]{:S(2)}, u32[]{:S(2)}) %collective-permute-start.27) | collective-permute-done | bytes 786464 | tf_op jit(solution)/shard_map/ppermute | solution.py:88
  406.3 1.3 maximum_bitcast_fusion.2
  (67 shorter events, 6.8 us)
Async XLA Ops:
  0.0 5.6 %copy-start.3 = (bf16[1,192,3072]{2,1,0:T(8,128)(2,1)S(1)}, bf16[1,192,3072]{2,1,0:T(8,128)(2,1)}, u32[]{:S(2)}) copy-start(bf16[1,192,3072]{2,1,0:T(8,128)(2,1)} %param.17) | copy-start | bytes 3538948
  1.8 1.6 collective-permute-start
  4.8 2.1 collective-permute-start.1
  5.6 1.7 copy-start.2
  6.9 3.5 copy-start.13
  6.9 3.5 copy-start.8
  7.4 50.9 %collective-permute-start.7 = (bf16[192,4608]{1,0:T(8,128)(2,1)S(1)}, bf16[192,4608]{1,0:T(8,128)(2,1)S(1)}, u32[]{:S(2)}, u32[]{:S(2)}) collective-permute-start(bf16[192,4608]{1,0:T(8,128)(2,1)S(1)} %pad_maximum_fusion.3), channel_id=1, source_target_pairs={{4,8},{5,9},{6,10},{7,11},{8,4},{9,5},{10,6},{11,7},{20,24},{21,25... | collective-permute-start | bytes 5308424 | tf_op jit(solution)/shard_map/ppermute | solution.py:88
  8.2 51.1 %collective-permute-start.4 = (bf16[192,4608]{1,0:T(8,128)(2,1)S(1)}, bf16[192,4608]{1,0:T(8,128)(2,1)S(1)}, u32[]{:S(2)}, u32[]{:S(2)}) collective-permute-start(bf16[192,4608]{1,0:T(8,128)(2,1)S(1)} %broadcast_select_fusion.1), channel_id=1, source_target_pairs={{0,2},{1,3},{2,0},{3,1},{4,6},{5,7},{6,4},{7,5},{8,10},{9,11},{10,... | collective-permute-start | bytes 5308424 | tf_op jit(solution)/shard_map/ppermute | solution.py:88
  9.9 49.4 %collective-permute-start.3 = (bf16[192,4608]{1,0:T(8,128)(2,1)S(1)}, bf16[192,4608]{1,0:T(8,128)(2,1)S(1)}, u32[]{:S(2)}, u32[]{:S(2)}) collective-permute-start(bf16[192,4608]{1,0:T(8,128)(2,1)S(1)} %broadcast_select_fusion.1), channel_id=1, source_target_pairs={{0,1},{1,0},{2,3},{3,2},{4,5},{5,4},{6,7},{7,6},{8,9},{9,8},{10,11... | collective-permute-start | bytes 5308424 | tf_op jit(solution)/shard_map/ppermute | solution.py:88
  10.5 48.1 %copy-start.10 = (bf16[1,192,1536]{2,1,0:T(8,128)(2,1)S(1)}, bf16[1,192,1536]{2,1,0:T(8,128)(2,1)}, u32[]{:S(2)}) copy-start(bf16[1,192,1536]{2,1,0:T(8,128)(2,1)} %param.19) | copy-start | bytes 1769476
  10.5 66.9 %collective-permute-start.2 = (bf16[272,1536]{1,0:T(8,128)(2,1)S(1)}, bf16[272,1536]{1,0:T(8,128)(2,1)S(1)}, u32[]{:S(2)}, u32[]{:S(2)}) collective-permute-start(bf16[272,1536]{1,0:T(8,128)(2,1)S(1)} %fusion.1), channel_id=1, source_target_pairs={{0,0},{1,8},{2,1},{3,9},{4,3},{5,11},{6,2},{7,10},{8,4},{9,12},{10... | collective-permute-start | bytes 2506760 | tf_op jit(solution)/shard_map/ppermute | solution.py:88
  58.6 48.5 %collective-permute-start.8 = (bf16[192,1536]{1,0:T(8,128)(2,1)S(1)}, bf16[192,1536]{1,0:T(8,128)(2,1)S(1)}, u32[]{:S(2)}, u32[]{:S(2)}) collective-permute-start(bf16[192,1536]{1,0:T(8,128)(2,1)S(1)} %bitcast.174), channel_id=1, source_target_pairs={{4,8},{5,9},{6,10},{7,11},{8,4},{9,5},{10,6},{11,7},{20,24},{21,25... | collective-permute-start | bytes 1769480 | tf_op jit(solution)/shard_map/ppermute | solution.py:88
  59.5 63.5 %collective-permute-start.10 = (bf16[192,2304]{1,0:T(8,128)(2,1)S(1)}, bf16[192,2304]{1,0:T(8,128)(2,1)S(1)}, u32[]{:S(2)}, u32[]{:S(2)}) collective-permute-start(bf16[192,2304]{1,0:T(8,128)(2,1)S(1)} %get-tuple-element.73), channel_id=1, source_target_pairs={{0,1},{1,0},{2,3},{3,2},{4,6},{5,7},{6,4},{7,5},{8,10},{9,11},{10,... | collective-permute-start | bytes 2654216 | tf_op jit(solution)/shard_map/ppermute | solution.py:88
  59.6 64.3 %collective-permute-start.9 = (bf16[192,2304]{1,0:T(8,128)(2,1)S(1)}, bf16[192,2304]{1,0:T(8,128)(2,1)S(1)}, u32[]{:S(2)}, u32[]{:S(2)}) collective-permute-start(bf16[192,2304]{1,0:T(8,128)(2,1)S(1)} %get-tuple-element.74), channel_id=1, source_target_pairs={{0,1},{1,0},{2,3},{3,2},{4,5},{5,4},{6,7},{7,6},{8,9},{9,8},{10,11... | collective-permute-start | bytes 2654216 | tf_op jit(solution)/shard_map/ppermute | solution.py:88
  77.4 46.5 %copy-start.4 = (bf16[272,1536]{1,0:T(8,128)(2,1)}, bf16[272,1536]{1,0:T(8,128)(2,1)S(1)}, u32[]{:S(2)}) copy-start(bf16[272,1536]{1,0:T(8,128)(2,1)S(1)} %collective-permute-done.2.own) | copy-start | bytes 2506756
  77.4 43.4 %collective-permute-start.6 = (bf16[272,1536]{1,0:T(8,128)(2,1)S(1)}, bf16[272,1536]{1,0:T(8,128)(2,1)S(1)}, u32[]{:S(2)}, u32[]{:S(2)}) collective-permute-start(bf16[272,1536]{1,0:T(8,128)(2,1)S(1)} %collective-permute-done.2.own), channel_id=1, source_target_pairs={{8,0},{1,8},{9,1},{3,9},{11,3},{2,11},{10,2},{12,4},{5,12},{13,5},... | collective-permute-start | bytes 2506760 | tf_op jit(solution)/shard_map/ppermute | solution.py:88
  105.2 17.8 %collective-permute-start.5 = (bf16[272,1536]{1,0:T(8,128)(2,1)S(1)}, bf16[272,1536]{1,0:T(8,128)(2,1)S(1)}, u32[]{:S(2)}, u32[]{:S(2)}) collective-permute-start(bf16[272,1536]{1,0:T(8,128)(2,1)S(1)} %collective-permute-done.2.own), channel_id=1, source_target_pairs={{0,8},{8,1},{1,9},{9,3},{3,11},{11,2},{2,10},{4,12},{12,5},{5,13},... | collective-permute-start | bytes 2506760 | tf_op jit(solution)/shard_map/ppermute | solution.py:88
  120.8 2.1 copy-start.5
  122.9 0.9 copy-start.6
  127.6 20.8 %collective-permute-start.11 = (bf16[4,192,4608]{2,1,0:T(8,128)(2,1)}, bf16[4,192,4608]{2,1,0:T(8,128)(2,1)}, u32[]{:S(2)}, u32[]{:S(2)}) collective-permute-start(bf16[4,192,4608]{2,1,0:T(8,128)(2,1)} %pad_maximum_fusion.rest_0_), channel_id=1, source_target_pairs={{0,8},{1,9},{2,10},{3,11},{4,12},{5,13},{6,14},{7,15},{8,0},{9,1},... | collective-permute-start | bytes 21233672 | tf_op jit(solution)/shard_map/ppermute | solution.py:88
  137.2 40.6 %collective-permute-start.13 = (bf16[192,4608]{1,0:T(8,128)(2,1)S(1)}, bf16[192,4608]{1,0:T(8,128)(2,1)S(1)}, u32[]{:S(2)}, u32[]{:S(2)}) collective-permute-start(bf16[192,4608]{1,0:T(8,128)(2,1)S(1)} %broadcast_select_fusion), channel_id=1, source_target_pairs={{0,2},{1,3},{2,0},{3,1},{4,6},{5,7},{6,4},{7,5},{8,10},{9,11},{10,... | collective-permute-start | bytes 5308424 | tf_op jit(solution)/shard_map/ppermute | solution.py:88
  138.3 40.8 %collective-permute-start.12 = (bf16[192,4608]{1,0:T(8,128)(2,1)S(1)}, bf16[192,4608]{1,0:T(8,128)(2,1)}, u32[]{:S(2)}, u32[]{:S(2)}) collective-permute-start(bf16[192,4608]{1,0:T(8,128)(2,1)S(1)} %broadcast_select_fusion), channel_id=1, source_target_pairs={{0,1},{1,0},{2,3},{3,2},{4,5},{5,4},{6,7},{7,6},{8,9},{9,8},{10,11... | collective-permute-start | bytes 5308424 | tf_op jit(solution)/shard_map/ppermute | solution.py:88
  144.0 0.6 copy-start.11
  180.5 21.3 %collective-permute-start.15 = (bf16[192,2304]{1,0:T(8,128)(2,1)S(1)}, bf16[192,2304]{1,0:T(8,128)(2,1)S(1)}, u32[]{:S(2)}, u32[]{:S(2)}) collective-permute-start(bf16[192,2304]{1,0:T(8,128)(2,1)S(1)} %get-tuple-element.71), channel_id=1, source_target_pairs={{0,1},{1,0},{2,3},{3,2},{4,6},{5,7},{6,4},{7,5},{8,10},{9,11},{10,... | collective-permute-start | bytes 2654216 | tf_op jit(solution)/shard_map/ppermute | solution.py:88
  182.1 29.1 %collective-permute-start.14 = (bf16[192,2304]{1,0:T(8,128)(2,1)S(1)}, bf16[192,2304]{1,0:T(8,128)(2,1)S(1)}, u32[]{:S(2)}, u32[]{:S(2)}) collective-permute-start(bf16[192,2304]{1,0:T(8,128)(2,1)S(1)} %get-tuple-element.72), channel_id=1, source_target_pairs={{0,1},{1,0},{2,3},{3,2},{4,5},{5,4},{6,7},{7,6},{8,9},{9,8},{10,11... | collective-permute-start | bytes 2654216 | tf_op jit(solution)/shard_map/ppermute | solution.py:88
  216.7 19.2 %collective-permute-start.16 = (bf16[4,192,4608]{2,1,0:T(8,128)(2,1)}, bf16[4,192,4608]{2,1,0:T(8,128)(2,1)}, u32[]{:S(2)}, u32[]{:S(2)}) collective-permute-start(bf16[4,192,4608]{2,1,0:T(8,128)(2,1)} %pad_maximum_fusion.1.rest_0_.rest_2_), channel_id=1, source_target_pairs={{0,8},{1,9},{2,10},{3,11},{4,12},{5,13},{6,14},{7,15},{8,0},{9,1},... | collective-permute-start | bytes 21233672 | tf_op jit(solution)/shard_map/ppermute | solution.py:88
  216.7 16.0 %collective-permute-start.18 = (bf16[192,1536]{1,0:T(8,128)(2,1)}, bf16[192,1536]{1,0:T(8,128)(2,1)S(1)}, u32[]{:S(2)}, u32[]{:S(2)}) collective-permute-start(bf16[192,1536]{1,0:T(8,128)(2,1)} %broadcast_select_fusion.3), channel_id=1, source_target_pairs={{0,2},{1,3},{2,0},{3,1},{4,6},{5,7},{6,4},{7,5},{8,10},{9,11},{10,... | collective-permute-start | bytes 1769480 | tf_op jit(solution)/shard_map/ppermute | solution.py:88
  218.1 15.7 %collective-permute-start.17 = (bf16[192,1536]{1,0:T(8,128)(2,1)}, bf16[192,1536]{1,0:T(8,128)(2,1)S(1)}, u32[]{:S(2)}, u32[]{:S(2)}) collective-permute-start(bf16[192,1536]{1,0:T(8,128)(2,1)} %broadcast_select_fusion.3), channel_id=1, source_target_pairs={{0,1},{1,0},{2,3},{3,2},{4,5},{5,4},{6,7},{7,6},{8,9},{9,8},{10,11... | collective-permute-start | bytes 1769480 | tf_op jit(solution)/shard_map/ppermute | solution.py:88
  233.8 25.1 %collective-permute-start.20 = (bf16[192,768]{1,0:T(8,128)(2,1)S(1)}, bf16[192,768]{1,0:T(8,128)(2,1)S(1)}, u32[]{:S(2)}, u32[]{:S(2)}) collective-permute-start(bf16[192,768]{1,0:T(8,128)(2,1)S(1)} %get-tuple-element.75), channel_id=1, source_target_pairs={{0,1},{1,0},{2,3},{3,2},{4,6},{5,7},{6,4},{7,5},{8,10},{9,11},{10,... | collective-permute-start | bytes 884744 | tf_op jit(solution)/shard_map/ppermute | solution.py:88
  235.5 23.5 %collective-permute-start.19 = (bf16[192,768]{1,0:T(8,128)(2,1)S(1)}, bf16[192,768]{1,0:T(8,128)(2,1)S(1)}, u32[]{:S(2)}, u32[]{:S(2)}) collective-permute-start(bf16[192,768]{1,0:T(8,128)(2,1)S(1)} %get-tuple-element.76), channel_id=1, source_target_pairs={{0,1},{1,0},{2,3},{3,2},{4,5},{5,4},{6,7},{7,6},{8,9},{9,8},{10,11... | collective-permute-start | bytes 884744 | tf_op jit(solution)/shard_map/ppermute | solution.py:88
  260.4 4.6 %copy-start = (bf16[4,192,1536]{2,1,0:T(8,128)(2,1)}, bf16[4,192,1536]{2,1,0:T(8,128)(2,1)S(1)}, u32[]{:S(2)}) copy-start(bf16[4,192,1536]{2,1,0:T(8,128)(2,1)S(1)} %pad_maximum_fusion.2.rest_0_.rest_4_) | copy-start | bytes 7077892
  260.4 4.6 %collective-permute-start.21 = (bf16[4,192,1536]{2,1,0:T(8,128)(2,1)S(1)}, bf16[4,192,1536]{2,1,0:T(8,128)(2,1)S(1)}, u32[]{:S(2)}, u32[]{:S(2)}) collective-permute-start(bf16[4,192,1536]{2,1,0:T(8,128)(2,1)S(1)} %pad_maximum_fusion.2.rest_0_.rest_4_), channel_id=1, source_target_pairs={{0,8},{1,9},{2,10},{3,11},{4,12},{5,13},{6,14},{7,15},{8,0},{9,1},... | collective-permute-start | bytes 7077896 | tf_op jit(solution)/shard_map/ppermute | solution.py:88
  260.5 14.4 %collective-permute-start.23 = (bf16[256,1536]{1,0:T(8,128)(2,1)}, bf16[256,1536]{1,0:T(8,128)(2,1)S(1)}, u32[]{:S(2)}, u32[]{:S(2)}) collective-permute-start(bf16[256,1536]{1,0:T(8,128)(2,1)} %bitcast.50), channel_id=1, source_target_pairs={{0,0},{1,8},{2,1},{3,9},{4,3},{5,11},{6,2},{7,10}} | collective-permute-start | bytes 2359304 | tf_op jit(solution)/shard_map/ppermute | solution.py:88
  265.0 1.4 copy-start.1
  272.1 49.8 %copy-start.12 = (s32[5,768]{1,0:T(8,128)S(1)}, s32[5,768]{1,0:T(8,128)}, u32[]{:S(2)}) copy-start(s32[5,768]{1,0:T(8,128)} %copy-done.11) | copy-start | bytes 46084
  272.2 51.7 %copy-start.9 = (bf16[256,1536]{1,0:T(8,128)(2,1)S(1)}, bf16[256,1536]{1,0:T(8,128)(2,1)}, u32[]{:S(2)}) copy-start(bf16[256,1536]{1,0:T(8,128)(2,1)} %mixing.1) | copy-start | bytes 2359300
  272.2 44.6 %collective-permute-start.24 = (bf16[256,1536]{1,0:T(8,128)(2,1)}, bf16[256,1536]{1,0:T(8,128)(2,1)S(1)}, u32[]{:S(2)}, u32[]{:S(2)}) collective-permute-start(bf16[256,1536]{1,0:T(8,128)(2,1)} %mixing.1), channel_id=1, source_target_pairs={{0,4},{8,12},{1,5},{9,13},{3,7},{11,15},{2,6},{10,14},{4,16},{12,2... | collective-permute-start | bytes 2359304 | tf_op jit(solution)/shard_map/ppermute | solution.py:88
  316.8 18.0 %copy-start.7 = (bf16[256,1536]{1,0:T(8,128)(2,1)}, bf16[256,1536]{1,0:T(8,128)(2,1)S(1)}, u32[]{:S(2)}) copy-start(bf16[256,1536]{1,0:T(8,128)(2,1)S(1)} %broadcast_select_fusion.2.own) | copy-start | bytes 2359300
  316.8 11.4 %collective-permute-start.26 = (bf16[256,1536]{1,0:T(8,128)(2,1)S(1)}, bf16[256,1536]{1,0:T(8,128)(2,1)S(1)}, u32[]{:S(2)}, u32[]{:S(2)}) collective-permute-start(bf16[256,1536]{1,0:T(8,128)(2,1)S(1)} %broadcast_select_fusion.2.own), channel_id=1, source_target_pairs={{8,0},{1,8},{9,1},{3,9},{11,3},{2,11},{10,2},{12,4},{5,12},{13,5},... | collective-permute-start | bytes 2359304 | tf_op jit(solution)/shard_map/ppermute | solution.py:88
  318.8 16.1 %collective-permute-start.25 = (bf16[256,1536]{1,0:T(8,128)(2,1)S(1)}, bf16[256,1536]{1,0:T(8,128)(2,1)}, u32[]{:S(2)}, u32[]{:S(2)}) collective-permute-start(bf16[256,1536]{1,0:T(8,128)(2,1)S(1)} %broadcast_select_fusion.2.own), channel_id=1, source_target_pairs={{0,8},{8,1},{1,9},{9,3},{3,11},{11,2},{2,10},{4,12},{12,5},{5,13},... | collective-permute-start | bytes 2359304 | tf_op jit(solution)/shard_map/ppermute | solution.py:88
  323.8 62.7 %collective-permute-start.22 = (bf16[256,1536]{1,0:T(8,128)(2,1)S(1)}, bf16[256,1536]{1,0:T(8,128)(2,1)S(1)}, u32[]{:S(2)}, u32[]{:S(2)}) collective-permute-start(bf16[256,1536]{1,0:T(8,128)(2,1)S(1)} %copy-done.9), channel_id=1, source_target_pairs={{0,0},{8,1},{1,2},{9,3},{3,4},{11,5},{2,6},{10,7},{4,8},{12,9},{5,... | collective-permute-start | bytes 2359304 | tf_op jit(solution)/shard_map/ppermute | solution.py:88
  328.3 6.6 %copy-start.14 = (bf16[256,1536]{1,0:T(8,128)(2,1)}, bf16[256,1536]{1,0:T(8,128)(2,1)S(1)}, u32[]{:S(2)}) copy-start(bf16[256,1536]{1,0:T(8,128)(2,1)S(1)} %collective-permute-done.26.up) | copy-start | bytes 2359300
  384.6 21.8 %collective-permute-start.27 = (bf16[256,1536]{1,0:T(8,128)(2,1)}, bf16[256,1536]{1,0:T(8,128)(2,1)S(1)}, u32[]{:S(2)}, u32[]{:S(2)}) collective-permute-start(bf16[256,1536]{1,0:T(8,128)(2,1)} %tick.1), channel_id=1, source_target_pairs={{0,0},{8,1},{1,2},{9,3},{3,4},{11,5},{2,6},{10,7},{4,8},{12,9},{5,... | collective-permute-start | bytes 2359304 | tf_op jit(solution)/shard_map/ppermute | solution.py:88

commit v5 on v4

--- a/solution.py
+++ b/solution.py
@@ -108,11 +108,13 @@
             return own, own
         return send(own, self.layout.flipped(0, 1)), send(own, self.layout.flipped(0, 2))
 
-    def to_diagonal(self, along_x, along_z):
+    def to_diagonal(self, along_x, along_z, even):
         if not self.tree:
             return along_x, along_z
         half = along_x.shape[1] // 2
         low = send(along_z[:, :half], self.layout.flipped(0, 1))
+        if even:
+            return low, send(along_x[:, half:], self.layout.flipped(0, 2))
         high = jnp.where(self.at_home, along_z[:, half:], along_x[:, half:])
         return low, send(high, self.layout.diagonal())
 
@@ -131,6 +133,15 @@
         own, sides, diagonal = behind((own, sides, diagonal), *earlier)
         near = jnp.stack([own, *sides, jnp.concatenate(diagonal, axis=1)])
         return near, send(near, self.layout.flipped(1, 0))
+
+    def whole_by_parts(self, own, sides, diagonal, *earlier):
+        if not self.tree:
+            return self.whole(own, sides, diagonal)
+        own, sides = behind((own, sides), *earlier)
+        near = jnp.stack([own, *sides])
+        far = send(near, self.layout.flipped(1, 0))
+        last = jnp.concatenate(diagonal, axis=1)[None]
+        return near, last, far, send(last, self.layout.flipped(1, 0))
 
 
 def cut(total, most):
@@ -524,7 +535,7 @@
     sides_2 = weights.to_sides(behind(own_2, sides_1))
     packed_out = behind(packed, sides_1)
     packed = (send(packed_out, layout.shifted(1)), packed, send(packed_out, layout.shifted(-1)))
-    diagonal_1 = weights.to_diagonal(*sides_1)
+    diagonal_1 = weights.to_diagonal(*sides_1, False)
     qkv = weights.whole(own_1, sides_1, diagonal_1, packed, own_3)
     packed = behind(packed, own_3)
 
@@ -540,10 +551,10 @@
             made = whole_tick(offsets, qkv, out_expand, mix, low, present, up, gain_a, gain_c, seg_wide, taps)
         else:
             context = attention(offsets, qkv, low, present, up, gain_a, seg_wide)
-            diagonal_2 = weights.to_diagonal(*behind(sides_2, context))
+            diagonal_2 = weights.to_diagonal(*behind(sides_2, context), True)
             sides_3 = weights.to_sides(behind(own_3, sides_2, context))
-            out_expand = weights.whole(own_2, sides_2, diagonal_2)
-            diagonal_3 = weights.to_diagonal(*behind(sides_3, diagonal_2))
+            out_expand = weights.whole_by_parts(own_2, sides_2, diagonal_2, context)
+            diagonal_3 = weights.to_diagonal(*behind(sides_3, diagonal_2), True)
             newcomers = behind(newcomer_groups, diagonal_2)
             newcomers = [send(newcomers[coming], layout.first()) for coming in range(ticks - 1)]
             act, resid = convolution(offsets, out_expand, context, low, present, up, gain_c, seg_wide, taps)

time: 412 us -> 402 us (0.976)
  waiting for transfers between devices: 148 us -> 131 us
  local copies, waits for them, and re-layouts: 19.2 us -> 28 us
    ppermute x28 -> x29, waiting for transfers between devices: 148 us -> 131 us  [send(): return lax.ppermute(value, AXES, moves)]
    another operation x6 -> x4, other arithmetic: 10.7 us -> 4 us  [whole(): near = jnp.stack([own, *sides, jnp.concatenate(diagonal, axis=1)])]
    another operation x3, local copies, waits for them, and re-layouts: 2.21 us -> 8.73 us  [convolution(): jnp.stack([seg_wide[first + tap:first + tap + rows] for tap in range(KERN...]
    another operation x0 -> x1, other arithmetic: none -> 4.38 us  [whole_by_parts(): near = jnp.stack([own, *sides])]
    ppermute x28 -> x29, starting transfers between devices: 116 us -> 117 us  [send(): return lax.ppermute(value, AXES, moves)]
  transfers between devices with their start and end apart: 28 -> 29, of which waited for: 16 -> 15; matrix products, arithmetic and copies ran while one was open for 4% -> 7% of each run, Pallas kernels for 26% -> 26%
where the time goes in v5:
time: 402 us; the launch traced here: 398 us
  waiting for transfers between devices  131 us (33%)
  starting transfers between devices  117 us (29%)
  Pallas kernels  105 us (26%)
  local copies, waits for them, and re-layouts  28 us (7%)
  other arithmetic  15.5 us (4%)
    ppermute x29, waiting for transfers between devices, send(): return lax.ppermute(value, AXES, moves)  131 us
    ppermute x29, starting transfers between devices, send(): return lax.ppermute(value, AXES, moves)  117 us
    pallas_call x1, Pallas kernels, whole_tick(): pl.pallas_call(functools.partial(tick_kernel, (len(qkv), len(expand), len...  49.7 us
    pallas_call x1, Pallas kernels, attention(): pl.pallas_call(functools.partial(attention_kernel, len(weight)), out_shap...  26.9 us
    pallas_call x1, Pallas kernels, convolution(): pl.pallas_call(functools.partial(convolution_kernel, len(weight)), out_sh...  23 us
    another operation x3, local copies, waits for them, and re-layouts, convolution(): jnp.stack([seg_wide[first + tap:first + tap + rows] for tap in range(KERN...  8.73 us
  transfers between devices with their start and end apart: 29, of which 15 were waited for; matrix products, arithmetic and copies ran while one was open for 7% of the time, Pallas kernels for 26%

profile of v5, /device:TPU:6, one launch (start us, length us, event | category | flops | bytes accessed | tf_op | source)
XLA Modules:
  0.0 397.9 jit_solution(17925725436953850248)
XLA Ops:
  0.0 1.0 copy.88
  1.0 0.8 pad_maximum_fusion.4
  1.9 1.5 collective-permute-done
  3.4 1.5 broadcast_select_fusion.4
  4.8 0.8 collective-permute-start.1
  5.6 1.3 pad_maximum_fusion.3
  7.4 0.8 collective-permute-start.7
  8.2 1.6 collective-permute-start.4
  10.5 47.9 %collective-permute-start.2 = (bf16[272,1536]{1,0:T(8,128)(2,1)S(1)}, bf16[272,1536]{1,0:T(8,128)(2,1)S(1)}, u32[]{:S(2)}, u32[]{:S(2)}) collective-permute-start(bf16[272,1536]{1,0:T(8,128)(2,1)S(1)} %fusion.1), channel_id=1, source_target_pairs={{0,0},{1,8},{2,1},{3,9},{4,3},{5,11},{6,2},{7,10},{8,4},{9,12},{10... | collective-permute-start | bytes 2506760 | tf_op jit(solution)/shard_map/ppermute | solution.py:88
  58.6 0.7 collective-permute-start.8
  59.6 2.0 collective-permute-start.9
  61.6 15.8 %collective-permute-done.2.own = bf16[272,1536]{1,0:T(8,128)(2,1)S(1)} collective-permute-done((bf16[272,1536]{1,0:T(8,128)(2,1)S(1)}, bf16[272,1536]{1,0:T(8,128)(2,1)S(1)}, u32[]{:S(2)}, u32[]{:S(2)}) %collective-permute-start.2) | collective-permute-done | bytes 835616 | tf_op jit(solution)/shard_map/ppermute | solution.py:88
  77.4 27.8 %collective-permute-start.6 = (bf16[272,1536]{1,0:T(8,128)(2,1)S(1)}, bf16[272,1536]{1,0:T(8,128)(2,1)S(1)}, u32[]{:S(2)}, u32[]{:S(2)}) collective-permute-start(bf16[272,1536]{1,0:T(8,128)(2,1)S(1)} %collective-permute-done.2.own), channel_id=1, source_target_pairs={{8,0},{1,8},{9,1},{3,9},{11,3},{2,11},{10,2},{12,4},{5,12},{13,5},... | collective-permute-start | bytes 2506760 | tf_op jit(solution)/shard_map/ppermute | solution.py:88
  105.2 2.1 collective-permute-start.5
  107.3 0.9 broadcast_select_fusion.3
  108.2 12.7 %collective-permute-done.6.up = bf16[272,1536]{1,0:T(8,128)(2,1)S(1)} collective-permute-done((bf16[272,1536]{1,0:T(8,128)(2,1)S(1)}, bf16[272,1536]{1,0:T(8,128)(2,1)S(1)}, u32[]{:S(2)}, u32[]{:S(2)}) %collective-permute-start.6) | collective-permute-done | bytes 835616 | tf_op jit(solution)/shard_map/ppermute | solution.py:88
  120.8 2.1 collective-permute-done.5.low
  122.9 0.9 copy-done.8
  124.0 3.5 pad_maximum_fusion.rest_0_
  127.5 9.5 %collective-permute-start.11 = (bf16[4,192,4608]{2,1,0:T(8,128)(2,1)}, bf16[4,192,4608]{2,1,0:T(8,128)(2,1)}, u32[]{:S(2)}, u32[]{:S(2)}) collective-permute-start(bf16[4,192,4608]{2,1,0:T(8,128)(2,1)} %pad_maximum_fusion.rest_0_), channel_id=1, source_target_pairs={{0,8},{1,9},{2,10},{3,11},{4,12},{5,13},{6,14},{7,15},{8,0},{9,1},... | collective-permute-start | bytes 21233672 | tf_op jit(solution)/shard_map/ppermute | solution.py:88
  137.1 1.2 collective-permute-start.13
  138.2 1.6 collective-permute-start.12
  140.4 1.5 fusion.2
  141.9 0.7 slice.298
  142.5 0.7 slice.299
  143.2 0.7 slice.300
  144.6 0.8 copy.79.seg_rows
  145.4 1.4 constant_dynamic-slice_fusion
  146.8 1.5 collective-permute-done.11.rest_1_
  148.3 26.9 %attention.1.context = bf16[288,1536]{1,0:T(8,128)(2,1)} custom-call(s32[8]{0:T(128)} %add_multiply_fusion.offsets, bf16[272,1536]{1,0:T(8,128)(2,1)} %copy-done.8, bf16[272,1536]{1,0:T(8,128)(2,1)} %copy-done.6, bf16[272,1536]{1,0:T(8,128)(2,1)} %copy-done.7, f32[1,1536]{1,0:T(1,128)} %get-tuple-element.70.gain.gain_a, s32[288,1]{1,0:T(8,128)} %copy.79.seg_rows, ...), custom_call_target="tpu_custom_call" | custom-call | flops 9965666304 | bytes 17301504 | tf_op jit(solution)/shard_map/attention/pallas_call | solution.py:254
  175.2 2.4 collective-permute-done.13
  177.6 1.4 collective-permute-done.12
  179.0 4.4 %pad_maximum_fusion.1.rest_0_.rest_2_ = bf16[3,192,4608]{2,1,0:T(8,128)(2,1)} fusion(bf16[1,192,4608]{2,1,0:T(8,128)(2,1)S(1)} %bitcast.162, bf16[1,192,4608]{2,1,0:T(8,128)(2,1)} %bitcast.42, bf16[1,192,4608]{2,1,0:T(8,128)(2,1)S(1)} %bitcast.160), kind=kLoop, calls=%fused_computation.1 | loop fusion | flops 5308416 | bytes 10616832 | tf_op jit(solution)/shard_map/stack | solution.py:141
  183.6 1.2 slice.339
  185.3 1.4 collective-permute-start.14
  186.7 20.2 %collective-permute-done.15 = bf16[192,2304]{1,0:T(8,128)(2,1)S(1)} collective-permute-done((bf16[192,2304]{1,0:T(8,128)(2,1)S(1)}, bf16[192,2304]{1,0:T(8,128)(2,1)S(1)}, u32[]{:S(2)}, u32[]{:S(2)}) %collective-permute-start.15) | collective-permute-done | bytes 884768 | tf_op jit(solution)/shard_map/ppermute | solution.py:88
  207.3 1.6 collective-permute-start.19
  208.9 1.6 collective-permute-start.18
  210.5 1.6 slice.379.taps
  212.1 2.6 dynamic-slice_bitcast_fusion.19
  214.7 0.8 copy.80.seg_rows
  215.5 2.0 dynamic-slice_bitcast_fusion.35
  217.5 5.2 %stack.274 = s32[256,31]{0,1:T(8,128)} concatenate(s32[256,1]{0,1:T(1,128)} %get-tuple-element.116, s32[256,1]{0,1:T(1,128)} %get-tuple-element.115, s32[256,1]{0,1:T(1,128)} %get-tuple-element.114, s32[256,1]{0,1:T(1,128)} %get-tuple-element.113, s32[256,1]{0,1:T(1,128)} %get-tuple-element.112, s32[256,1]{0,1:T(1,128)} %get-tuple-element.111, s32[256,1]{0,1:T(1,128)} %get-tuple-element.110, ...), dimensions={1} | concatenate | bytes 63488 | tf_op jit(solution)/shard_map/stack | solution.py:360
  222.8 1.5 copy.81.masks_seg
  224.9 1.5 collective-permute-start.20
  226.4 23.0 %convolution.1 = (bf16[256,1536]{1,0:T(8,128)(2,1)}, f32[256,1536]{1,0:T(8,128)}) custom-call(s32[8]{0:T(128)} %add_multiply_fusion.offsets, bf16[288,1536]{1,0:T(8,128)(2,1)} %attention.1.context, bf16[272,1536]{1,0:T(8,128)(2,1)} %copy-done.8, bf16[272,1536]{1,0:T(8,128)(2,1)} %copy-done.6, bf16[272,1536]{1,0:T(8,128)(2,1)} %copy-done.7, ...), custom_call_target="tpu_custom_call" | custom-call | flops 4113432576 | bytes 17301504 | tf_op jit(solution)/shard_map/convolution/pallas_call | solution.py:361
  249.9 0.7 collective-permute-start.24
  250.6 3.8 collective-permute-done.22.rest_1_.rest_7_
  254.4 1.5 copy-done.3
  255.9 5.8 %mixing.1 = bf16[256,1536]{1,0:T(8,128)(2,1)} custom-call(s32[8]{0:T(128)} %add_multiply_fusion.offsets, bf16[256,1536]{1,0:T(8,128)(2,1)} %get-tuple-element.54.act, f32[256,1536]{1,0:T(8,128)} %get-tuple-element.55.resid, bf16[4,192,1536]{2,1,0:T(8,128)(2,1)} %copy-done, bf16[4,192,1536]{2,1,0:T(8,128)(2,1)} %copy-done.3), custom_call_target="tpu_custom_call" | custom-call | flops 1207959552 | bytes 7864320 | tf_op jit(solution)/shard_map/mixing/pallas_call | solution.py:408
  261.9 4.1 %collective-permute-start.25 = (bf16[256,1536]{1,0:T(8,128)(2,1)}, bf16[256,1536]{1,0:T(8,128)(2,1)S(1)}, u32[]{:S(2)}, u32[]{:S(2)}) collective-permute-start(bf16[256,1536]{1,0:T(8,128)(2,1)} %mixing.1), channel_id=1, source_target_pairs={{0,4},{8,12},{1,5},{9,13},{3,7},{11,15},{2,6},{10,14},{4,16},{12,2... | collective-permute-start | bytes 2359304 | tf_op jit(solution)/shard_map/ppermute | solution.py:88
  265.9 41.4 %collective-permute-done.25 = bf16[256,1536]{1,0:T(8,128)(2,1)S(1)} collective-permute-done((bf16[256,1536]{1,0:T(8,128)(2,1)}, bf16[256,1536]{1,0:T(8,128)(2,1)S(1)}, u32[]{:S(2)}, u32[]{:S(2)}) %collective-permute-start.25) | collective-permute-done | bytes 786464 | tf_op jit(solution)/shard_map/ppermute | solution.py:88
  307.4 1.9 collective-permute-start.27
  309.3 2.8 collective-permute-start.26
  312.2 0.8 copy.83.seg_rows
  313.4 0.8 copy.84.masks_seg
  314.1 0.8 copy.82.seg_queries
  314.9 1.9 collective-permute-start.23
  316.8 2.0 collective-permute-done.27.up
  318.8 6.1 %collective-permute-done.26.low = bf16[256,1536]{1,0:T(8,128)(2,1)} collective-permute-done((bf16[256,1536]{1,0:T(8,128)(2,1)S(1)}, bf16[256,1536]{1,0:T(8,128)(2,1)}, u32[]{:S(2)}, u32[]{:S(2)}) %collective-permute-start.26) | collective-permute-done | bytes 786464 | tf_op jit(solution)/shard_map/ppermute | solution.py:88
  324.9 49.7 %tick.1 = bf16[256,1536]{1,0:T(8,128)(2,1)} custom-call(s32[8]{0:T(128)} %add_multiply_fusion.offsets, bf16[256,1536]{1,0:T(8,128)(2,1)} %collective-permute-done.26.low, bf16[256,1536]{1,0:T(8,128)(2,1)} %copy-done.9, bf16[256,1536]{1,0:T(8,128)(2,1)} %copy-done.28, f32[1,1536]{1,0:T(1,128)} %get-tuple-element.70.gain.gain_a, ...), custom_call_target="tpu_custom_call" | custom-call | flops 14042529792 | bytes 33030144 | tf_op jit(solution)/shard_map/tick/pallas_call | solution.py:460
  374.6 1.9 collective-permute-start.28
  376.6 19.8 %collective-permute-done.28 = bf16[256,1536]{1,0:T(8,128)(2,1)S(1)} collective-permute-done((bf16[256,1536]{1,0:T(8,128)(2,1)}, bf16[256,1536]{1,0:T(8,128)(2,1)S(1)}, u32[]{:S(2)}, u32[]{:S(2)}) %collective-permute-start.28) | collective-permute-done | bytes 786464 | tf_op jit(solution)/shard_map/ppermute | solution.py:88
  396.4 1.3 maximum_bitcast_fusion.2
  (99 shorter events, 5.5 us)
Async XLA Ops:
  0.0 5.6 %copy-start.5 = (bf16[1,192,3072]{2,1,0:T(8,128)(2,1)S(1)}, bf16[1,192,3072]{2,1,0:T(8,128)(2,1)}, u32[]{:S(2)}) copy-start(bf16[1,192,3072]{2,1,0:T(8,128)(2,1)} %param.17) | copy-start | bytes 3538948
  1.8 1.6 collective-permute-start
  4.8 2.1 collective-permute-start.1
  5.6 1.7 copy-start.4
  6.9 3.5 copy-start.15
  6.9 3.5 copy-start.10
  7.4 50.9 %collective-permute-start.7 = (bf16[192,4608]{1,0:T(8,128)(2,1)S(1)}, bf16[192,4608]{1,0:T(8,128)(2,1)S(1)}, u32[]{:S(2)}, u32[]{:S(2)}) collective-permute-start(bf16[192,4608]{1,0:T(8,128)(2,1)S(1)} %pad_maximum_fusion.3), channel_id=1, source_target_pairs={{4,8},{5,9},{6,10},{7,11},{8,4},{9,5},{10,6},{11,7},{20,24},{21,25... | collective-permute-start | bytes 5308424 | tf_op jit(solution)/shard_map/ppermute | solution.py:88
  8.2 51.1 %collective-permute-start.4 = (bf16[192,4608]{1,0:T(8,128)(2,1)S(1)}, bf16[192,4608]{1,0:T(8,128)(2,1)S(1)}, u32[]{:S(2)}, u32[]{:S(2)}) collective-permute-start(bf16[192,4608]{1,0:T(8,128)(2,1)S(1)} %broadcast_select_fusion.1), channel_id=1, source_target_pairs={{0,2},{1,3},{2,0},{3,1},{4,6},{5,7},{6,4},{7,5},{8,10},{9,11},{10,... | collective-permute-start | bytes 5308424 | tf_op jit(solution)/shard_map/ppermute | solution.py:88
  9.9 49.4 %collective-permute-start.3 = (bf16[192,4608]{1,0:T(8,128)(2,1)S(1)}, bf16[192,4608]{1,0:T(8,128)(2,1)S(1)}, u32[]{:S(2)}, u32[]{:S(2)}) collective-permute-start(bf16[192,4608]{1,0:T(8,128)(2,1)S(1)} %broadcast_select_fusion.1), channel_id=1, source_target_pairs={{0,1},{1,0},{2,3},{3,2},{4,5},{5,4},{6,7},{7,6},{8,9},{9,8},{10,11... | collective-permute-start | bytes 5308424 | tf_op jit(solution)/shard_map/ppermute | solution.py:88
  10.5 48.1 %copy-start.12 = (bf16[1,192,1536]{2,1,0:T(8,128)(2,1)S(1)}, bf16[1,192,1536]{2,1,0:T(8,128)(2,1)}, u32[]{:S(2)}) copy-start(bf16[1,192,1536]{2,1,0:T(8,128)(2,1)} %param.19) | copy-start | bytes 1769476
  10.5 66.9 %collective-permute-start.2 = (bf16[272,1536]{1,0:T(8,128)(2,1)S(1)}, bf16[272,1536]{1,0:T(8,128)(2,1)S(1)}, u32[]{:S(2)}, u32[]{:S(2)}) collective-permute-start(bf16[272,1536]{1,0:T(8,128)(2,1)S(1)} %fusion.1), channel_id=1, source_target_pairs={{0,0},{1,8},{2,1},{3,9},{4,3},{5,11},{6,2},{7,10},{8,4},{9,12},{10... | collective-permute-start | bytes 2506760 | tf_op jit(solution)/shard_map/ppermute | solution.py:88
  58.6 48.7 %collective-permute-start.8 = (bf16[192,1536]{1,0:T(8,128)(2,1)S(1)}, bf16[192,1536]{1,0:T(8,128)(2,1)S(1)}, u32[]{:S(2)}, u32[]{:S(2)}) collective-permute-start(bf16[192,1536]{1,0:T(8,128)(2,1)S(1)} %bitcast.175), channel_id=1, source_target_pairs={{4,8},{5,9},{6,10},{7,11},{8,4},{9,5},{10,6},{11,7},{20,24},{21,25... | collective-permute-start | bytes 1769480 | tf_op jit(solution)/shard_map/ppermute | solution.py:88
  59.5 63.5 %collective-permute-start.10 = (bf16[192,2304]{1,0:T(8,128)(2,1)S(1)}, bf16[192,2304]{1,0:T(8,128)(2,1)S(1)}, u32[]{:S(2)}, u32[]{:S(2)}) collective-permute-start(bf16[192,2304]{1,0:T(8,128)(2,1)S(1)} %get-tuple-element.67), channel_id=1, source_target_pairs={{0,1},{1,0},{2,3},{3,2},{4,6},{5,7},{6,4},{7,5},{8,10},{9,11},{10,... | collective-permute-start | bytes 2654216 | tf_op jit(solution)/shard_map/ppermute | solution.py:88
  59.6 64.3 %collective-permute-start.9 = (bf16[192,2304]{1,0:T(8,128)(2,1)S(1)}, bf16[192,2304]{1,0:T(8,128)(2,1)S(1)}, u32[]{:S(2)}, u32[]{:S(2)}) collective-permute-start(bf16[192,2304]{1,0:T(8,128)(2,1)S(1)} %get-tuple-element.68), channel_id=1, source_target_pairs={{0,1},{1,0},{2,3},{3,2},{4,5},{5,4},{6,7},{7,6},{8,9},{9,8},{10,11... | collective-permute-start | bytes 2654216 | tf_op jit(solution)/shard_map/ppermute | solution.py:88
  77.4 46.6 %copy-start.6 = (bf16[272,1536]{1,0:T(8,128)(2,1)}, bf16[272,1536]{1,0:T(8,128)(2,1)S(1)}, u32[]{:S(2)}) copy-start(bf16[272,1536]{1,0:T(8,128)(2,1)S(1)} %collective-permute-done.2.own) | copy-start | bytes 2506756
  77.4 43.4 %collective-permute-start.6 = (bf16[272,1536]{1,0:T(8,128)(2,1)S(1)}, bf16[272,1536]{1,0:T(8,128)(2,1)S(1)}, u32[]{:S(2)}, u32[]{:S(2)}) collective-permute-start(bf16[272,1536]{1,0:T(8,128)(2,1)S(1)} %collective-permute-done.2.own), channel_id=1, source_target_pairs={{8,0},{1,8},{9,1},{3,9},{11,3},{2,11},{10,2},{12,4},{5,12},{13,5},... | collective-permute-start | bytes 2506760 | tf_op jit(solution)/shard_map/ppermute | solution.py:88
  105.2 17.8 %collective-permute-start.5 = (bf16[272,1536]{1,0:T(8,128)(2,1)S(1)}, bf16[272,1536]{1,0:T(8,128)(2,1)S(1)}, u32[]{:S(2)}, u32[]{:S(2)}) collective-permute-start(bf16[272,1536]{1,0:T(8,128)(2,1)S(1)} %collective-permute-done.2.own), channel_id=1, source_target_pairs={{0,8},{8,1},{1,9},{9,3},{3,11},{11,2},{2,10},{4,12},{12,5},{5,13},... | collective-permute-start | bytes 2506760 | tf_op jit(solution)/shard_map/ppermute | solution.py:88
  120.8 2.1 copy-start.7
  122.9 0.9 copy-start.8
  127.5 20.8 %collective-permute-start.11 = (bf16[4,192,4608]{2,1,0:T(8,128)(2,1)}, bf16[4,192,4608]{2,1,0:T(8,128)(2,1)}, u32[]{:S(2)}, u32[]{:S(2)}) collective-permute-start(bf16[4,192,4608]{2,1,0:T(8,128)(2,1)} %pad_maximum_fusion.rest_0_), channel_id=1, source_target_pairs={{0,8},{1,9},{2,10},{3,11},{4,12},{5,13},{6,14},{7,15},{8,0},{9,1},... | collective-permute-start | bytes 21233672 | tf_op jit(solution)/shard_map/ppermute | solution.py:88
  137.1 40.6 %collective-permute-start.13 = (bf16[192,4608]{1,0:T(8,128)(2,1)S(1)}, bf16[192,4608]{1,0:T(8,128)(2,1)S(1)}, u32[]{:S(2)}, u32[]{:S(2)}) collective-permute-start(bf16[192,4608]{1,0:T(8,128)(2,1)S(1)} %broadcast_select_fusion), channel_id=1, source_target_pairs={{0,2},{1,3},{2,0},{3,1},{4,6},{5,7},{6,4},{7,5},{8,10},{9,11},{10,... | collective-permute-start | bytes 5308424 | tf_op jit(solution)/shard_map/ppermute | solution.py:88
  138.2 40.8 %collective-permute-start.12 = (bf16[192,4608]{1,0:T(8,128)(2,1)S(1)}, bf16[192,4608]{1,0:T(8,128)(2,1)}, u32[]{:S(2)}, u32[]{:S(2)}) collective-permute-start(bf16[192,4608]{1,0:T(8,128)(2,1)S(1)} %broadcast_select_fusion), channel_id=1, source_target_pairs={{0,1},{1,0},{2,3},{3,2},{4,5},{5,4},{6,7},{7,6},{8,9},{9,8},{10,11... | collective-permute-start | bytes 5308424 | tf_op jit(solution)/shard_map/ppermute | solution.py:88
  143.9 0.6 copy-start.13
  183.4 43.0 %collective-permute-start.16 = (bf16[3,192,4608]{2,1,0:T(8,128)(2,1)}, bf16[3,192,4608]{2,1,0:T(8,128)(2,1)}, u32[]{:S(2)}, u32[]{:S(2)}) collective-permute-start(bf16[3,192,4608]{2,1,0:T(8,128)(2,1)} %pad_maximum_fusion.1.rest_0_.rest_2_), channel_id=1, source_target_pairs={{0,8},{1,9},{2,10},{3,11},{4,12},{5,13},{6,14},{7,15},{8,0},{9,1},... | collective-permute-start | bytes 15925256 | tf_op jit(solution)/shard_map/ppermute | solution.py:88
  184.8 22.5 %copy-start.2 = (bf16[192,1536]{1,0:T(8,128)(2,1)S(1)}, bf16[192,1536]{1,0:T(8,128)(2,1)}, u32[]{:S(2)}) copy-start(bf16[192,1536]{1,0:T(8,128)(2,1)} %broadcast_select_fusion.3) | copy-start | bytes 1769476
  184.8 22.1 %collective-permute-start.15 = (bf16[192,2304]{1,0:T(8,128)(2,1)S(1)}, bf16[192,2304]{1,0:T(8,128)(2,1)S(1)}, u32[]{:S(2)}, u32[]{:S(2)}) collective-permute-start(bf16[192,2304]{1,0:T(8,128)(2,1)S(1)} %slice.339), channel_id=1, source_target_pairs={{0,2},{1,3},{2,0},{3,1},{4,6},{5,7},{6,4},{7,5},{8,10},{9,11},{10,... | collective-permute-start | bytes 2654216 | tf_op jit(solution)/shard_map/ppermute | solution.py:88
  185.3 21.8 %collective-permute-start.14 = (bf16[192,2304]{1,0:T(8,128)(2,1)S(1)}, bf16[192,2304]{1,0:T(8,128)(2,1)S(1)}, u32[]{:S(2)}, u32[]{:S(2)}) collective-permute-start(bf16[192,2304]{1,0:T(8,128)(2,1)S(1)} %slice.338), channel_id=1, source_target_pairs={{0,1},{1,0},{2,3},{3,2},{4,5},{5,4},{6,7},{7,6},{8,9},{9,8},{10,11... | collective-permute-start | bytes 2654216 | tf_op jit(solution)/shard_map/ppermute | solution.py:88
  207.2 19.2 %copy-start.1 = (bf16[1,192,4608]{2,1,0:T(8,128)(2,1)}, bf16[1,192,4608]{2,1,0:T(8,128)(2,1)S(1)}, u32[]{:S(2)}) copy-start(bf16[1,192,4608]{2,1,0:T(8,128)(2,1)S(1)} %maximum_bitcast_fusion.1.rest_1_.rest_3_) | copy-start | bytes 5308420
  207.2 19.2 %collective-permute-start.17 = (bf16[1,192,4608]{2,1,0:T(8,128)(2,1)S(1)}, bf16[1,192,4608]{2,1,0:T(8,128)(2,1)}, u32[]{:S(2)}, u32[]{:S(2)}) collective-permute-start(bf16[1,192,4608]{2,1,0:T(8,128)(2,1)S(1)} %maximum_bitcast_fusion.1.rest_1_.rest_3_), channel_id=1, source_target_pairs={{0,8},{1,9},{2,10},{3,11},{4,12},{5,13},{6,14},{7,15},{8,0},{9,1},... | collective-permute-start | bytes 5308424 | tf_op jit(solution)/shard_map/ppermute | solution.py:88
  207.3 17.0 %collective-permute-start.19 = (bf16[192,1536]{1,0:T(8,128)(2,1)S(1)}, bf16[192,1536]{1,0:T(8,128)(2,1)S(1)}, u32[]{:S(2)}, u32[]{:S(2)}) collective-permute-start(bf16[192,1536]{1,0:T(8,128)(2,1)S(1)} %copy-done.2), channel_id=1, source_target_pairs={{0,2},{1,3},{2,0},{3,1},{4,6},{5,7},{6,4},{7,5},{8,10},{9,11},{10,... | collective-permute-start | bytes 1769480 | tf_op jit(solution)/shard_map/ppermute | solution.py:88
  208.9 15.4 %collective-permute-start.18 = (bf16[192,1536]{1,0:T(8,128)(2,1)S(1)}, bf16[192,1536]{1,0:T(8,128)(2,1)S(1)}, u32[]{:S(2)}, u32[]{:S(2)}) collective-permute-start(bf16[192,1536]{1,0:T(8,128)(2,1)S(1)} %copy-done.2), channel_id=1, source_target_pairs={{0,1},{1,0},{2,3},{3,2},{4,5},{5,4},{6,7},{7,6},{8,9},{9,8},{10,11... | collective-permute-start | bytes 1769480 | tf_op jit(solution)/shard_map/ppermute | solution.py:88
  224.4 25.0 %collective-permute-start.21 = (bf16[192,768]{1,0:T(8,128)(2,1)S(1)}, bf16[192,768]{1,0:T(8,128)(2,1)S(1)}, u32[]{:S(2)}, u32[]{:S(2)}) collective-permute-start(bf16[192,768]{1,0:T(8,128)(2,1)S(1)} %slice.341), channel_id=1, source_target_pairs={{0,2},{1,3},{2,0},{3,1},{4,6},{5,7},{6,4},{7,5},{8,10},{9,11},{10,... | collective-permute-start | bytes 884744 | tf_op jit(solution)/shard_map/ppermute | solution.py:88
  224.9 24.5 %collective-permute-start.20 = (bf16[192,768]{1,0:T(8,128)(2,1)S(1)}, bf16[192,768]{1,0:T(8,128)(2,1)S(1)}, u32[]{:S(2)}, u32[]{:S(2)}) collective-permute-start(bf16[192,768]{1,0:T(8,128)(2,1)S(1)} %slice.340), channel_id=1, source_target_pairs={{0,1},{1,0},{2,3},{3,2},{4,5},{5,4},{6,7},{7,6},{8,9},{9,8},{10,11... | collective-permute-start | bytes 884744 | tf_op jit(solution)/shard_map/ppermute | solution.py:88
  249.8 4.6 %copy-start = (bf16[4,192,1536]{2,1,0:T(8,128)(2,1)}, bf16[4,192,1536]{2,1,0:T(8,128)(2,1)S(1)}, u32[]{:S(2)}) copy-start(bf16[4,192,1536]{2,1,0:T(8,128)(2,1)S(1)} %pad_maximum_fusion.2.rest_0_.rest_6_) | copy-start | bytes 7077892
  249.8 4.6 %collective-permute-start.22 = (bf16[4,192,1536]{2,1,0:T(8,128)(2,1)S(1)}, bf16[4,192,1536]{2,1,0:T(8,128)(2,1)S(1)}, u32[]{:S(2)}, u32[]{:S(2)}) collective-permute-start(bf16[4,192,1536]{2,1,0:T(8,128)(2,1)S(1)} %pad_maximum_fusion.2.rest_0_.rest_6_), channel_id=1, source_target_pairs={{0,8},{1,9},{2,10},{3,11},{4,12},{5,13},{6,14},{7,15},{8,0},{9,1},... | collective-permute-start | bytes 7077896 | tf_op jit(solution)/shard_map/ppermute | solution.py:88
  249.9 16.1 %collective-permute-start.24 = (bf16[256,1536]{1,0:T(8,128)(2,1)}, bf16[256,1536]{1,0:T(8,128)(2,1)S(1)}, u32[]{:S(2)}, u32[]{:S(2)}) collective-permute-start(bf16[256,1536]{1,0:T(8,128)(2,1)} %bitcast.50), channel_id=1, source_target_pairs={{0,0},{1,8},{2,1},{3,9},{4,3},{5,11},{6,2},{7,10}} | collective-permute-start | bytes 2359304 | tf_op jit(solution)/shard_map/ppermute | solution.py:88
  254.4 1.5 copy-start.3
  261.7 51.3 %copy-start.14 = (s32[5,768]{1,0:T(8,128)S(1)}, s32[5,768]{1,0:T(8,128)}, u32[]{:S(2)}) copy-start(s32[5,768]{1,0:T(8,128)} %copy-done.13) | copy-start | bytes 46084
  261.7 51.4 %copy-start.16 = (s32[256,1]{0,1:T(1,128)S(1)}, s32[256,1]{0,1:T(1,128)}, u32[]{:S(2)}) copy-start(s32[256,1]{0,1:T(1,128)} %get-tuple-element.89) | copy-start | bytes 3076
  261.7 51.4 %copy-start.17 = (s32[256,1]{0,1:T(1,128)S(1)}, s32[256,1]{0,1:T(1,128)}, u32[]{:S(2)}) copy-start(s32[256,1]{0,1:T(1,128)} %get-tuple-element.90) | copy-start | bytes 3076
  261.7 51.4 %copy-start.18 = (s32[256,1]{0,1:T(1,128)S(1)}, s32[256,1]{0,1:T(1,128)}, u32[]{:S(2)}) copy-start(s32[256,1]{0,1:T(1,128)} %get-tuple-element.91) | copy-start | bytes 3076
  261.8 51.4 %copy-start.19 = (s32[256,1]{0,1:T(1,128)S(1)}, s32[256,1]{0,1:T(1,128)}, u32[]{:S(2)}) copy-start(s32[256,1]{0,1:T(1,128)} %get-tuple-element.92) | copy-start | bytes 3076
  261.8 51.4 %copy-start.20 = (s32[256,1]{0,1:T(1,128)S(1)}, s32[256,1]{0,1:T(1,128)}, u32[]{:S(2)}) copy-start(s32[256,1]{0,1:T(1,128)} %get-tuple-element.93) | copy-start | bytes 3076
  261.8 51.4 %copy-start.21 = (s32[256,1]{0,1:T(1,128)S(1)}, s32[256,1]{0,1:T(1,128)}, u32[]{:S(2)}) copy-start(s32[256,1]{0,1:T(1,128)} %get-tuple-element.94) | copy-start | bytes 3076
  261.8 51.4 %copy-start.22 = (s32[256,1]{0,1:T(1,128)S(1)}, s32[256,1]{0,1:T(1,128)}, u32[]{:S(2)}) copy-start(s32[256,1]{0,1:T(1,128)} %get-tuple-element.95) | copy-start | bytes 3076
  261.8 51.4 %copy-start.23 = (s32[256,1]{0,1:T(1,128)S(1)}, s32[256,1]{0,1:T(1,128)}, u32[]{:S(2)}) copy-start(s32[256,1]{0,1:T(1,128)} %get-tuple-element.96) | copy-start | bytes 3076
  261.8 51.4 %copy-start.24 = (s32[256,1]{0,1:T(1,128)S(1)}, s32[256,1]{0,1:T(1,128)}, u32[]{:S(2)}) copy-start(s32[256,1]{0,1:T(1,128)} %get-tuple-element.97) | copy-start | bytes 3076
  261.8 51.4 %copy-start.25 = (s32[256,1]{0,1:T(1,128)S(1)}, s32[256,1]{0,1:T(1,128)}, u32[]{:S(2)}) copy-start(s32[256,1]{0,1:T(1,128)} %get-tuple-element.98) | copy-start | bytes 3076
  261.8 51.4 %copy-start.26 = (s32[256,1]{0,1:T(1,128)S(1)}, s32[256,1]{0,1:T(1,128)}, u32[]{:S(2)}) copy-start(s32[256,1]{0,1:T(1,128)} %get-tuple-element.99) | copy-start | bytes 3076
  261.8 51.4 %copy-start.27 = (s32[256,1]{0,1:T(1,128)S(1)}, s32[256,1]{0,1:T(1,128)}, u32[]{:S(2)}) copy-start(s32[256,1]{0,1:T(1,128)} %get-tuple-element.100) | copy-start | bytes 3076
  261.8 53.1 %copy-start.11 = (bf16[256,1536]{1,0:T(8,128)(2,1)S(1)}, bf16[256,1536]{1,0:T(8,128)(2,1)}, u32[]{:S(2)}) copy-start(bf16[256,1536]{1,0:T(8,128)(2,1)} %mixing.1) | copy-start | bytes 2359300
  261.9 45.5 %collective-permute-start.25 = (bf16[256,1536]{1,0:T(8,128)(2,1)}, bf16[256,1536]{1,0:T(8,128)(2,1)S(1)}, u32[]{:S(2)}, u32[]{:S(2)}) collective-permute-start(bf16[256,1536]{1,0:T(8,128)(2,1)} %mixing.1), channel_id=1, source_target_pairs={{0,4},{8,12},{1,5},{9,13},{3,7},{11,15},{2,6},{10,14},{4,16},{12,2... | collective-permute-start | bytes 2359304 | tf_op jit(solution)/shard_map/ppermute | solution.py:88
  307.4 17.5 %copy-start.9 = (bf16[256,1536]{1,0:T(8,128)(2,1)}, bf16[256,1536]{1,0:T(8,128)(2,1)S(1)}, u32[]{:S(2)}) copy-start(bf16[256,1536]{1,0:T(8,128)(2,1)S(1)} %broadcast_select_fusion.2.own) | copy-start | bytes 2359300
  307.4 11.4 %collective-permute-start.27 = (bf16[256,1536]{1,0:T(8,128)(2,1)S(1)}, bf16[256,1536]{1,0:T(8,128)(2,1)S(1)}, u32[]{:S(2)}, u32[]{:S(2)}) collective-permute-start(bf16[256,1536]{1,0:T(8,128)(2,1)S(1)} %broadcast_select_fusion.2.own), channel_id=1, source_target_pairs={{8,0},{1,8},{9,1},{3,9},{11,3},{2,11},{10,2},{12,4},{5,12},{13,5},... | collective-permute-start | bytes 2359304 | tf_op jit(solution)/shard_map/ppermute | solution.py:88
  309.3 15.6 %collective-permute-start.26 = (bf16[256,1536]{1,0:T(8,128)(2,1)S(1)}, bf16[256,1536]{1,0:T(8,128)(2,1)}, u32[]{:S(2)}, u32[]{:S(2)}) collective-permute-start(bf16[256,1536]{1,0:T(8,128)(2,1)S(1)} %broadcast_select_fusion.2.own), channel_id=1, source_target_pairs={{0,8},{8,1},{1,9},{9,3},{3,11},{11,2},{2,10},{4,12},{12,5},{5,13},... | collective-permute-start | bytes 2359304 | tf_op jit(solution)/shard_map/ppermute | solution.py:88
  314.9 61.7 %collective-permute-start.23 = (bf16[256,1536]{1,0:T(8,128)(2,1)S(1)}, bf16[256,1536]{1,0:T(8,128)(2,1)S(1)}, u32[]{:S(2)}, u32[]{:S(2)}) collective-permute-start(bf16[256,1536]{1,0:T(8,128)(2,1)S(1)} %copy-done.11), channel_id=1, source_target_pairs={{0,0},{8,1},{1,2},{9,3},{3,4},{11,5},{2,6},{10,7},{4,8},{12,9},{5,... | collective-permute-start | bytes 2359304 | tf_op jit(solution)/shard_map/ppermute | solution.py:88
  318.8 6.1 %copy-start.28 = (bf16[256,1536]{1,0:T(8,128)(2,1)}, bf16[256,1536]{1,0:T(8,128)(2,1)S(1)}, u32[]{:S(2)}) copy-start(bf16[256,1536]{1,0:T(8,128)(2,1)S(1)} %collective-permute-done.27.up) | copy-start | bytes 2359300
  374.6 21.8 %collective-permute-start.28 = (bf16[256,1536]{1,0:T(8,128)(2,1)}, bf16[256,1536]{1,0:T(8,128)(2,1)S(1)}, u32[]{:S(2)}, u32[]{:S(2)}) collective-permute-start(bf16[256,1536]{1,0:T(8,128)(2,1)} %tick.1), channel_id=1, source_target_pairs={{0,0},{8,1},{1,2},{9,3},{3,4},{11,5},{2,6},{10,7},{4,8},{12,9},{5,... | collective-permute-start | bytes 2359304 | tf_op jit(solution)/shard_map/ppermute | solution.py:88

commit v6 on v5

--- a/solution.py
+++ b/solution.py
@@ -560,11 +560,12 @@
             act, resid = convolution(offsets, out_expand, context, low, present, up, gain_c, seg_wide, taps)
             mix = weights.whole(own_3, sides_3, diagonal_3, act)
             made = mixing(offsets, mix, act, resid)
-        made_all.append(send(made, layout.to_homes()))
         if tick + 1 < ticks:
             arrived = send(made, layout.relay())
             present = jnp.where(section == 0, newcomers[tick], arrived)
             low, up = send(present, layout.shifted(1)), send(present, layout.shifted(-1))
+            made = behind(made, low, up)
+        made_all.append(send(made, layout.to_homes()))
     return jnp.stack(made_all)[:, None]
 
 

time: 402 us -> 404 us (level)
  no operation moved by 1% of the time
where the time goes in v6:
time: 404 us; the launch traced here: 400 us
  waiting for transfers between devices  130 us (32%)
  starting transfers between devices  120 us (30%)
  Pallas kernels  105 us (26%)
  local copies, waits for them, and re-layouts  28 us (7%)
  other arithmetic  15.5 us (4%)
    ppermute x29, waiting for transfers between devices, send(): return lax.ppermute(value, AXES, moves)  130 us
    ppermute x29, starting transfers between devices, send(): return lax.ppermute(value, AXES, moves)  120 us
    pallas_call x1, Pallas kernels, whole_tick(): pl.pallas_call(functools.partial(tick_kernel, (len(qkv), len(expand), len...  49.7 us
    pallas_call x1, Pallas kernels, attention(): pl.pallas_call(functools.partial(attention_kernel, len(weight)), out_shap...  26.9 us
    pallas_call x1, Pallas kernels, convolution(): pl.pallas_call(functools.partial(convolution_kernel, len(weight)), out_sh...  23 us
    another operation x3, local copies, waits for them, and re-layouts, convolution(): jnp.stack([seg_wide[first + tap:first + tap + rows] for tap in range(KERN...  8.73 us
  transfers between devices with their start and end apart: 29, of which 15 were waited for; matrix products, arithmetic and copies ran while one was open for 7% of the time, Pallas kernels for 26%

profile of v6, /device:TPU:6, one launch (start us, length us, event | category | flops | bytes accessed | tf_op | source)
XLA Modules:
  0.0 400.1 jit_solution(1119327176006657496)
XLA Ops:
  0.0 1.0 copy.88
  1.0 0.8 pad_maximum_fusion.4
  1.9 1.5 collective-permute-done
  3.4 1.5 broadcast_select_fusion.4
  4.8 0.8 collective-permute-start.1
  5.6 1.3 pad_maximum_fusion.3
  7.4 0.8 collective-permute-start.7
  8.2 1.6 collective-permute-start.4
  10.5 47.9 %collective-permute-start.2 = (bf16[272,1536]{1,0:T(8,128)(2,1)S(1)}, bf16[272,1536]{1,0:T(8,128)(2,1)S(1)}, u32[]{:S(2)}, u32[]{:S(2)}) collective-permute-start(bf16[272,1536]{1,0:T(8,128)(2,1)S(1)} %fusion.1), channel_id=1, source_target_pairs={{0,0},{1,8},{2,1},{3,9},{4,3},{5,11},{6,2},{7,10},{8,4},{9,12},{10... | collective-permute-start | bytes 2506760 | tf_op jit(solution)/shard_map/ppermute | solution.py:88
  58.6 0.7 collective-permute-start.8
  59.6 2.0 collective-permute-start.9
  61.6 15.8 %collective-permute-done.2.own = bf16[272,1536]{1,0:T(8,128)(2,1)S(1)} collective-permute-done((bf16[272,1536]{1,0:T(8,128)(2,1)S(1)}, bf16[272,1536]{1,0:T(8,128)(2,1)S(1)}, u32[]{:S(2)}, u32[]{:S(2)}) %collective-permute-start.2) | collective-permute-done | bytes 835616 | tf_op jit(solution)/shard_map/ppermute | solution.py:88
  77.4 27.8 %collective-permute-start.6 = (bf16[272,1536]{1,0:T(8,128)(2,1)S(1)}, bf16[272,1536]{1,0:T(8,128)(2,1)S(1)}, u32[]{:S(2)}, u32[]{:S(2)}) collective-permute-start(bf16[272,1536]{1,0:T(8,128)(2,1)S(1)} %collective-permute-done.2.own), channel_id=1, source_target_pairs={{8,0},{1,8},{9,1},{3,9},{11,3},{2,11},{10,2},{12,4},{5,12},{13,5},... | collective-permute-start | bytes 2506760 | tf_op jit(solution)/shard_map/ppermute | solution.py:88
  105.2 2.1 collective-permute-start.5
  107.3 0.9 broadcast_select_fusion.3
  108.2 12.7 %collective-permute-done.6.up = bf16[272,1536]{1,0:T(8,128)(2,1)S(1)} collective-permute-done((bf16[272,1536]{1,0:T(8,128)(2,1)S(1)}, bf16[272,1536]{1,0:T(8,128)(2,1)S(1)}, u32[]{:S(2)}, u32[]{:S(2)}) %collective-permute-start.6) | collective-permute-done | bytes 835616 | tf_op jit(solution)/shard_map/ppermute | solution.py:88
  120.8 2.1 collective-permute-done.5.low
  122.9 0.9 copy-done.8
  124.0 3.5 pad_maximum_fusion.rest_0_
  127.5 9.5 %collective-permute-start.11 = (bf16[4,192,4608]{2,1,0:T(8,128)(2,1)}, bf16[4,192,4608]{2,1,0:T(8,128)(2,1)}, u32[]{:S(2)}, u32[]{:S(2)}) collective-permute-start(bf16[4,192,4608]{2,1,0:T(8,128)(2,1)} %pad_maximum_fusion.rest_0_), channel_id=1, source_target_pairs={{0,8},{1,9},{2,10},{3,11},{4,12},{5,13},{6,14},{7,15},{8,0},{9,1},... | collective-permute-start | bytes 21233672 | tf_op jit(solution)/shard_map/ppermute | solution.py:88
  137.1 1.2 collective-permute-start.13
  138.2 1.6 collective-permute-start.12
  140.4 1.5 fusion.2
  141.9 0.7 slice.298
  142.5 0.7 slice.299
  143.2 0.7 slice.300
  144.6 0.8 copy.79.seg_rows
  145.4 1.4 constant_dynamic-slice_fusion
  146.8 1.5 collective-permute-done.11.rest_1_
  148.3 26.9 %attention.1.context = bf16[288,1536]{1,0:T(8,128)(2,1)} custom-call(s32[8]{0:T(128)} %add_multiply_fusion.offsets, bf16[272,1536]{1,0:T(8,128)(2,1)} %copy-done.8, bf16[272,1536]{1,0:T(8,128)(2,1)} %copy-done.6, bf16[272,1536]{1,0:T(8,128)(2,1)} %copy-done.7, f32[1,1536]{1,0:T(1,128)} %get-tuple-element.72.gain.gain_a, s32[288,1]{1,0:T(8,128)} %copy.79.seg_rows, ...), custom_call_target="tpu_custom_call" | custom-call | flops 9965666304 | bytes 17301504 | tf_op jit(solution)/shard_map/attention/pallas_call | solution.py:254
  175.2 2.4 collective-permute-done.13
  177.6 1.4 collective-permute-done.12
  179.0 4.4 %pad_maximum_fusion.1.rest_0_.rest_2_ = bf16[3,192,4608]{2,1,0:T(8,128)(2,1)} fusion(bf16[1,192,4608]{2,1,0:T(8,128)(2,1)S(1)} %bitcast.162, bf16[1,192,4608]{2,1,0:T(8,128)(2,1)} %bitcast.42, bf16[1,192,4608]{2,1,0:T(8,128)(2,1)S(1)} %bitcast.160), kind=kLoop, calls=%fused_computation.1 | loop fusion | flops 5308416 | bytes 10616832 | tf_op jit(solution)/shard_map/stack | solution.py:141
  183.6 1.2 slice.339
  185.3 1.4 collective-permute-start.14
  186.7 20.2 %collective-permute-done.15 = bf16[192,2304]{1,0:T(8,128)(2,1)S(1)} collective-permute-done((bf16[192,2304]{1,0:T(8,128)(2,1)S(1)}, bf16[192,2304]{1,0:T(8,128)(2,1)S(1)}, u32[]{:S(2)}, u32[]{:S(2)}) %collective-permute-start.15) | collective-permute-done | bytes 884768 | tf_op jit(solution)/shard_map/ppermute | solution.py:88
  207.3 1.6 collective-permute-start.19
  208.9 1.6 collective-permute-start.18
  210.5 1.6 slice.379.taps
  212.1 2.6 dynamic-slice_bitcast_fusion.19
  214.7 0.8 copy.80.seg_rows
  215.5 2.0 dynamic-slice_bitcast_fusion.35
  217.5 5.2 %stack.274 = s32[256,31]{0,1:T(8,128)} concatenate(s32[256,1]{0,1:T(1,128)} %get-tuple-element.118, s32[256,1]{0,1:T(1,128)} %get-tuple-element.117, s32[256,1]{0,1:T(1,128)} %get-tuple-element.116, s32[256,1]{0,1:T(1,128)} %get-tuple-element.115, s32[256,1]{0,1:T(1,128)} %get-tuple-element.114, s32[256,1]{0,1:T(1,128)} %get-tuple-element.113, s32[256,1]{0,1:T(1,128)} %get-tuple-element.112, ...), dimensions={1} | concatenate | bytes 63488 | tf_op jit(solution)/shard_map/stack | solution.py:360
  222.8 1.5 copy.81.masks_seg
  224.9 1.5 collective-permute-start.20
  226.4 23.0 %convolution.1 = (bf16[256,1536]{1,0:T(8,128)(2,1)}, f32[256,1536]{1,0:T(8,128)}) custom-call(s32[8]{0:T(128)} %add_multiply_fusion.offsets, bf16[288,1536]{1,0:T(8,128)(2,1)} %attention.1.context, bf16[272,1536]{1,0:T(8,128)(2,1)} %copy-done.8, bf16[272,1536]{1,0:T(8,128)(2,1)} %copy-done.6, bf16[272,1536]{1,0:T(8,128)(2,1)} %copy-done.7, ...), custom_call_target="tpu_custom_call" | custom-call | flops 4113432576 | bytes 17301504 | tf_op jit(solution)/shard_map/convolution/pallas_call | solution.py:361
  249.9 0.7 collective-permute-start.23
  250.6 3.8 collective-permute-done.22.rest_1_.rest_7_
  254.4 1.5 copy-done.3
  255.9 5.8 %mixing.1 = bf16[256,1536]{1,0:T(8,128)(2,1)} custom-call(s32[8]{0:T(128)} %add_multiply_fusion.offsets, bf16[256,1536]{1,0:T(8,128)(2,1)} %get-tuple-element.55.act, f32[256,1536]{1,0:T(8,128)} %get-tuple-element.56.resid, bf16[4,192,1536]{2,1,0:T(8,128)(2,1)} %copy-done, bf16[4,192,1536]{2,1,0:T(8,128)(2,1)} %copy-done.3), custom_call_target="tpu_custom_call" | custom-call | flops 1207959552 | bytes 7864320 | tf_op jit(solution)/shard_map/mixing/pallas_call | solution.py:408
  261.9 4.1 %collective-permute-start.24 = (bf16[256,1536]{1,0:T(8,128)(2,1)}, bf16[256,1536]{1,0:T(8,128)(2,1)S(1)}, u32[]{:S(2)}, u32[]{:S(2)}) collective-permute-start(bf16[256,1536]{1,0:T(8,128)(2,1)} %mixing.1), channel_id=1, source_target_pairs={{0,4},{8,12},{1,5},{9,13},{3,7},{11,15},{2,6},{10,14},{4,16},{12,2... | collective-permute-start | bytes 2359304 | tf_op jit(solution)/shard_map/ppermute | solution.py:88
  265.9 41.4 %collective-permute-done.24 = bf16[256,1536]{1,0:T(8,128)(2,1)S(1)} collective-permute-done((bf16[256,1536]{1,0:T(8,128)(2,1)}, bf16[256,1536]{1,0:T(8,128)(2,1)S(1)}, u32[]{:S(2)}, u32[]{:S(2)}) %collective-permute-start.24) | collective-permute-done | bytes 786464 | tf_op jit(solution)/shard_map/ppermute | solution.py:88
  307.4 1.9 collective-permute-start.26
  309.3 2.8 collective-permute-start.25
  312.2 0.8 copy.83.seg_rows
  313.4 0.8 copy.84.masks_seg
  314.1 0.8 copy.82.seg_queries
  314.9 3.9 collective-permute-done.26.up
  318.8 3.9 collective-permute-done.25.low
  322.8 5.2 %collective-permute-start.27 = (bf16[256,1536]{1,0:T(8,128)(2,1)S(1)}, bf16[256,1536]{1,0:T(8,128)(2,1)S(1)}, u32[]{:S(2)}, u32[]{:S(2)}) collective-permute-start(bf16[256,1536]{1,0:T(8,128)(2,1)S(1)} %copy-done.11), channel_id=1, source_target_pairs={{0,0},{8,1},{1,2},{9,3},{3,4},{11,5},{2,6},{10,7},{4,8},{12,9},{5,... | collective-permute-start | bytes 2359304 | tf_op jit(solution)/shard_map/ppermute | solution.py:88
  328.0 49.7 %tick.1 = bf16[256,1536]{1,0:T(8,128)(2,1)} custom-call(s32[8]{0:T(128)} %add_multiply_fusion.offsets, bf16[256,1536]{1,0:T(8,128)(2,1)} %collective-permute-done.25.low, bf16[256,1536]{1,0:T(8,128)(2,1)} %copy-done.9, bf16[256,1536]{1,0:T(8,128)(2,1)} %copy-done.28, f32[1,1536]{1,0:T(1,128)} %get-tuple-element.72.gain.gain_a, ...), custom_call_target="tpu_custom_call" | custom-call | flops 14042529792 | bytes 33030144 | tf_op jit(solution)/shard_map/tick/pallas_call | solution.py:460
  377.7 1.9 collective-permute-start.28
  379.7 19.0 %collective-permute-done.28 = bf16[256,1536]{1,0:T(8,128)(2,1)S(1)} collective-permute-done((bf16[256,1536]{1,0:T(8,128)(2,1)}, bf16[256,1536]{1,0:T(8,128)(2,1)S(1)}, u32[]{:S(2)}, u32[]{:S(2)}) %collective-permute-start.28) | collective-permute-done | bytes 786464 | tf_op jit(solution)/shard_map/ppermute | solution.py:88
  398.6 1.3 maximum_bitcast_fusion.2
  (99 shorter events, 5.5 us)
Async XLA Ops:
  0.0 5.6 %copy-start.5 = (bf16[1,192,3072]{2,1,0:T(8,128)(2,1)S(1)}, bf16[1,192,3072]{2,1,0:T(8,128)(2,1)}, u32[]{:S(2)}) copy-start(bf16[1,192,3072]{2,1,0:T(8,128)(2,1)} %param.17) | copy-start | bytes 3538948
  1.8 1.6 collective-permute-start
  4.8 2.1 collective-permute-start.1
  5.6 1.7 copy-start.4
  6.9 3.5 copy-start.15
  6.9 3.5 copy-start.10
  7.4 50.9 %collective-permute-start.7 = (bf16[192,4608]{1,0:T(8,128)(2,1)S(1)}, bf16[192,4608]{1,0:T(8,128)(2,1)S(1)}, u32[]{:S(2)}, u32[]{:S(2)}) collective-permute-start(bf16[192,4608]{1,0:T(8,128)(2,1)S(1)} %pad_maximum_fusion.3), channel_id=1, source_target_pairs={{4,8},{5,9},{6,10},{7,11},{8,4},{9,5},{10,6},{11,7},{20,24},{21,25... | collective-permute-start | bytes 5308424 | tf_op jit(solution)/shard_map/ppermute | solution.py:88
  8.2 51.1 %collective-permute-start.4 = (bf16[192,4608]{1,0:T(8,128)(2,1)S(1)}, bf16[192,4608]{1,0:T(8,128)(2,1)S(1)}, u32[]{:S(2)}, u32[]{:S(2)}) collective-permute-start(bf16[192,4608]{1,0:T(8,128)(2,1)S(1)} %broadcast_select_fusion.1), channel_id=1, source_target_pairs={{0,2},{1,3},{2,0},{3,1},{4,6},{5,7},{6,4},{7,5},{8,10},{9,11},{10,... | collective-permute-start | bytes 5308424 | tf_op jit(solution)/shard_map/ppermute | solution.py:88
  9.9 49.4 %collective-permute-start.3 = (bf16[192,4608]{1,0:T(8,128)(2,1)S(1)}, bf16[192,4608]{1,0:T(8,128)(2,1)S(1)}, u32[]{:S(2)}, u32[]{:S(2)}) collective-permute-start(bf16[192,4608]{1,0:T(8,128)(2,1)S(1)} %broadcast_select_fusion.1), channel_id=1, source_target_pairs={{0,1},{1,0},{2,3},{3,2},{4,5},{5,4},{6,7},{7,6},{8,9},{9,8},{10,11... | collective-permute-start | bytes 5308424 | tf_op jit(solution)/shard_map/ppermute | solution.py:88
  10.5 48.1 %copy-start.12 = (bf16[1,192,1536]{2,1,0:T(8,128)(2,1)S(1)}, bf16[1,192,1536]{2,1,0:T(8,128)(2,1)}, u32[]{:S(2)}) copy-start(bf16[1,192,1536]{2,1,0:T(8,128)(2,1)} %param.19) | copy-start | bytes 1769476
  10.5 66.9 %collective-permute-start.2 = (bf16[272,1536]{1,0:T(8,128)(2,1)S(1)}, bf16[272,1536]{1,0:T(8,128)(2,1)S(1)}, u32[]{:S(2)}, u32[]{:S(2)}) collective-permute-start(bf16[272,1536]{1,0:T(8,128)(2,1)S(1)} %fusion.1), channel_id=1, source_target_pairs={{0,0},{1,8},{2,1},{3,9},{4,3},{5,11},{6,2},{7,10},{8,4},{9,12},{10... | collective-permute-start | bytes 2506760 | tf_op jit(solution)/shard_map/ppermute | solution.py:88
  58.6 48.7 %collective-permute-start.8 = (bf16[192,1536]{1,0:T(8,128)(2,1)S(1)}, bf16[192,1536]{1,0:T(8,128)(2,1)S(1)}, u32[]{:S(2)}, u32[]{:S(2)}) collective-permute-start(bf16[192,1536]{1,0:T(8,128)(2,1)S(1)} %bitcast.175), channel_id=1, source_target_pairs={{4,8},{5,9},{6,10},{7,11},{8,4},{9,5},{10,6},{11,7},{20,24},{21,25... | collective-permute-start | bytes 1769480 | tf_op jit(solution)/shard_map/ppermute | solution.py:88
  59.5 63.5 %collective-permute-start.10 = (bf16[192,2304]{1,0:T(8,128)(2,1)S(1)}, bf16[192,2304]{1,0:T(8,128)(2,1)S(1)}, u32[]{:S(2)}, u32[]{:S(2)}) collective-permute-start(bf16[192,2304]{1,0:T(8,128)(2,1)S(1)} %get-tuple-element.69), channel_id=1, source_target_pairs={{0,1},{1,0},{2,3},{3,2},{4,6},{5,7},{6,4},{7,5},{8,10},{9,11},{10,... | collective-permute-start | bytes 2654216 | tf_op jit(solution)/shard_map/ppermute | solution.py:88
  59.6 64.3 %collective-permute-start.9 = (bf16[192,2304]{1,0:T(8,128)(2,1)S(1)}, bf16[192,2304]{1,0:T(8,128)(2,1)S(1)}, u32[]{:S(2)}, u32[]{:S(2)}) collective-permute-start(bf16[192,2304]{1,0:T(8,128)(2,1)S(1)} %get-tuple-element.70), channel_id=1, source_target_pairs={{0,1},{1,0},{2,3},{3,2},{4,5},{5,4},{6,7},{7,6},{8,9},{9,8},{10,11... | collective-permute-start | bytes 2654216 | tf_op jit(solution)/shard_map/ppermute | solution.py:88
  77.4 46.6 %copy-start.6 = (bf16[272,1536]{1,0:T(8,128)(2,1)}, bf16[272,1536]{1,0:T(8,128)(2,1)S(1)}, u32[]{:S(2)}) copy-start(bf16[272,1536]{1,0:T(8,128)(2,1)S(1)} %collective-permute-done.2.own) | copy-start | bytes 2506756
  77.4 43.4 %collective-permute-start.6 = (bf16[272,1536]{1,0:T(8,128)(2,1)S(1)}, bf16[272,1536]{1,0:T(8,128)(2,1)S(1)}, u32[]{:S(2)}, u32[]{:S(2)}) collective-permute-start(bf16[272,1536]{1,0:T(8,128)(2,1)S(1)} %collective-permute-done.2.own), channel_id=1, source_target_pairs={{8,0},{1,8},{9,1},{3,9},{11,3},{2,11},{10,2},{12,4},{5,12},{13,5},... | collective-permute-start | bytes 2506760 | tf_op jit(solution)/shard_map/ppermute | solution.py:88
  105.2 17.8 %collective-permute-start.5 = (bf16[272,1536]{1,0:T(8,128)(2,1)S(1)}, bf16[272,1536]{1,0:T(8,128)(2,1)S(1)}, u32[]{:S(2)}, u32[]{:S(2)}) collective-permute-start(bf16[272,1536]{1,0:T(8,128)(2,1)S(1)} %collective-permute-done.2.own), channel_id=1, source_target_pairs={{0,8},{8,1},{1,9},{9,3},{3,11},{11,2},{2,10},{4,12},{12,5},{5,13},... | collective-permute-start | bytes 2506760 | tf_op jit(solution)/shard_map/ppermute | solution.py:88
  120.8 2.1 copy-start.7
  122.9 0.9 copy-start.8
  127.5 20.8 %collective-permute-start.11 = (bf16[4,192,4608]{2,1,0:T(8,128)(2,1)}, bf16[4,192,4608]{2,1,0:T(8,128)(2,1)}, u32[]{:S(2)}, u32[]{:S(2)}) collective-permute-start(bf16[4,192,4608]{2,1,0:T(8,128)(2,1)} %pad_maximum_fusion.rest_0_), channel_id=1, source_target_pairs={{0,8},{1,9},{2,10},{3,11},{4,12},{5,13},{6,14},{7,15},{8,0},{9,1},... | collective-permute-start | bytes 21233672 | tf_op jit(solution)/shard_map/ppermute | solution.py:88
  137.1 40.6 %collective-permute-start.13 = (bf16[192,4608]{1,0:T(8,128)(2,1)S(1)}, bf16[192,4608]{1,0:T(8,128)(2,1)S(1)}, u32[]{:S(2)}, u32[]{:S(2)}) collective-permute-start(bf16[192,4608]{1,0:T(8,128)(2,1)S(1)} %broadcast_select_fusion), channel_id=1, source_target_pairs={{0,2},{1,3},{2,0},{3,1},{4,6},{5,7},{6,4},{7,5},{8,10},{9,11},{10,... | collective-permute-start | bytes 5308424 | tf_op jit(solution)/shard_map/ppermute | solution.py:88
  138.2 40.8 %collective-permute-start.12 = (bf16[192,4608]{1,0:T(8,128)(2,1)S(1)}, bf16[192,4608]{1,0:T(8,128)(2,1)}, u32[]{:S(2)}, u32[]{:S(2)}) collective-permute-start(bf16[192,4608]{1,0:T(8,128)(2,1)S(1)} %broadcast_select_fusion), channel_id=1, source_target_pairs={{0,1},{1,0},{2,3},{3,2},{4,5},{5,4},{6,7},{7,6},{8,9},{9,8},{10,11... | collective-permute-start | bytes 5308424 | tf_op jit(solution)/shard_map/ppermute | solution.py:88
  143.9 0.6 copy-start.13
  183.4 43.0 %collective-permute-start.16 = (bf16[3,192,4608]{2,1,0:T(8,128)(2,1)}, bf16[3,192,4608]{2,1,0:T(8,128)(2,1)}, u32[]{:S(2)}, u32[]{:S(2)}) collective-permute-start(bf16[3,192,4608]{2,1,0:T(8,128)(2,1)} %pad_maximum_fusion.1.rest_0_.rest_2_), channel_id=1, source_target_pairs={{0,8},{1,9},{2,10},{3,11},{4,12},{5,13},{6,14},{7,15},{8,0},{9,1},... | collective-permute-start | bytes 15925256 | tf_op jit(solution)/shard_map/ppermute | solution.py:88
  184.8 22.5 %copy-start.2 = (bf16[192,1536]{1,0:T(8,128)(2,1)S(1)}, bf16[192,1536]{1,0:T(8,128)(2,1)}, u32[]{:S(2)}) copy-start(bf16[192,1536]{1,0:T(8,128)(2,1)} %broadcast_select_fusion.3) | copy-start | bytes 1769476
  184.8 22.1 %collective-permute-start.15 = (bf16[192,2304]{1,0:T(8,128)(2,1)S(1)}, bf16[192,2304]{1,0:T(8,128)(2,1)S(1)}, u32[]{:S(2)}, u32[]{:S(2)}) collective-permute-start(bf16[192,2304]{1,0:T(8,128)(2,1)S(1)} %slice.339), channel_id=1, source_target_pairs={{0,2},{1,3},{2,0},{3,1},{4,6},{5,7},{6,4},{7,5},{8,10},{9,11},{10,... | collective-permute-start | bytes 2654216 | tf_op jit(solution)/shard_map/ppermute | solution.py:88
  185.3 21.8 %collective-permute-start.14 = (bf16[192,2304]{1,0:T(8,128)(2,1)S(1)}, bf16[192,2304]{1,0:T(8,128)(2,1)S(1)}, u32[]{:S(2)}, u32[]{:S(2)}) collective-permute-start(bf16[192,2304]{1,0:T(8,128)(2,1)S(1)} %slice.338), channel_id=1, source_target_pairs={{0,1},{1,0},{2,3},{3,2},{4,5},{5,4},{6,7},{7,6},{8,9},{9,8},{10,11... | collective-permute-start | bytes 2654216 | tf_op jit(solution)/shard_map/ppermute | solution.py:88
  207.2 19.2 %copy-start.1 = (bf16[1,192,4608]{2,1,0:T(8,128)(2,1)}, bf16[1,192,4608]{2,1,0:T(8,128)(2,1)S(1)}, u32[]{:S(2)}) copy-start(bf16[1,192,4608]{2,1,0:T(8,128)(2,1)S(1)} %maximum_bitcast_fusion.1.rest_1_.rest_3_) | copy-start | bytes 5308420
  207.2 19.2 %collective-permute-start.17 = (bf16[1,192,4608]{2,1,0:T(8,128)(2,1)S(1)}, bf16[1,192,4608]{2,1,0:T(8,128)(2,1)}, u32[]{:S(2)}, u32[]{:S(2)}) collective-permute-start(bf16[1,192,4608]{2,1,0:T(8,128)(2,1)S(1)} %maximum_bitcast_fusion.1.rest_1_.rest_3_), channel_id=1, source_target_pairs={{0,8},{1,9},{2,10},{3,11},{4,12},{5,13},{6,14},{7,15},{8,0},{9,1},... | collective-permute-start | bytes 5308424 | tf_op jit(solution)/shard_map/ppermute | solution.py:88
  207.3 17.0 %collective-permute-start.19 = (bf16[192,1536]{1,0:T(8,128)(2,1)S(1)}, bf16[192,1536]{1,0:T(8,128)(2,1)S(1)}, u32[]{:S(2)}, u32[]{:S(2)}) collective-permute-start(bf16[192,1536]{1,0:T(8,128)(2,1)S(1)} %copy-done.2), channel_id=1, source_target_pairs={{0,2},{1,3},{2,0},{3,1},{4,6},{5,7},{6,4},{7,5},{8,10},{9,11},{10,... | collective-permute-start | bytes 1769480 | tf_op jit(solution)/shard_map/ppermute | solution.py:88
  208.9 15.4 %collective-permute-start.18 = (bf16[192,1536]{1,0:T(8,128)(2,1)S(1)}, bf16[192,1536]{1,0:T(8,128)(2,1)S(1)}, u32[]{:S(2)}, u32[]{:S(2)}) collective-permute-start(bf16[192,1536]{1,0:T(8,128)(2,1)S(1)} %copy-done.2), channel_id=1, source_target_pairs={{0,1},{1,0},{2,3},{3,2},{4,5},{5,4},{6,7},{7,6},{8,9},{9,8},{10,11... | collective-permute-start | bytes 1769480 | tf_op jit(solution)/shard_map/ppermute | solution.py:88
  224.4 25.0 %collective-permute-start.21 = (bf16[192,768]{1,0:T(8,128)(2,1)S(1)}, bf16[192,768]{1,0:T(8,128)(2,1)S(1)}, u32[]{:S(2)}, u32[]{:S(2)}) collective-permute-start(bf16[192,768]{1,0:T(8,128)(2,1)S(1)} %slice.341), channel_id=1, source_target_pairs={{0,2},{1,3},{2,0},{3,1},{4,6},{5,7},{6,4},{7,5},{8,10},{9,11},{10,... | collective-permute-start | bytes 884744 | tf_op jit(solution)/shard_map/ppermute | solution.py:88
  224.9 24.5 %collective-permute-start.20 = (bf16[192,768]{1,0:T(8,128)(2,1)S(1)}, bf16[192,768]{1,0:T(8,128)(2,1)S(1)}, u32[]{:S(2)}, u32[]{:S(2)}) collective-permute-start(bf16[192,768]{1,0:T(8,128)(2,1)S(1)} %slice.340), channel_id=1, source_target_pairs={{0,1},{1,0},{2,3},{3,2},{4,5},{5,4},{6,7},{7,6},{8,9},{9,8},{10,11... | collective-permute-start | bytes 884744 | tf_op jit(solution)/shard_map/ppermute | solution.py:88
  249.8 4.6 %copy-start = (bf16[4,192,1536]{2,1,0:T(8,128)(2,1)}, bf16[4,192,1536]{2,1,0:T(8,128)(2,1)S(1)}, u32[]{:S(2)}) copy-start(bf16[4,192,1536]{2,1,0:T(8,128)(2,1)S(1)} %pad_maximum_fusion.2.rest_0_.rest_6_) | copy-start | bytes 7077892
  249.8 4.6 %collective-permute-start.22 = (bf16[4,192,1536]{2,1,0:T(8,128)(2,1)S(1)}, bf16[4,192,1536]{2,1,0:T(8,128)(2,1)S(1)}, u32[]{:S(2)}, u32[]{:S(2)}) collective-permute-start(bf16[4,192,1536]{2,1,0:T(8,128)(2,1)S(1)} %pad_maximum_fusion.2.rest_0_.rest_6_), channel_id=1, source_target_pairs={{0,8},{1,9},{2,10},{3,11},{4,12},{5,13},{6,14},{7,15},{8,0},{9,1},... | collective-permute-start | bytes 7077896 | tf_op jit(solution)/shard_map/ppermute | solution.py:88
  249.9 16.1 %collective-permute-start.23 = (bf16[256,1536]{1,0:T(8,128)(2,1)}, bf16[256,1536]{1,0:T(8,128)(2,1)S(1)}, u32[]{:S(2)}, u32[]{:S(2)}) collective-permute-start(bf16[256,1536]{1,0:T(8,128)(2,1)} %bitcast.49), channel_id=1, source_target_pairs={{0,0},{1,8},{2,1},{3,9},{4,3},{5,11},{6,2},{7,10}} | collective-permute-start | bytes 2359304 | tf_op jit(solution)/shard_map/ppermute | solution.py:88
  254.4 1.5 copy-start.3
  261.7 51.3 %copy-start.14 = (s32[5,768]{1,0:T(8,128)S(1)}, s32[5,768]{1,0:T(8,128)}, u32[]{:S(2)}) copy-start(s32[5,768]{1,0:T(8,128)} %copy-done.13) | copy-start | bytes 46084
  261.7 51.4 %copy-start.16 = (s32[256,1]{0,1:T(1,128)S(1)}, s32[256,1]{0,1:T(1,128)}, u32[]{:S(2)}) copy-start(s32[256,1]{0,1:T(1,128)} %get-tuple-element.91) | copy-start | bytes 3076
  261.7 51.4 %copy-start.17 = (s32[256,1]{0,1:T(1,128)S(1)}, s32[256,1]{0,1:T(1,128)}, u32[]{:S(2)}) copy-start(s32[256,1]{0,1:T(1,128)} %get-tuple-element.92) | copy-start | bytes 3076
  261.7 51.4 %copy-start.18 = (s32[256,1]{0,1:T(1,128)S(1)}, s32[256,1]{0,1:T(1,128)}, u32[]{:S(2)}) copy-start(s32[256,1]{0,1:T(1,128)} %get-tuple-element.93) | copy-start | bytes 3076
  261.8 51.4 %copy-start.19 = (s32[256,1]{0,1:T(1,128)S(1)}, s32[256,1]{0,1:T(1,128)}, u32[]{:S(2)}) copy-start(s32[256,1]{0,1:T(1,128)} %get-tuple-element.94) | copy-start | bytes 3076
  261.8 51.4 %copy-start.20 = (s32[256,1]{0,1:T(1,128)S(1)}, s32[256,1]{0,1:T(1,128)}, u32[]{:S(2)}) copy-start(s32[256,1]{0,1:T(1,128)} %get-tuple-element.95) | copy-start | bytes 3076
  261.8 51.4 %copy-start.21 = (s32[256,1]{0,1:T(1,128)S(1)}, s32[256,1]{0,1:T(1,128)}, u32[]{:S(2)}) copy-start(s32[256,1]{0,1:T(1,128)} %get-tuple-element.96) | copy-start | bytes 3076
  261.8 51.4 %copy-start.22 = (s32[256,1]{0,1:T(1,128)S(1)}, s32[256,1]{0,1:T(1,128)}, u32[]{:S(2)}) copy-start(s32[256,1]{0,1:T(1,128)} %get-tuple-element.97) | copy-start | bytes 3076
  261.8 51.4 %copy-start.23 = (s32[256,1]{0,1:T(1,128)S(1)}, s32[256,1]{0,1:T(1,128)}, u32[]{:S(2)}) copy-start(s32[256,1]{0,1:T(1,128)} %get-tuple-element.98) | copy-start | bytes 3076
  261.8 51.4 %copy-start.24 = (s32[256,1]{0,1:T(1,128)S(1)}, s32[256,1]{0,1:T(1,128)}, u32[]{:S(2)}) copy-start(s32[256,1]{0,1:T(1,128)} %get-tuple-element.99) | copy-start | bytes 3076
  261.8 51.4 %copy-start.25 = (s32[256,1]{0,1:T(1,128)S(1)}, s32[256,1]{0,1:T(1,128)}, u32[]{:S(2)}) copy-start(s32[256,1]{0,1:T(1,128)} %get-tuple-element.100) | copy-start | bytes 3076
  261.8 51.4 %copy-start.26 = (s32[256,1]{0,1:T(1,128)S(1)}, s32[256,1]{0,1:T(1,128)}, u32[]{:S(2)}) copy-start(s32[256,1]{0,1:T(1,128)} %get-tuple-element.101) | copy-start | bytes 3076
  261.8 51.4 %copy-start.27 = (s32[256,1]{0,1:T(1,128)S(1)}, s32[256,1]{0,1:T(1,128)}, u32[]{:S(2)}) copy-start(s32[256,1]{0,1:T(1,128)} %get-tuple-element.102) | copy-start | bytes 3076
  261.8 60.9 %copy-start.11 = (bf16[256,1536]{1,0:T(8,128)(2,1)S(1)}, bf16[256,1536]{1,0:T(8,128)(2,1)}, u32[]{:S(2)}) copy-start(bf16[256,1536]{1,0:T(8,128)(2,1)} %mixing.1) | copy-start | bytes 2359300
  261.9 45.5 %collective-permute-start.24 = (bf16[256,1536]{1,0:T(8,128)(2,1)}, bf16[256,1536]{1,0:T(8,128)(2,1)S(1)}, u32[]{:S(2)}, u32[]{:S(2)}) collective-permute-start(bf16[256,1536]{1,0:T(8,128)(2,1)} %mixing.1), channel_id=1, source_target_pairs={{0,4},{8,12},{1,5},{9,13},{3,7},{11,15},{2,6},{10,14},{4,16},{12,2... | collective-permute-start | bytes 2359304 | tf_op jit(solution)/shard_map/ppermute | solution.py:88
  307.4 20.5 %copy-start.9 = (bf16[256,1536]{1,0:T(8,128)(2,1)}, bf16[256,1536]{1,0:T(8,128)(2,1)S(1)}, u32[]{:S(2)}) copy-start(bf16[256,1536]{1,0:T(8,128)(2,1)S(1)} %broadcast_select_fusion.2.own) | copy-start | bytes 2359300
  307.4 11.4 %collective-permute-start.26 = (bf16[256,1536]{1,0:T(8,128)(2,1)S(1)}, bf16[256,1536]{1,0:T(8,128)(2,1)S(1)}, u32[]{:S(2)}, u32[]{:S(2)}) collective-permute-start(bf16[256,1536]{1,0:T(8,128)(2,1)S(1)} %broadcast_select_fusion.2.own), channel_id=1, source_target_pairs={{8,0},{1,8},{9,1},{3,9},{11,3},{2,11},{10,2},{12,4},{5,12},{13,5},... | collective-permute-start | bytes 2359304 | tf_op jit(solution)/shard_map/ppermute | solution.py:88
  309.3 13.4 %collective-permute-start.25 = (bf16[256,1536]{1,0:T(8,128)(2,1)S(1)}, bf16[256,1536]{1,0:T(8,128)(2,1)}, u32[]{:S(2)}, u32[]{:S(2)}) collective-permute-start(bf16[256,1536]{1,0:T(8,128)(2,1)S(1)} %broadcast_select_fusion.2.own), channel_id=1, source_target_pairs={{0,8},{8,1},{1,9},{9,3},{3,11},{11,2},{2,10},{4,12},{12,5},{5,13},... | collective-permute-start | bytes 2359304 | tf_op jit(solution)/shard_map/ppermute | solution.py:88
  318.8 9.1 %copy-start.28 = (bf16[256,1536]{1,0:T(8,128)(2,1)}, bf16[256,1536]{1,0:T(8,128)(2,1)S(1)}, u32[]{:S(2)}) copy-start(bf16[256,1536]{1,0:T(8,128)(2,1)S(1)} %collective-permute-done.26.up) | copy-start | bytes 2359300
  322.8 56.9 %collective-permute-start.27 = (bf16[256,1536]{1,0:T(8,128)(2,1)S(1)}, bf16[256,1536]{1,0:T(8,128)(2,1)S(1)}, u32[]{:S(2)}, u32[]{:S(2)}) collective-permute-start(bf16[256,1536]{1,0:T(8,128)(2,1)S(1)} %copy-done.11), channel_id=1, source_target_pairs={{0,0},{8,1},{1,2},{9,3},{3,4},{11,5},{2,6},{10,7},{4,8},{12,9},{5,... | collective-permute-start | bytes 2359304 | tf_op jit(solution)/shard_map/ppermute | solution.py:88
  377.7 20.9 %collective-permute-start.28 = (bf16[256,1536]{1,0:T(8,128)(2,1)}, bf16[256,1536]{1,0:T(8,128)(2,1)S(1)}, u32[]{:S(2)}, u32[]{:S(2)}) collective-permute-start(bf16[256,1536]{1,0:T(8,128)(2,1)} %tick.1), channel_id=1, source_target_pairs={{0,0},{8,1},{1,2},{9,3},{3,4},{11,5},{2,6},{10,7},{4,8},{12,9},{5,... | collective-permute-start | bytes 2359304 | tf_op jit(solution)/shard_map/ppermute | solution.py:88
